TPU v7x, 512 devices: a whole 4x4x16 slice. The times are simulated.
512 devices in a mesh: seq: 64 (over x, z), head: 8 (over y, core).
Axes of the slice: x: 4, y: 4, z: 16, core: 2. Of those that a mesh axis runs over, the one named last changes fastest.
Arguments:
- query_rows: bfloat16 [8192, 4096], P('seq', 'head'), may hold values from -2.5 to 2.5
- key_rows: bfloat16 [8192, 4096], P('seq', 'head'), may hold values from -2.5 to 2.5
- value_rows: bfloat16 [8192, 4096], P('seq', 'head'), may hold values from -6 to 6
- out_grad: bfloat16 [8192, 4096], P('seq', 'head'), may hold values from -6 to 6
- norm_gain: float32 [4096], P('head'), may hold values from 0.25 to 1.75
- decay_rate: float32 [32], P('head'), as said below
- doc_ids: int32 [8192], P('seq'), may hold values from 0 to 7, never falling along the last dimension, each value on 1 to 4096 neighbouring positions
Outputs:
- query_grad: bfloat16 [8192, 4096], P('seq', 'head')
- key_grad: bfloat16 [8192, 4096], P('seq', 'head')
- value_grad: bfloat16 [8192, 4096], P('seq', 'head')
Inputs may be any that keep to these rules, and one draw needn't show every extreme that they name: `doc_ids`: document numbers never fall along the window; each of the 8 documents holds 1 to 4096 tokens, and one holds exactly 4096. `decay_rate`: every rate is positive and lies between 3 / 81920 and 1 / 30.
All inputs are finite; a program needn't handle non-finite values.
Results may differ from a plain program's by a relative error of at most 0.0063.
Values sent between devices are 32-bit elements; how exact they have to be, the bound alone decides.
No kernel may reach another device: no remote copies, remote signals or barrier semaphores. Data moves between devices by JAX's collectives and lax.ppermute only.
A program may use at most 128 MiB of HBM per device.

v0:
```python
import jax
import jax.numpy as jnp
from jax import lax
from jax.sharding import PartitionSpec as P

HEADS = 32
HEAD_DIM = 128


epsilon = 1e-06


def shifted(shard, axis, by):
    devices = lax.axis_size(axis)
    pairs = [(i, i + by) for i in range(devices) if 0 <= i + by < devices]
    return lax.ppermute(shard, axis, pairs)


def entering(value, axis, join, neutral, backward):
    count, mine = (lax.axis_size(axis), lax.axis_index(axis))
    pieces = jax.tree.map(lambda part: lax.all_gather(part, axis), value)
    if backward:
        pieces = jax.tree.map(lambda part: part[::-1], pieces)
        mine = count - 1 - mine
    total = jax.tree.map(
        lambda part, zero: jnp.full_like(part, 0) + jnp.asarray(zero, part.dtype), value, neutral
    )

    def lap(position, total):
        longer = join(total, jax.tree.map(lambda part: part[position], pieces))
        return jax.tree.map(lambda new, old: jnp.where(position < mine, new, old), longer, total)

    return lax.fori_loop(0, count - 1, lap, total)


def factors(docs, prev_doc, rates):
    block_len = docs.shape[0]
    position = jnp.arange(block_len).astype(jnp.float32)
    same_prev = docs == prev_doc
    same_last = docs == docs[block_len - 1]
    inflow = jnp.where(
        same_prev[:, None], jnp.exp(-rates[None, :] * (position[:, None] + 1.0)), 0.0
    )
    outflow = jnp.where(
        same_last[:, None], jnp.exp(-rates[None, :] * (block_len - 1.0 - position[:, None])), 0.0
    )
    passage = jnp.where(same_prev[block_len - 1], jnp.exp(-rates * block_len), 0.0)
    offset = position[:, None] - position[None, :]
    inside = (offset >= 0.0) & (docs[:, None] == docs[None, :])
    decays = jnp.where(
        inside[None], jnp.exp(-rates[:, None, None] * jnp.where(inside, offset, 0.0)[None]), 0.0
    )
    return (inflow, outflow, passage, decays)


def combine_states(earlier, later):
    return (earlier[0] * later[0], later[0][:, None, None] * earlier[1] + later[1])


def per_device(query_rows, key_rows, value_rows, out_grad, norm_gain, decay_rate, doc_ids):
    block_len = query_rows.shape[0]
    head_count = decay_rate.shape[0]
    head_width = query_rows.shape[1] // head_count
    width_all = HEADS * HEAD_DIM
    split_shape = (block_len, head_count, head_width)
    query_heads = query_rows.reshape(split_shape)
    key_heads = key_rows.reshape(split_shape)
    value_heads = value_rows.reshape(split_shape)
    prev_doc = shifted(doc_ids[block_len - 1 :] + 1, "seq", 1)[0] - 1
    inflow, outflow, passage, decays = factors(doc_ids, prev_doc, decay_rate)
    key_out = (key_heads.astype(jnp.float32) * outflow[:, :, None]).astype(jnp.bfloat16)
    local_state = jnp.einsum(
        "uhd,uhe->hde", key_out, value_heads, preferred_element_type=jnp.float32
    )
    identity = (
        jnp.ones((head_count,), jnp.float32),
        jnp.zeros((head_count, head_width, head_width), jnp.float32),
    )
    state_full = entering((passage, local_state), "seq", combine_states, identity, False)[1]
    state_low = state_full.astype(jnp.bfloat16)
    scores = jnp.einsum("phd,uhd->hpu", query_heads, key_heads, preferred_element_type=jnp.float32)
    weights = (scores * decays).astype(jnp.bfloat16)
    attended = jnp.einsum("hpu,uhe->phe", weights, value_heads, preferred_element_type=jnp.float32)
    attended = attended + inflow[:, :, None] * jnp.einsum(
        "phd,hde->phe", query_heads, state_low, preferred_element_type=jnp.float32
    )
    flat_out = attended.reshape(block_len, head_count * head_width)
    scaled = norm_gain[None, :] * out_grad.astype(jnp.float32)
    square_sum = jnp.sum(flat_out * flat_out, axis=1)
    cross_sum = jnp.sum(scaled * flat_out, axis=1)
    square_tot, cross_tot = lax.psum((square_sum, cross_sum), "head")
    inv_rms = lax.rsqrt(square_tot / width_all + epsilon)
    grad_flat = scaled * inv_rms[:, None] - flat_out * (cross_tot * inv_rms**3 / width_all)[:, None]
    grad_heads = grad_flat.astype(jnp.bfloat16).reshape(split_shape)
    query_in = (query_heads.astype(jnp.float32) * inflow[:, :, None]).astype(jnp.bfloat16)
    local_grad = jnp.einsum(
        "phd,phe->hde", query_in, grad_heads, preferred_element_type=jnp.float32
    )
    state_back = entering((passage, local_grad), "seq", combine_states, identity, True)[1]
    out_low = state_back.astype(jnp.bfloat16)
    grad_scores = jnp.einsum(
        "phe,uhe->hpu", grad_heads, value_heads, preferred_element_type=jnp.float32
    )
    grad_weights = (grad_scores * decays).astype(jnp.bfloat16)
    query_grad = jnp.einsum(
        "hpu,uhd->phd", grad_weights, key_heads, preferred_element_type=jnp.float32
    )
    query_grad = query_grad + inflow[:, :, None] * jnp.einsum(
        "phe,hde->phd", grad_heads, state_low, preferred_element_type=jnp.float32
    )
    key_grad = jnp.einsum(
        "hpu,phd->uhd", grad_weights, query_heads, preferred_element_type=jnp.float32
    )
    key_grad = key_grad + outflow[:, :, None] * jnp.einsum(
        "uhe,hde->uhd", value_heads, out_low, preferred_element_type=jnp.float32
    )
    value_grad = jnp.einsum("hpu,phe->uhe", weights, grad_heads, preferred_element_type=jnp.float32)
    value_grad = value_grad + outflow[:, :, None] * jnp.einsum(
        "uhd,hde->uhe", key_heads, out_low, preferred_element_type=jnp.float32
    )
    flat_shape = (block_len, head_count * head_width)
    return (
        query_grad.astype(jnp.bfloat16).reshape(flat_shape),
        key_grad.astype(jnp.bfloat16).reshape(flat_shape),
        value_grad.astype(jnp.bfloat16).reshape(flat_shape),
    )


def solution(mesh):
    return jax.shard_map(
        per_device,
        mesh=mesh,
        in_specs=(
            P("seq", "head"),
            P("seq", "head"),
            P("seq", "head"),
            P("seq", "head"),
            P("head"),
            P("head"),
            P("seq"),
        ),
        out_specs=(P("seq", "head"), P("seq", "head"), P("seq", "head")),
        check_vma=False,
    )
```

profile of v0, /device:TPU:6, one launch (start us, length us, event | category | flops | bytes accessed | tf_op | source)
XLA Modules:
  0.0 581.6 jit_solution(2705827687804894941)
XLA Ops:
  7.2 1.3 slice.7
  9.1 5.1 collective-permute-start
  15.3 1.3 dynamic-slice
  17.2 5.2 collective-permute-done
  23.0 1.3 broadcast_compare_fusion
  24.9 1.4 fusion.33
  30.1 122.2 %all-reduce = f32[256]{0:T(256)S(1)} all-reduce(f32[256]{0:T(256)S(1)} %get-tuple-element.266), channel_id=2, replica_groups=mesh['seq'=64,'head'=8] {'seq'}, use_global_device_ids=true, to_apply=%add | all-reduce | flops 256 | bytes 2048
  152.9 65.4 %all-gather.6.cloned.1.call-done = f32[256,128,128]{2,1,0:T(8,128)} async-done(((f32[4,128,128]{2,1,0:T(8,128)}), f32[256,128,128]{2,1,0:T(8,128)}) %all-gather.6.cloned.1.call-update) | async-done | bytes 16777232 | tf_op jit(solution)/shard_map/all_gather | solution.py:21
  218.3 68.9 %while.28 = (s32[]{:T(128)}, f32[4,128,128]{2,1,0:T(8,128)S(1)}, s32[]{:T(128)}, f32[64,4]{1,0:T(8,128)S(1)}, f32[64,4,128,128]{3,2,1,0:T(8,128)}, /*index=5*/s32[]{:T(128)}, s32[]{:T(128)}) while((s32[]{:T(128)}, f32[4,128,128]{2,1,0:T(8,128)S(1)}, s32[]{:T(128)}, f32[64,4]{1,0:T(8,128)S(1)}, f32[64,4,128,128]{3,2,1,0:T(8,128)}, ...), condition=%wide.region_1.2_spmd.clone, body=%wide.region_0.1_spmd.clone.sunk | while | flops 262148 | bytes 786585 | solution.py:33
  288.6 14.2 %all-reduce.1 = (f32[128]{0:T(128)S(1)}, f32[128]{0:T(128)S(1)}) all-reduce(f32[128]{0:T(128)S(1)} %multiply_reduce_fusion, f32[128]{0:T(128)S(1)} %get-tuple-element.268), channel_id=1, replica_groups=mesh['seq'=64,'head'=8] {'head'}, use_global_device_ids=true, to_apply=%region_5.6 | all-reduce | flops 256 | bytes 2048 | tf_op jit(solution)/shard_map/psum | solution.py:91
  306.6 185.5 %all-gather.8.cloned.1.call-done = f32[256,128,128]{2,1,0:T(8,128)} async-done(((f32[4,128,128]{2,1,0:T(8,128)}), f32[256,128,128]{2,1,0:T(8,128)}) %all-gather.8.cloned.1.call-update) | async-done | bytes 16777232 | tf_op jit(solution)/shard_map/all_gather | solution.py:21
  492.1 11.6 %rev.7 = f32[64,4,128,128]{3,2,1,0:T(8,128)} reverse(f32[64,4,128,128]{3,2,1,0:T(8,128)} %bitcast.107), dimensions={0} | reverse | bytes 33554432 | tf_op jit(solution)/shard_map/rev | solution.py:23
  503.7 68.9 %while.29 = (s32[]{:T(128)}, f32[4,128,128]{2,1,0:T(8,128)S(1)}, s32[]{:T(128)}, f32[64,4]{1,0:T(8,128)S(1)}, f32[64,4,128,128]{3,2,1,0:T(8,128)}, /*index=5*/s32[]{:T(128)}, s32[]{:T(128)}) while((s32[]{:T(128)}, f32[4,128,128]{2,1,0:T(8,128)S(1)}, s32[]{:T(128)}, f32[64,4]{1,0:T(8,128)S(1)}, f32[64,4,128,128]{3,2,1,0:T(8,128)}, ...), condition=%wide.region_7.8_spmd.clone, body=%wide.region_6.7_spmd.clone.sunk | while | flops 262148 | bytes 786585 | solution.py:33
  504.8 1.1 fusion.56
  505.9 1.1 fusion.56
  508.1 1.1 fusion.56
  509.2 1.1 fusion.56
  510.3 1.1 fusion.56
  511.4 1.1 fusion.56
  512.4 1.1 fusion.56
  514.6 1.1 fusion.56
  515.7 1.1 fusion.56
  516.8 1.1 fusion.56
  517.9 1.1 fusion.56
  519.0 1.1 fusion.56
  520.1 1.1 fusion.56
  521.2 1.1 fusion.56
  522.3 1.1 fusion.56
  523.4 1.1 fusion.56
  524.5 1.1 fusion.56
  525.6 1.1 fusion.56
  526.7 1.1 fusion.56
  (272 shorter events, 127.0 us)
Async XLA Ops:
  7.2 19.2 %copy-start = (bf16[128,512]{1,0:T(8,128)(2,1)S(1)}, bf16[128,512]{1,0:T(8,128)(2,1)}, u32[]{:S(2)}) copy-start(bf16[128,512]{1,0:T(8,128)(2,1)} %param.13) | copy-start | bytes 393220
  7.2 211.1 %all-gather.6.cloned.1.call-start = ((), (), s32[]{:S(2)}) async-start(), calls=%async_computation | async-start | bytes 17039360 | tf_op jit(solution)/shard_map/all_gather | solution.py:21
  9.1 13.3 %collective-permute-start = (s32[1]{0:T(128)}, s32[1]{0:T(128)}, u32[]{:S(2)}, u32[]{:S(2)}) collective-permute-start(s32[1]{0:T(128)} %add.96), channel_id=1, source_target_pairs={{0,8},{8,16},{16,24},{24,32},{32,40},{40,48},{48,56},{56,64},{64,7... | collective-permute-start | bytes 20 | tf_op jit(solution)/shard_map/ppermute | solution.py:16
  27.3 464.8 %all-gather.8.cloned.1.call-start = ((), (), s32[]{:S(2)}) async-start(), calls=%async_computation.1 | async-start | bytes 17039360 | tf_op jit(solution)/shard_map/all_gather | solution.py:21
Sparse Core Ops, SparseCore 0:
  27.4 190.8 all-gather.5
  305.1 186.9 all-gather.7
where the time goes:
time: 588 us; the launch traced here: 582 us
  waiting for transfers between devices  256 us (44%)
  other arithmetic  139 us (24%)
  blocking collectives  136 us (23%)
  local copies, waits for them, and re-layouts  20.7 us (4%)
  between operations  16.1 us (3%)
    all_gather x2, waiting for transfers between devices, entering(): pieces = jax.tree.map(lambda part: lax.all_gather(part, axis), value)  251 us
    select_n x126, other arithmetic, lap(): jnp.where(position < mine, new, old)  133 us
    unnamed x1, blocking collectives  122 us
    psum x1, blocking collectives, per_device(): square_tot, cross_tot = lax.psum((square_sum, cross_sum), 'head')  14.2 us
  transfers between devices with their start and end apart: 3, of which 3 were waited for; matrix products, arithmetic and copies ran while one was open for 1% of the time, Pallas kernels for 0%

commit v1 on v0

v1 whole, which is shorter than its diff:
```python
import functools

import jax
import jax.numpy as jnp
from jax import lax
from jax.experimental import pallas as pl
from jax.experimental.pallas import tpu as pltpu
from jax.sharding import PartitionSpec as P

HEADS = 32
HEAD_DIM = 128
BLOCK = 128
LOCAL = 4
ROW = 16
ROWS = 4
PIECE = LOCAL * HEAD_DIM // ROW
PAD = 8

epsilon = 1e-06
f32 = jnp.float32
bf16 = jnp.bfloat16

VMEM = pl.BlockSpec(memory_space=pltpu.VMEM)
SMEM = pl.BlockSpec(memory_space=pltpu.SMEM)


def dot(a, b, a_dim, b_dim):
    return lax.dot_general(a, b, (((a_dim,), (b_dim,)), ((), ())), preferred_element_type=f32)


def square(row):
    return jnp.broadcast_to(row, (BLOCK, BLOCK))


def iota(axis):
    return lax.broadcasted_iota(jnp.int32, (BLOCK, BLOCK), axis).astype(f32)


def head(h):
    return slice(h * HEAD_DIM, (h + 1) * HEAD_DIM)


def outflow_of(doc_col, doc_row, rate):
    last = doc_row[:, BLOCK - 1 :]
    return jnp.where(doc_col == last, jnp.exp(-rate * (BLOCK - 1.0 - iota(0))), 0.0)


def inflow_of(doc_col, prev, rate):
    return jnp.where(doc_col == prev, jnp.exp(-rate * (iota(0) + 1.0)), 0.0)


def decays_of(doc_col, doc_row, rate):
    offset = iota(0) - iota(1)
    inside = (offset >= 0.0) & (doc_col == doc_row)
    return jnp.where(inside, jnp.exp(-rate * jnp.maximum(offset, 0.0)), 0.0)


def docs_of(docs):
    row = docs[...].astype(f32)
    wide = square(row)
    return wide.T, wide


def put_pieces(out, h, matrix):
    each = ROW // LOCAL
    for i in range(each):
        out[h * each + i, 0:PIECE, :] = matrix[i * PIECE : (i + 1) * PIECE]


def get_pieces(pieces, h):
    each = ROW // LOCAL
    return jnp.concatenate([pieces[h * each + i, 0:PIECE, :] for i in range(each)], axis=0)


def local_state_kernel(rates, docs, key, value, out):
    doc_col, doc_row = docs_of(docs)
    for h in range(LOCAL):
        outflow = outflow_of(doc_col, doc_row, rates[h])
        key_out = (key[:, head(h)].astype(f32) * outflow).astype(bf16)
        put_pieces(out, h, dot(key_out, value[:, head(h)], 0, 0))
    last = jnp.broadcast_to(doc_row[0:PAD, BLOCK - 1 :], (PAD, BLOCK))
    for i in range(ROW):
        out[i, PIECE:, :] = last


def intra_kernel(rates, docs, query, key, value, weights, attended):
    doc_col, doc_row = docs_of(docs)
    for h in range(LOCAL):
        scores = dot(query[:, head(h)], key[:, head(h)], 1, 1)
        low = (scores * decays_of(doc_col, doc_row, rates[h])).astype(bf16)
        weights[h] = low
        attended[:, head(h)] = dot(low, value[:, head(h)], 1, 0)


def my_place():
    place = lax.axis_index("seq")
    return place // ROW, place % ROW


def my_rate(rates):
    return rates[my_place()[1] // (ROW // LOCAL)]


def faded(rate, blocks):
    return jnp.exp(jnp.full((1, BLOCK), -BLOCK * blocks, f32) * rate)


def row_total_kernel(rates, pieces, out):
    fade = faded(my_rate(rates), 1.0)
    total = pieces[0, 0:PIECE, :]
    for z in range(1, ROW):
        same = pieces[z, PIECE : PIECE + 1, :] == pieces[z - 1, PIECE : PIECE + 1, :]
        total = jnp.where(same, fade, 0.0) * total + pieces[z, 0:PIECE, :]
    for x in range(ROWS):
        out[x, 0:PIECE, :] = total
        out[x, PIECE:, :] = pieces[ROW - 1, PIECE:, :]


def row_scan_kernel(rates, pieces, totals, out):
    rate, (mine, _) = my_rate(rates), my_place()
    fade = faded(rate, 1.0)
    before = jnp.maximum(mine - 1, 0)
    prev = totals[before, PIECE:, :]
    state = jnp.zeros((PIECE, BLOCK), f32)
    for x in range(ROWS - 1):
        same = (totals[x, PIECE : PIECE + 1, :] == prev[0:1]) & (x < mine)
        gap = jnp.maximum(mine - 1 - x, 0).astype(f32) * ROW
        state = state + jnp.where(same, faded(rate, gap), 0.0) * totals[x, 0:PIECE, :]
    prev = jnp.where(mine > 0, prev, -1.0)
    for z in range(ROW):
        out[z, 0:PIECE, :] = state
        out[z, PIECE:, :] = prev
        last = pieces[z, PIECE:, :]
        state = jnp.where(last[0:1] == prev[0:1], fade, 0.0) * state + pieces[z, 0:PIECE, :]
        prev = last


def attend_kernel(rates, docs, gain, query, grad, intra, states, attended, sums):
    doc_col, _ = docs_of(docs)
    prev = states[0, PIECE : PIECE + 1, :]
    squares = jnp.zeros((BLOCK, BLOCK), f32)
    crosses = jnp.zeros((BLOCK, BLOCK), f32)
    for h in range(LOCAL):
        low = get_pieces(states, h).astype(bf16)
        inflow = inflow_of(doc_col, prev, rates[h])
        both = intra[:, head(h)] + inflow * dot(query[:, head(h)], low, 1, 0)
        attended[:, head(h)] = both
        squares = squares + both * both
        crosses = crosses + gain[:, head(h)] * grad[:, head(h)].astype(f32) * both
    square_row = jnp.sum(squares.T, axis=0, keepdims=True)
    cross_row = jnp.sum(crosses.T, axis=0, keepdims=True)
    for i in range(sums.shape[0]):
        sums[i, 0:1, :] = square_row
        sums[i, 1:2, :] = cross_row


def grad_kernel(rates, docs, gain, query, grad, attended, states, sums, low_grad, out):
    doc_col, _ = docs_of(docs)
    prev = states[0, PIECE : PIECE + 1, :]
    both = jnp.sum(sums[...], axis=0)
    width = HEADS * HEAD_DIM
    inv_rms = lax.rsqrt(both[0:1] / width + epsilon)
    slope = both[1:2] * (inv_rms * inv_rms * inv_rms) / width
    inv_col, slope_col = square(inv_rms).T, square(slope).T
    for h in range(LOCAL):
        scaled = gain[:, head(h)] * grad[:, head(h)].astype(f32)
        low = (scaled * inv_col - attended[:, head(h)] * slope_col).astype(bf16)
        low_grad[:, head(h)] = low
        inflow = inflow_of(doc_col, prev, rates[h])
        query_in = (query[:, head(h)].astype(f32) * inflow).astype(bf16)
        put_pieces(out, h, dot(query_in, low, 0, 0))


def back_intra_kernel(
    rates, docs, query, key, value, weights, low_grad, states, query_grad, key_part, value_part
):
    doc_col, doc_row = docs_of(docs)
    prev = states[0, PIECE : PIECE + 1, :]
    for h in range(LOCAL):
        low = low_grad[:, head(h)]
        scores = dot(low, value[:, head(h)], 1, 1)
        grad_weights = (scores * decays_of(doc_col, doc_row, rates[h])).astype(bf16)
        state = get_pieces(states, h).astype(bf16)
        inflow = inflow_of(doc_col, prev, rates[h])
        whole = dot(grad_weights, key[:, head(h)], 1, 0) + inflow * dot(low, state, 1, 1)
        query_grad[:, head(h)] = whole.astype(bf16)
        key_part[:, head(h)] = dot(grad_weights, query[:, head(h)], 0, 0)
        value_part[:, head(h)] = dot(weights[h], low, 0, 0)


def back_total_kernel(rates, pieces, totals, grads, out):
    fade = faded(my_rate(rates), 1.0)
    total = grads[ROW - 1]
    mine, _ = my_place()
    before = totals[jnp.maximum(mine - 1, 0), PIECE : PIECE + 1, :]
    before = jnp.where(mine > 0, before, -1.0)
    for z in range(ROW - 2, -1, -1):
        older = pieces[z - 1, PIECE : PIECE + 1, :] if z else before
        same = pieces[z, PIECE : PIECE + 1, :] == older
        total = jnp.where(same, fade, 0.0) * total + grads[z]
    for x in range(ROWS):
        out[x] = total


def back_scan_kernel(rates, pieces, totals, grads, later, out):
    rate, (mine, _) = my_rate(rates), my_place()
    fade = faded(rate, 1.0)
    here = pieces[ROW - 1, PIECE : PIECE + 1, :]
    state = jnp.zeros((PIECE, BLOCK), f32)
    for x in range(1, ROWS):
        same = (totals[x - 1, PIECE : PIECE + 1, :] == here) & (x > mine)
        gap = jnp.maximum(x - 1 - mine, 0).astype(f32) * ROW
        state = state + jnp.where(same, faded(rate, gap), 0.0) * later[x]
    for z in range(ROW - 1, -1, -1):
        out[z] = state
        if z:
            same = pieces[z, PIECE : PIECE + 1, :] == pieces[z - 1, PIECE : PIECE + 1, :]
            state = jnp.where(same, fade, 0.0) * state + grads[z]


def finish_kernel(rates, docs, key, value, key_part, value_part, states, key_grad, value_grad):
    doc_col, doc_row = docs_of(docs)
    for h in range(LOCAL):
        low = get_pieces(states, h).astype(bf16)
        outflow = outflow_of(doc_col, doc_row, rates[h])
        more = outflow * dot(value[:, head(h)], low, 1, 1)
        key_grad[:, head(h)] = (key_part[:, head(h)] + more).astype(bf16)
        more = outflow * dot(key[:, head(h)], low, 1, 0)
        value_grad[:, head(h)] = (value_part[:, head(h)] + more).astype(bf16)


def call(kernel, name, outs, *args, flops=1):
    shapes = [jax.ShapeDtypeStruct(shape, dtype) for shape, dtype in outs]
    moved = sum(a.size * a.dtype.itemsize for a in (*args, *shapes))
    out = pl.pallas_call(
        kernel,
        out_shape=shapes,
        in_specs=[SMEM] + [VMEM] * (len(args) - 1),
        out_specs=[VMEM] * len(shapes),
        name=name,
        compiler_params=pltpu.CompilerParams(vmem_limit_bytes=32 * 1024 * 1024),
        cost_estimate=pl.CostEstimate(flops=flops, bytes_accessed=moved, transcendentals=0),
    )(*args)
    return out[0] if len(out) == 1 else out


def per_device(query, key, value, grad, gain, rates, doc_ids):
    along = [[x * ROW + z for z in range(ROW)] for x in range(ROWS)]
    across = [[x * ROW + z for x in range(ROWS)] for z in range(ROW)]
    swap_z = functools.partial(
        lax.all_to_all, axis_name="seq", split_axis=0, concat_axis=0, axis_index_groups=along, tiled=True
    )
    swap_x = functools.partial(
        lax.all_to_all, axis_name="seq", split_axis=0, concat_axis=0, axis_index_groups=across, tiled=True
    )
    docs = doc_ids.reshape(1, BLOCK)
    gain = gain.reshape(1, LOCAL * HEAD_DIM)
    wide = (BLOCK, LOCAL * HEAD_DIM)
    tall = (PIECE + PAD, BLOCK)
    one = 2 * LOCAL * BLOCK * BLOCK * HEAD_DIM

    local = call(local_state_kernel, "local_state", [((ROW, *tall), f32)], rates, docs, key, value, flops=one)
    pieces = swap_z(local)
    weights, intra = call(
        intra_kernel, "intra", [((LOCAL, BLOCK, BLOCK), bf16), (wide, f32)], rates, docs, query, key, value, flops=2 * one
    )
    total = call(row_total_kernel, "row_total", [((ROWS, *tall), f32)], rates, pieces)
    totals = swap_x(total)
    scanned = call(row_scan_kernel, "row_scan", [((ROW, *tall), f32)], rates, pieces, totals)
    states = swap_z(scanned)
    attended, sums = call(
        attend_kernel, "attend", [(wide, f32), ((8, 2, BLOCK), f32)], rates, docs, gain, query, grad, intra, states, flops=one
    )
    sums = lax.all_to_all(sums, "head", 0, 0, tiled=True)
    low_grad, local_grad = call(
        grad_kernel, "grad", [(wide, bf16), ((ROW, PIECE, BLOCK), f32)],
        rates, docs, gain, query, grad, attended, states, sums, flops=one,
    )
    grads = swap_z(local_grad)
    query_grad, key_part, value_part = call(
        back_intra_kernel, "back_intra", [(wide, bf16), (wide, f32), (wide, f32)],
        rates, docs, query, key, value, weights, low_grad, states, flops=5 * one,
    )
    back_total = call(back_total_kernel, "back_total", [((ROWS, PIECE, BLOCK), f32)], rates, pieces, totals, grads)
    later = swap_x(back_total)
    back = call(back_scan_kernel, "back_scan", [((ROW, PIECE, BLOCK), f32)], rates, pieces, totals, grads, later)
    states_out = swap_z(back)
    key_grad, value_grad = call(
        finish_kernel, "finish", [(wide, bf16), (wide, bf16)],
        rates, docs, key, value, key_part, value_part, states_out, flops=2 * one,
    )
    return query_grad, key_grad, value_grad


def solution(mesh):
    return jax.shard_map(
        per_device,
        mesh=mesh,
        in_specs=(
            P("seq", "head"),
            P("seq", "head"),
            P("seq", "head"),
            P("seq", "head"),
            P("head"),
            P("head"),
            P("seq"),
        ),
        out_specs=(P("seq", "head"), P("seq", "head"), P("seq", "head")),
        check_vma=False,
    )
```

time: 588 us -> 148 us (0.25)
  waiting for transfers between devices: 256 us -> 33.6 us
  other arithmetic: 139 us -> 0 us
  blocking collectives: 136 us -> 85.6 us
  local copies, waits for them, and re-layouts: 20.7 us -> 2.49 us
  between operations: 16.1 us -> 0.74 us
  Pallas kernels: 0 us -> 11.3 us
  starting transfers between devices: 5.19 us -> 12.1 us
    all_gather x2 -> x0, waiting for transfers between devices: 251 us -> none  [entering(): pieces = jax.tree.map(lambda part: lax.all_gather(part, axis), value)]
    select_n x128 -> x0, other arithmetic: 134 us -> none  [the longest x126 133 us: lap(): jnp.where(position < mine, new, old)]
    unnamed x1 -> x0, blocking collectives: 122 us -> none
    all_to_all x0 -> x5, blocking collectives: none -> 85.6 us  [the longest x1 35.8 us: per_device(): pieces = swap_z(local)]
    all_to_all x0 -> x2, waiting for transfers between devices: none -> 33.6 us  [the longest x1 18.2 us: per_device(): states = swap_z(scanned)]
    psum x1 -> x0, blocking collectives: 14.2 us -> none  [per_device(): square_tot, cross_tot = lax.psum((square_sum, cross_sum), 'head')]
    all_to_all x0 -> x2, starting transfers between devices: none -> 12.1 us  [the longest x1 6.31 us: per_device(): states = swap_z(scanned)]
    rev x2 -> x0, local copies, waits for them, and re-layouts: 11.6 us -> none  [entering(): pieces = jax.tree.map(lambda part: part[::-1], pieces)]
  transfers between devices with their start and end apart: 3 -> 2, of which waited for: 3 -> 2; matrix products, arithmetic and copies ran while one was open for 1% -> 0% of each run, Pallas kernels for 0% -> 2%
where the time goes in v1:
time: 148 us; the launch traced here: 146 us
  blocking collectives  85.6 us (58%)
  waiting for transfers between devices  33.6 us (23%)
  starting transfers between devices  12.1 us (8%)
  Pallas kernels  11.3 us (8%)
  local copies, waits for them, and re-layouts  2.49 us (2%)
    all_to_all x1, blocking collectives, per_device(): pieces = swap_z(local)  35.8 us
    all_to_all x1, blocking collectives, per_device(): grads = swap_z(local_grad)  24.1 us
    all_to_all x1, waiting for transfers between devices, per_device(): states = swap_z(scanned)  18.2 us
    all_to_all x1, waiting for transfers between devices, per_device(): states_out = swap_z(back)  15.4 us
    pallas_call x10, Pallas kernels, call(): pl.pallas_call(kernel, out_shape=shapes, in_specs=[SMEM] + [VMEM] * (len(...  11.3 us
    all_to_all x1, blocking collectives, per_device(): sums = lax.all_to_all(sums, 'head', 0, 0, tiled=True)  9.58 us
    all_to_all x1, blocking collectives, per_device(): totals = swap_x(total)  8.22 us
    all_to_all x1, blocking collectives, per_device(): later = swap_x(back_total)  7.88 us
  transfers between devices with their start and end apart: 2, of which 2 were waited for; matrix products, arithmetic and copies ran while one was open for 0% of the time, Pallas kernels for 2%

profile of v1, /device:TPU:6, one launch (start us, length us, event | category | flops | bytes accessed | tf_op | source)
XLA Modules:
  0.0 145.8 jit_solution(10945500864677890080)
XLA Ops:
  0.6 0.0 copy-start.6
  0.6 0.0 copy-start.7
  0.7 0.6 copy-done.6
  1.3 0.0 copy-done.7
  1.3 0.9 copy-done
  2.2 0.9 copy-done.2
  3.1 0.9 local_state.1
  4.0 35.8 %all_to_all.35.pieces = f32[16,40,128]{2,1,0:T(8,128)S(1)} all-to-all(f32[16,40,128]{2,1,0:T(8,128)S(1)} %local_state.1), channel_id=1, replica_groups={{0,8,16,24,32,40,48,56,64,72,80,88,96,104,112,120},{128,136,144,152,160..., dimensions={0} | all-to-all | bytes 655360 | tf_op jit(solution)/shard_map/all_to_all | solution.py:263
  39.8 0.6 row_total.1
  40.4 8.2 %all_to_all.36.totals = f32[4,40,128]{2,1,0:T(8,128)S(1)} all-to-all(f32[4,40,128]{2,1,0:T(8,128)S(1)} %row_total.1), channel_id=1, replica_groups={{0,128,256,384},{8,136,264,392},{16,144,272,400},{24,152,280,408},{32,1..., dimensions={0} | all-to-all | bytes 163840 | tf_op jit(solution)/shard_map/all_to_all | solution.py:268
  48.6 1.3 row_scan.1
  49.9 6.3 %all-to-all-start.2 = ((f32[16,40,128]{2,1,0:T(8,128)}), f32[16,40,128]{2,1,0:T(8,128)S(1)}, u32[]{:S(2)}, u32[]{:S(2)}) async-start(f32[16,40,128]{2,1,0:T(8,128)} %row_scan.1), calls=%async_computation.2 | async-start | bytes 655360 | tf_op jit(solution)/shard_map/all_to_all | solution.py:270
  56.2 0.0 copy-done.1
  56.2 0.0 copy-done.3
  56.3 0.0 copy-done.4
  56.3 0.0 copy-start.5
  56.3 1.3 intra.1
  57.6 0.0 copy-start.8
  57.6 18.2 %all-to-all-done.2.states = f32[16,40,128]{2,1,0:T(8,128)S(1)} async-done(((f32[16,40,128]{2,1,0:T(8,128)}), f32[16,40,128]{2,1,0:T(8,128)S(1)}, u32[]{:S(2)}, u32[]{:S(2)}) %all-to-all-start.2) | async-done | bytes 327712 | tf_op jit(solution)/shard_map/all_to_all | solution.py:270
  75.8 0.0 copy-done.5
  75.8 0.0 copy-done.8
  75.8 0.8 attend.1
  76.6 9.6 %all_to_all.37.sums = f32[8,2,128]{2,1,0:T(2,128)S(1)} all-to-all(f32[8,2,128]{2,1,0:T(2,128)S(1)} %get-tuple-element.17), channel_id=1, replica_groups=mesh['seq'=64,'head'=8] {'head'}, dimensions={0} | all-to-all | bytes 16384 | tf_op jit(solution)/shard_map/all_to_all | solution.py:274
  86.2 0.9 grad.4
  87.0 24.1 %all_to_all.38.grads = f32[16,32,128]{2,1,0:T(8,128)S(1)} all-to-all(f32[16,32,128]{2,1,0:T(8,128)S(1)} %get-tuple-element.22), channel_id=1, replica_groups={{0,8,16,24,32,40,48,56,64,72,80,88,96,104,112,120},{128,136,144,152,160..., dimensions={0} | all-to-all | bytes 524288 | tf_op jit(solution)/shard_map/all_to_all | solution.py:279
  111.2 0.6 back_total.1
  111.8 7.9 %all_to_all.39.later = f32[4,32,128]{2,1,0:T(8,128)S(1)} all-to-all(f32[4,32,128]{2,1,0:T(8,128)S(1)} %back_total.1), channel_id=1, replica_groups={{0,128,256,384},{8,136,264,392},{16,144,272,400},{24,152,280,408},{32,1..., dimensions={0} | all-to-all | bytes 131072 | tf_op jit(solution)/shard_map/all_to_all | solution.py:285
  119.7 1.3 back_scan.1
  121.0 5.7 %all-to-all-start.6 = ((f32[16,32,128]{2,1,0:T(8,128)}), f32[16,32,128]{2,1,0:T(8,128)S(1)}, u32[]{:S(2)}, u32[]{:S(2)}) async-start(f32[16,32,128]{2,1,0:T(8,128)} %back_scan.1), calls=%async_computation.6 | async-start | bytes 524288 | tf_op jit(solution)/shard_map/all_to_all | solution.py:287
  126.7 2.1 %back_intra.1 = (bf16[128,512]{1,0:T(8,128)(2,1)}, f32[128,512]{1,0:T(8,128)S(1)}, f32[128,512]{1,0:T(8,128)S(1)}) custom-call(f32[4]{0:T(128)S(1)} %copy-done.6, s32[1,128]{1,0:T(1,128)S(1)} %bitcast.6, bf16[128,512]{1,0:T(8,128)(2,1)S(1)} %copy-done.4, bf16[128,512]{1,0:T(8,128)(2,1)S(1)} %copy-done.1, bf16[128,512]{1,0:T(8,128)(2,1)S(1)} %copy-done.3, ...), custom_call_target="tpu_custom_call" | custom-call | flops 83886080 | bytes 1638928 | tf_op jit(solution)/shard_map/back_intra/pallas_call | solution.py:235
  128.9 15.4 %all-to-all-done.6.states = f32[16,32,128]{2,1,0:T(8,128)S(1)} async-done(((f32[16,32,128]{2,1,0:T(8,128)}), f32[16,32,128]{2,1,0:T(8,128)S(1)}, u32[]{:S(2)}, u32[]{:S(2)}) %all-to-all-start.6) | async-done | bytes 262176 | tf_op jit(solution)/shard_map/all_to_all | solution.py:287
  144.3 1.5 %finish.1 = (bf16[128,512]{1,0:T(8,128)(2,1)}, bf16[128,512]{1,0:T(8,128)(2,1)}) custom-call(f32[4]{0:T(128)S(1)} %copy-done.6, s32[1,128]{1,0:T(1,128)S(1)} %bitcast.7, bf16[128,512]{1,0:T(8,128)(2,1)S(1)} %copy-done.1, bf16[128,512]{1,0:T(8,128)(2,1)S(1)} %copy-done.3, f32[128,512]{1,0:T(8,128)S(1)} %get-tuple-element.20.key_part, ...), custom_call_target="tpu_custom_call" | custom-call | flops 33554432 | bytes 1311248 | tf_op jit(solution)/shard_map/finish/pallas_call | solution.py:235
  (5 shorter events, 0.0 us)
Async XLA Ops:
  0.6 0.7 copy-start.6
  0.6 0.7 copy-start.7
  1.3 0.9 copy-start
  2.2 0.9 copy-start.2
  49.9 6.3 %copy-start.1 = (bf16[128,512]{1,0:T(8,128)(2,1)S(1)}, bf16[128,512]{1,0:T(8,128)(2,1)}, u32[]{:S(2)}) copy-start(bf16[128,512]{1,0:T(8,128)(2,1)} %key.7) | copy-start | bytes 393220
  49.9 6.3 %copy-start.3 = (bf16[128,512]{1,0:T(8,128)(2,1)S(1)}, bf16[128,512]{1,0:T(8,128)(2,1)}, u32[]{:S(2)}) copy-start(bf16[128,512]{1,0:T(8,128)(2,1)} %value.7) | copy-start | bytes 393220
  49.9 6.3 %copy-start.4 = (bf16[128,512]{1,0:T(8,128)(2,1)S(1)}, bf16[128,512]{1,0:T(8,128)(2,1)}, u32[]{:S(2)}) copy-start(bf16[128,512]{1,0:T(8,128)(2,1)} %query.7) | copy-start | bytes 393220
  49.9 25.8 %all-to-all-start.2 = ((f32[16,40,128]{2,1,0:T(8,128)}), f32[16,40,128]{2,1,0:T(8,128)S(1)}, u32[]{:S(2)}, u32[]{:S(2)}) async-start(f32[16,40,128]{2,1,0:T(8,128)} %row_scan.1), calls=%async_computation.2 | async-start | bytes 655360 | tf_op jit(solution)/shard_map/all_to_all | solution.py:270
  56.3 19.5 %copy-start.5 = (bf16[128,512]{1,0:T(8,128)(2,1)S(1)}, bf16[128,512]{1,0:T(8,128)(2,1)}, u32[]{:S(2)}) copy-start(bf16[128,512]{1,0:T(8,128)(2,1)} %grad.5) | copy-start | bytes 393220
  57.6 18.2 %copy-start.8 = (f32[512]{0:T(512)S(1)}, f32[512]{0:T(512)}, u32[]{:S(2)}) copy-start(f32[512]{0:T(512)} %param.11) | copy-start | bytes 6148
  121.0 23.3 %all-to-all-start.6 = ((f32[16,32,128]{2,1,0:T(8,128)}), f32[16,32,128]{2,1,0:T(8,128)S(1)}, u32[]{:S(2)}, u32[]{:S(2)}) async-start(f32[16,32,128]{2,1,0:T(8,128)} %back_scan.1), calls=%async_computation.6 | async-start | bytes 524288 | tf_op jit(solution)/shard_map/all_to_all | solution.py:287

commit v2 on v0

v2 whole, which is shorter than its diff:
```python
import functools

import jax
import jax.numpy as jnp
from jax import lax
from jax.experimental import pallas as pl
from jax.experimental.pallas import tpu as pltpu
from jax.sharding import PartitionSpec as P

HEADS = 32
HEAD_DIM = 128
BLOCK = 128
LOCAL = 4
GROUPS = 4
ROWS = 4
HEAD_PARTS = 8
DOC = HEAD_DIM
TALL = HEAD_DIM + 8

epsilon = 1e-06
f32 = jnp.float32
bf16 = jnp.bfloat16

VMEM = pl.BlockSpec(memory_space=pltpu.VMEM)
SMEM = pl.BlockSpec(memory_space=pltpu.SMEM)


def dot(a, b, a_dim, b_dim):
    return lax.dot_general(a, b, (((a_dim,), (b_dim,)), ((), ())), preferred_element_type=f32)


def square(row):
    return jnp.broadcast_to(row, (BLOCK, BLOCK))


def iota(axis):
    return lax.broadcasted_iota(jnp.int32, (BLOCK, BLOCK), axis).astype(f32)


def head(h):
    start = h * HEAD_DIM
    if not isinstance(h, int):
        start = pl.multiple_of(start, HEAD_DIM)
    return pl.ds(start, HEAD_DIM)


def outflow_of(doc_row, rate):
    doc_col = square(doc_row).T
    last = doc_row[:, BLOCK - 1 :]
    return jnp.where(doc_col == last, jnp.exp(-rate * (BLOCK - 1.0 - iota(0))), 0.0)


def inflow_of(doc_row, rate):
    doc_col = square(doc_row).T
    return jnp.where(doc_col == doc_row[:, 0:1], jnp.exp(-rate * (iota(0) + 1.0)), 0.0)


def decays_of(doc_row, rate):
    doc_col = square(doc_row).T
    offset = iota(0) - iota(1)
    inside = (offset >= 0.0) & (doc_col == doc_row)
    return jnp.where(inside, jnp.exp(-rate * jnp.maximum(offset, 0.0)), 0.0)


def place():
    mine = lax.axis_index("seq")
    return mine // (GROUPS * LOCAL), (mine // LOCAL) % GROUPS, mine % LOCAL


def faded(rate, blocks):
    return jnp.exp(jnp.full((1, BLOCK), -BLOCK * blocks, f32) * rate)


def passing(same, fade):
    return jnp.where(same, fade, 0.0)


def first_doc(pieces, i):
    return jnp.broadcast_to(pieces[i, DOC : DOC + 1, 0:1], (1, BLOCK))


def last_doc(pieces, i):
    return jnp.broadcast_to(pieces[i, DOC : DOC + 1, BLOCK - 1 :], (1, BLOCK))


def row_doc(row, k):
    return row[k, DOC : DOC + 1, :]


def before_row(x, earlier):
    return jnp.where(x > 0, earlier[DOC : DOC + 1, :], -1.0)


def before_group(x, k, row, earlier):
    inside = row_doc(row, jnp.maximum(k - 1, 0))
    return jnp.where(k > 0, inside, before_row(x, earlier))


def local_state_kernel(rates, docs, key, value, out):
    doc_row = docs[...].astype(f32)
    for h in range(LOCAL):
        key_out = (key[:, head(h)].astype(f32) * outflow_of(doc_row, rates[h])).astype(bf16)
        out[h, 0:HEAD_DIM, :] = dot(key_out, value[:, head(h)], 0, 0)
        out[h, DOC:, :] = jnp.broadcast_to(doc_row, (TALL - DOC, BLOCK))


def intra_kernel(rates, docs, gain, query, key, value, grad, weights, *outs):
    doc_row = docs[...].astype(f32)
    member = place()[2]
    for d in range(LOCAL):
        h = member ^ d
        scores = dot(query[:, head(h)], key[:, head(h)], 1, 1)
        low = (scores * decays_of(doc_row, rates[h])).astype(bf16)
        weights[d] = low
        outs[d][0] = dot(low, value[:, head(h)], 1, 0)
        outs[d][1] = query[:, head(h)].astype(f32)
        outs[d][2] = gain[:, head(h)] * grad[:, head(h)].astype(f32)


def back_intra_kernel(
    rates, docs, query, key, value, weights, in0, in1, in2, in3, query_grad, key_part, value_part
):
    doc_row = docs[...].astype(f32)
    member = place()[2]
    for d, piece in enumerate((in0, in1, in2, in3)):
        h = member ^ d
        low = piece[0].astype(bf16)
        scores = dot(low, value[:, head(h)], 1, 1)
        grad_weights = (scores * decays_of(doc_row, rates[h])).astype(bf16)
        whole = dot(grad_weights, key[:, head(h)], 1, 0) + piece[1]
        query_grad[:, head(h)] = whole.astype(bf16)
        key_part[:, head(h)] = dot(grad_weights, query[:, head(h)], 0, 0)
        value_part[:, head(h)] = dot(weights[d], low, 0, 0)


def finish_kernel(rates, docs, key, value, key_part, value_part, states, key_grad, value_grad):
    doc_row = docs[...].astype(f32)
    for h in range(LOCAL):
        low = states[h].astype(bf16)
        outflow = outflow_of(doc_row, rates[h])
        more = outflow * dot(value[:, head(h)], low, 1, 1)
        key_grad[:, head(h)] = (key_part[:, head(h)] + more).astype(bf16)
        more = outflow * dot(key[:, head(h)], low, 1, 0)
        value_grad[:, head(h)] = (value_part[:, head(h)] + more).astype(bf16)


def group_total_kernel(rates, pieces, out):
    fade = faded(rates[place()[2]], 1.0)
    total = pieces[0, 0:HEAD_DIM, :]
    for i in range(1, LOCAL):
        same = last_doc(pieces, i) == last_doc(pieces, i - 1)
        total = passing(same, fade) * total + pieces[i, 0:HEAD_DIM, :]
    last = jnp.broadcast_to(last_doc(pieces, LOCAL - 1), (TALL - DOC, BLOCK))
    for k in range(GROUPS):
        out[k, 0:HEAD_DIM, :] = total
        out[k, DOC:, :] = last


def row_total_kernel(rates, row, out):
    fade = faded(rates[place()[2]], 1.0 * LOCAL)
    total = row[0, 0:HEAD_DIM, :]
    for k in range(1, GROUPS):
        same = row_doc(row, k) == row_doc(row, k - 1)
        total = passing(same, fade) * total + row[k, 0:HEAD_DIM, :]
    out[0:HEAD_DIM, :] = total
    out[DOC:, :] = row[GROUPS - 1, DOC:, :]


def attend_kernel(
    rates, pieces, row, near, far, in0, in1, in2, in3, attended, state_low, sums
):
    x, group, member = place()
    rate = rates[member]
    prev = before_row(x, near)
    same = (far[DOC : DOC + 1, :] == prev) & (x > 1)
    state = near[0:HEAD_DIM, :] + passing(same, faded(rate, 16.0)) * far[0:HEAD_DIM, :]
    for k in range(GROUPS - 1):
        last = row_doc(row, k)
        longer = passing(last == prev, faded(rate, 1.0 * LOCAL)) * state + row[k, 0:HEAD_DIM, :]
        state = jnp.where(k < group, longer, state)
        prev = jnp.where(k < group, last, prev)
    for i in range(LOCAL):
        low = passing(first_doc(pieces, i) == prev, 1.0) * state
        state_low[i] = low.astype(bf16)
        last = last_doc(pieces, i)
        if i < LOCAL - 1:
            state = passing(last == prev, faded(rate, 1.0)) * state + pieces[i, 0:HEAD_DIM, :]
        prev = last
    line = lax.broadcasted_iota(jnp.int32, (2 * LOCAL, BLOCK), 0)
    both = jnp.zeros((2 * LOCAL, BLOCK), f32)
    for d, piece in enumerate((in0, in1, in2, in3)):
        i = member ^ d
        inflow = inflow_of(pieces[i, DOC : DOC + 1, :], rate)
        whole = piece[0] + inflow * dot(piece[1].astype(bf16), state_low[i], 1, 0)
        attended[d] = whole
        squares = jnp.sum((whole * whole).T, axis=0, keepdims=True)
        crosses = jnp.sum((whole * piece[2]).T, axis=0, keepdims=True)
        both = both + jnp.where(line == i, squares, 0.0) + jnp.where(line == LOCAL + i, crosses, 0.0)
    for j in range(sums.shape[0]):
        sums[j] = both


def grad_kernel(
    rates, pieces, row, near, in0, in1, in2, in3, attended, state_low, sums, *outs
):
    x, group, member = place()
    rate = rates[member]
    both = jnp.sum(sums[...], axis=0)
    line = lax.broadcasted_iota(jnp.int32, (2 * LOCAL, BLOCK), 0)
    width = HEADS * HEAD_DIM
    local_grads, totals = outs[LOCAL:]
    for d, piece in enumerate((in0, in1, in2, in3)):
        i = member ^ d
        square_sum = jnp.sum(jnp.where(line == i, both, 0.0), axis=0, keepdims=True)
        cross_sum = jnp.sum(jnp.where(line == LOCAL + i, both, 0.0), axis=0, keepdims=True)
        inv_rms = lax.rsqrt(square_sum / width + epsilon)
        slope = cross_sum * (inv_rms * inv_rms * inv_rms) / width
        low = (piece[2] * square(inv_rms).T - attended[d] * square(slope).T).astype(bf16)
        inflow = inflow_of(pieces[i, DOC : DOC + 1, :], rate)
        outs[d][0] = low.astype(f32)
        outs[d][1] = inflow * dot(low, state_low[i], 1, 1)
        local_grads[i] = dot((piece[1] * inflow).astype(bf16), low, 0, 0)
    prev = before_group(x, group, row, near)
    fade = faded(rate, 1.0)
    total = jnp.zeros((HEAD_DIM, HEAD_DIM), f32)
    for i in range(LOCAL - 1, -1, -1):
        older = last_doc(pieces, i - 1) if i else prev
        mine = passing(first_doc(pieces, i) == older, 1.0) * local_grads[i]
        local_grads[i] = mine
        total = passing(last_doc(pieces, i) == older, fade) * total + mine
    for k in range(GROUPS):
        totals[k] = total


def back_row_kernel(rates, row, near, grads, out):
    x, _, member = place()
    fade = faded(rates[member], 1.0 * LOCAL)
    total = grads[GROUPS - 1]
    for k in range(GROUPS - 2, -1, -1):
        older = row_doc(row, k - 1) if k else before_row(x, near)
        total = passing(row_doc(row, k) == older, fade) * total + grads[k]
    out[0:HEAD_DIM, :] = total
    out[DOC:, :] = row[GROUPS - 1, DOC:, :]


def back_state_kernel(rates, pieces, row, grads, near, far, local_grads, out):
    x, group, member = place()
    rate = rates[member]
    same = (near[DOC : DOC + 1, :] == row_doc(row, GROUPS - 1)) & (x < ROWS - 2)
    state = near[0:HEAD_DIM, :] + passing(same, faded(rate, 16.0)) * far[0:HEAD_DIM, :]
    for k in range(GROUPS - 1, 0, -1):
        same = row_doc(row, k) == row_doc(row, k - 1)
        longer = passing(same, faded(rate, 1.0 * LOCAL)) * state + grads[k]
        state = jnp.where(k > group, longer, state)
    for i in range(LOCAL - 1, -1, -1):
        out[i] = state
        if i:
            same = last_doc(pieces, i) == last_doc(pieces, i - 1)
            state = passing(same, faded(rate, 1.0)) * state + local_grads[i]


def call(kernel, name, outs, *args, flops=1):
    shapes = [jax.ShapeDtypeStruct(shape, dtype) for shape, dtype in outs]
    moved = sum(a.size * a.dtype.itemsize for a in (*args, *shapes))
    out = pl.pallas_call(
        kernel,
        out_shape=shapes,
        in_specs=[SMEM] + [VMEM] * (len(args) - 1),
        out_specs=[VMEM] * len(shapes),
        name=name,
        compiler_params=pltpu.CompilerParams(vmem_limit_bytes=32 * 1024 * 1024),
        cost_estimate=pl.CostEstimate(flops=flops, bytes_accessed=moved, transcendentals=0),
    )(*args)
    return out[0] if len(out) == 1 else out


def per_device(query, key, value, grad, gain, rates, doc_ids):
    row_len = GROUPS * LOCAL
    blocks = range(ROWS * row_len)
    near_groups = [[i + j for j in range(LOCAL)] for i in blocks if i % LOCAL == 0]
    far_groups = [
        [x * row_len + k * LOCAL + j for k in range(GROUPS)] for x in range(ROWS) for j in range(LOCAL)
    ]
    sum_groups = [[i * HEAD_PARTS + h for i in near for h in range(HEAD_PARTS)] for near in near_groups]
    swap = functools.partial(lax.all_to_all, axis_name="seq", split_axis=0, concat_axis=0, tiled=True)

    def partner(piece, d):
        return lax.ppermute(piece, "seq", [(i, i ^ d) for i in blocks]) if d else piece

    def to_row(piece, by):
        pairs = [(i, i + by * row_len) for i in blocks if 0 <= i + by * row_len < len(blocks)]
        return lax.ppermute(piece, "seq", pairs)

    docs = doc_ids.reshape(1, BLOCK)
    gain = gain.reshape(1, LOCAL * HEAD_DIM)
    wide = (BLOCK, LOCAL * HEAD_DIM)
    tall = (TALL, HEAD_DIM)
    mat = (BLOCK, HEAD_DIM)
    one = 2 * LOCAL * BLOCK * BLOCK * HEAD_DIM

    local = call(local_state_kernel, "local_state", [((LOCAL, *tall), f32)], rates, docs, key, value, flops=one)
    pieces = swap(local, axis_index_groups=near_groups)
    total = call(group_total_kernel, "group_total", [((GROUPS, *tall), f32)], rates, pieces)
    row = swap(total, axis_index_groups=far_groups)
    weights, *sent = call(
        intra_kernel, "intra", [((LOCAL, *mat), bf16)] + [((3, *mat), f32)] * LOCAL,
        rates, docs, gain, query, key, value, grad, flops=2 * one,
    )
    tokens = [partner(piece, d) for d, piece in enumerate(sent)]
    row_total = call(row_total_kernel, "row_total", [(tall, f32)], rates, row)
    near, far = to_row(row_total, 1), to_row(row_total, 2)
    attended, state_low, sums = call(
        attend_kernel, "attend",
        [((LOCAL, *mat), f32), ((LOCAL, *mat), bf16), ((LOCAL * HEAD_PARTS, 2 * LOCAL, BLOCK), f32)],
        rates, pieces, row, near, far, *tokens, flops=one,
    )
    sums = lax.all_to_all(sums, ("seq", "head"), 0, 0, axis_index_groups=sum_groups, tiled=True)
    *sent, local_grads, totals = call(
        grad_kernel, "grad", [((2, *mat), f32)] * LOCAL + [((LOCAL, *mat), f32), ((GROUPS, *mat), f32)],
        rates, pieces, row, near, *tokens, attended, state_low, sums, flops=2 * one,
    )
    row_grads = swap(totals, axis_index_groups=far_groups)
    back = [partner(piece, d) for d, piece in enumerate(sent)]
    query_grad, key_part, value_part = call(
        back_intra_kernel, "back_intra", [(wide, bf16), (wide, f32), (wide, f32)],
        rates, docs, query, key, value, weights, *back, flops=4 * one,
    )
    back_total = call(back_row_kernel, "back_row", [(tall, f32)], rates, row, near, row_grads)
    later, latest = to_row(back_total, -1), to_row(back_total, -2)
    states = call(
        back_state_kernel, "back_state", [((LOCAL, *mat), f32)],
        rates, pieces, row, row_grads, later, latest, local_grads,
    )
    states, key_part, value_part = lax.optimization_barrier((states, key_part, value_part))
    states = swap(states, axis_index_groups=near_groups)
    key_grad, value_grad = call(
        finish_kernel, "finish", [(wide, bf16), (wide, bf16)],
        rates, docs, key, value, key_part, value_part, states, flops=2 * one,
    )
    return query_grad, key_grad, value_grad


def solution(mesh):
    return jax.shard_map(
        per_device,
        mesh=mesh,
        in_specs=(
            P("seq", "head"),
            P("seq", "head"),
            P("seq", "head"),
            P("seq", "head"),
            P("head"),
            P("head"),
            P("seq"),
        ),
        out_specs=(P("seq", "head"), P("seq", "head"), P("seq", "head")),
        check_vma=False,
    )
```

time: 588 us -> 137 us (0.23)
  waiting for transfers between devices: 256 us -> 24.8 us
  other arithmetic: 139 us -> 0 us
  blocking collectives: 136 us -> 47.7 us
  starting transfers between devices: 5.19 us -> 47.4 us
  local copies, waits for them, and re-layouts: 20.7 us -> 2.48 us
  between operations: 16.1 us -> 0.84 us
  Pallas kernels: 0 us -> 11.7 us
    all_gather x2 -> x0, waiting for transfers between devices: 251 us -> none  [entering(): pieces = jax.tree.map(lambda part: lax.all_gather(part, axis), value)]
    select_n x128 -> x0, other arithmetic: 134 us -> none  [the longest x126 133 us: lap(): jnp.where(position < mine, new, old)]
    unnamed x1 -> x0, blocking collectives: 122 us -> none
    all_to_all x0 -> x3, blocking collectives: none -> 47.7 us  [the longest x1 17.4 us: per_device(): lax.all_to_all(sums, ('seq', 'head'), 0, 0, axis_index_groups=sum_groups,...]
    ppermute x1 -> x10, starting transfers between devices: 5.11 us -> 27.9 us  [the longest x6 20.2 us: partner(): lax.ppermute(piece, 'seq', [(i, i ^ d) for i in blocks])]
    all_to_all x0 -> x2, waiting for transfers between devices: none -> 19.6 us  [the longest x1 10.4 us: per_device(): row = swap(total, axis_index_groups=far_groups)]
    all_to_all x0 -> x2, starting transfers between devices: none -> 19.4 us  [the longest x1 12.5 us: per_device(): row = swap(total, axis_index_groups=far_groups)]
    psum x1 -> x0, blocking collectives: 14.2 us -> none  [per_device(): square_tot, cross_tot = lax.psum((square_sum, cross_sum), 'head')]
  transfers between devices with their start and end apart: 3 -> 12, of which waited for: 3 -> 4; matrix products, arithmetic and copies ran while one was open for 1% -> 0% of each run, Pallas kernels for 0% -> 3%
where the time goes in v2:
time: 137 us; the launch traced here: 135 us
  blocking collectives  47.7 us (35%)
  starting transfers between devices  47.4 us (35%)
  waiting for transfers between devices  24.8 us (18%)
  Pallas kernels  11.7 us (9%)
  local copies, waits for them, and re-layouts  2.48 us (2%)
    ppermute x6, starting transfers between devices, partner(): lax.ppermute(piece, 'seq', [(i, i ^ d) for i in blocks])  20.2 us
    all_to_all x1, blocking collectives, per_device(): lax.all_to_all(sums, ('seq', 'head'), 0, 0, axis_index_groups=sum_groups,...  17.4 us
    all_to_all x1, blocking collectives, per_device(): states = swap(states, axis_index_groups=near_groups)  15.4 us
    all_to_all x1, blocking collectives, per_device(): pieces = swap(local, axis_index_groups=near_groups)  14.9 us
    all_to_all x1, starting transfers between devices, per_device(): row = swap(total, axis_index_groups=far_groups)  12.5 us
    pallas_call x10, Pallas kernels, call(): pl.pallas_call(kernel, out_shape=shapes, in_specs=[SMEM] + [VMEM] * (len(...  11.7 us
    all_to_all x1, waiting for transfers between devices, per_device(): row = swap(total, axis_index_groups=far_groups)  10.4 us
    all_to_all x1, waiting for transfers between devices, per_device(): row_grads = swap(totals, axis_index_groups=far_groups)  9.24 us
  transfers between devices with their start and end apart: 12, of which 4 were waited for; matrix products, arithmetic and copies ran while one was open for 0% of the time, Pallas kernels for 3%

profile of v2, /device:TPU:6, one launch (start us, length us, event | category | flops | bytes accessed | tf_op | source)
XLA Modules:
  0.0 135.0 jit_solution(4642329918850185105)
XLA Ops:
  0.7 0.6 copy-done.6
  1.3 0.9 copy-done
  2.2 0.9 copy-done.2
  3.1 0.9 local_state.1
  4.0 14.9 %all_to_all.25.pieces = f32[4,136,128]{2,1,0:T(8,128)S(1)} all-to-all(f32[4,136,128]{2,1,0:T(8,128)S(1)} %local_state.1), channel_id=1, replica_groups={{0,8,16,24},{32,40,48,56},{64,72,80,88},{96,104,112,120},{128,136,144,1..., dimensions={0} | all-to-all | bytes 557056 | tf_op jit(solution)/shard_map/all_to_all | solution.py:302
  18.9 1.4 %group_total.1 = f32[4,136,128]{2,1,0:T(8,128)} custom-call(f32[4]{0:T(128)S(1)} %copy-done.6, f32[4,136,128]{2,1,0:T(8,128)S(1)} %all_to_all.25.pieces), custom_call_target="tpu_custom_call" | custom-call | flops 1 | bytes 557072 | tf_op jit(solution)/shard_map/group_total/pallas_call | solution.py:265
  20.3 12.5 %all-to-all-start.1 = ((f32[4,136,128]{2,1,0:T(8,128)}), f32[4,136,128]{2,1,0:T(8,128)S(1)}, u32[]{:S(2)}, u32[]{:S(2)}) async-start(f32[4,136,128]{2,1,0:T(8,128)} %group_total.1), calls=%async_computation.1 | async-start | bytes 557056 | tf_op jit(solution)/shard_map/all_to_all | solution.py:304
  32.8 1.3 intra.1
  34.1 2.4 %collective-permute-start.1 = (f32[3,128,128]{2,1,0:T(8,128)S(1)}, f32[3,128,128]{2,1,0:T(8,128)S(1)}, u32[]{:S(2)}, u32[]{:S(2)}) collective-permute-start(f32[3,128,128]{2,1,0:T(8,128)S(1)} %get-tuple-element.27), channel_id=1, source_target_pairs={{0,8},{8,0},{16,24},{24,16},{32,40},{40,32},{48,56},{56,48},{64,72... | collective-permute-start | bytes 589832 | tf_op jit(solution)/shard_map/ppermute | solution.py:288
  36.6 3.4 %collective-permute-start.2 = (f32[3,128,128]{2,1,0:T(8,128)S(1)}, f32[3,128,128]{2,1,0:T(8,128)S(1)}, u32[]{:S(2)}, u32[]{:S(2)}) collective-permute-start(f32[3,128,128]{2,1,0:T(8,128)S(1)} %get-tuple-element.28), channel_id=1, source_target_pairs={{0,16},{8,24},{16,0},{24,8},{32,48},{40,56},{48,32},{56,40},{64,80... | collective-permute-start | bytes 589832 | tf_op jit(solution)/shard_map/ppermute | solution.py:288
  40.0 4.3 %collective-permute-start.3 = (f32[3,128,128]{2,1,0:T(8,128)S(1)}, f32[3,128,128]{2,1,0:T(8,128)S(1)}, u32[]{:S(2)}, u32[]{:S(2)}) collective-permute-start(f32[3,128,128]{2,1,0:T(8,128)S(1)} %get-tuple-element.29), channel_id=1, source_target_pairs={{0,24},{8,16},{16,8},{24,0},{32,56},{40,48},{48,40},{56,32},{64,88... | collective-permute-start | bytes 589832 | tf_op jit(solution)/shard_map/ppermute | solution.py:288
  44.3 10.4 %all-to-all-done.1.row = f32[4,136,128]{2,1,0:T(8,128)S(1)} async-done(((f32[4,136,128]{2,1,0:T(8,128)}), f32[4,136,128]{2,1,0:T(8,128)S(1)}, u32[]{:S(2)}, u32[]{:S(2)}) %all-to-all-start.1) | async-done | bytes 278560 | tf_op jit(solution)/shard_map/all_to_all | solution.py:304
  54.7 0.6 row_total.1
  55.3 1.3 collective-permute-start.4
  56.6 1.3 collective-permute-start
  57.9 1.8 %collective-permute-done.2.in2 = f32[3,128,128]{2,1,0:T(8,128)S(1)} collective-permute-done((f32[3,128,128]{2,1,0:T(8,128)S(1)}, f32[3,128,128]{2,1,0:T(8,128)S(1)}, u32[]{:S(2)}, u32[]{:S(2)}) %collective-permute-start.2) | collective-permute-done | bytes 196640 | tf_op jit(solution)/shard_map/ppermute | solution.py:288
  59.7 3.3 %collective-permute-done.4.far = f32[136,128]{1,0:T(8,128)S(1)} collective-permute-done((f32[136,128]{1,0:T(8,128)S(1)}, f32[136,128]{1,0:T(8,128)S(1)}, u32[]{:S(2)}, u32[]{:S(2)}) %collective-permute-start.4) | collective-permute-done | bytes 69664 | tf_op jit(solution)/shard_map/ppermute | solution.py:292
  63.0 1.0 attend.1
  64.0 17.4 %all_to_all.26.sums = f32[32,8,128]{2,1,0:T(8,128)S(1)} all-to-all(f32[32,8,128]{2,1,0:T(8,128)S(1)} %get-tuple-element.32), channel_id=1, replica_groups={{0,1,2,3,4,5,6,7,8,9,10,11,12,13,14,15,16,17,18,19,20,21,22,23,24,25,26..., dimensions={0} | all-to-all | bytes 262144 | tf_op jit(solution)/shard_map/all_to_all | solution.py:317
  81.5 1.8 %grad.3 = (f32[2,128,128]{2,1,0:T(8,128)S(1)}, f32[2,128,128]{2,1,0:T(8,128)S(1)}, f32[2,128,128]{2,1,0:T(8,128)S(1)}, f32[2,128,128]{2,1,0:T(8,128)S(1)}, f32[4...) custom-call(f32[4]{0:T(128)S(1)} %copy-done.6, f32[4,136,128]{2,1,0:T(8,128)S(1)} %all_to_all.25.pieces, ...), custom_call_target="tpu_custom_call" | custom-call | flops 33554432 | bytes 2986000 | tf_op jit(solution)/shard_map/grad/pallas_call | solution.py:265
  83.2 6.9 %all-to-all-start.3 = ((f32[4,128,128]{2,1,0:T(8,128)}), f32[4,128,128]{2,1,0:T(8,128)S(1)}, u32[]{:S(2)}, u32[]{:S(2)}) async-start(f32[4,128,128]{2,1,0:T(8,128)} %get-tuple-element.38), calls=%async_computation.3 | async-start | bytes 524288 | tf_op jit(solution)/shard_map/all_to_all | solution.py:322
  90.2 2.4 %collective-permute-start.5 = (f32[2,128,128]{2,1,0:T(8,128)S(1)}, f32[2,128,128]{2,1,0:T(8,128)S(1)}, u32[]{:S(2)}, u32[]{:S(2)}) collective-permute-start(f32[2,128,128]{2,1,0:T(8,128)S(1)} %get-tuple-element.34), channel_id=1, source_target_pairs={{0,8},{8,0},{16,24},{24,16},{32,40},{40,32},{48,56},{56,48},{64,72... | collective-permute-start | bytes 393224 | tf_op jit(solution)/shard_map/ppermute | solution.py:288
  92.6 3.2 %collective-permute-start.6 = (f32[2,128,128]{2,1,0:T(8,128)S(1)}, f32[2,128,128]{2,1,0:T(8,128)S(1)}, u32[]{:S(2)}, u32[]{:S(2)}) collective-permute-start(f32[2,128,128]{2,1,0:T(8,128)S(1)} %get-tuple-element.35), channel_id=1, source_target_pairs={{0,16},{8,24},{16,0},{24,8},{32,48},{40,56},{48,32},{56,40},{64,80... | collective-permute-start | bytes 393224 | tf_op jit(solution)/shard_map/ppermute | solution.py:288
  95.8 4.5 %collective-permute-start.7 = (f32[2,128,128]{2,1,0:T(8,128)S(1)}, f32[2,128,128]{2,1,0:T(8,128)S(1)}, u32[]{:S(2)}, u32[]{:S(2)}) collective-permute-start(f32[2,128,128]{2,1,0:T(8,128)S(1)} %get-tuple-element.36), channel_id=1, source_target_pairs={{0,24},{8,16},{16,8},{24,0},{32,56},{40,48},{48,40},{56,32},{64,88... | collective-permute-start | bytes 393224 | tf_op jit(solution)/shard_map/ppermute | solution.py:288
  100.3 9.2 %all-to-all-done.3.grads = f32[4,128,128]{2,1,0:T(8,128)S(1)} async-done(((f32[4,128,128]{2,1,0:T(8,128)}), f32[4,128,128]{2,1,0:T(8,128)S(1)}, u32[]{:S(2)}, u32[]{:S(2)}) %all-to-all-start.3) | async-done | bytes 262176 | tf_op jit(solution)/shard_map/all_to_all | solution.py:322
  109.5 0.6 back_row.1
  110.1 3.3 %collective-permute-start.9 = (f32[136,128]{1,0:T(8,128)S(1)}, f32[136,128]{1,0:T(8,128)S(1)}, u32[]{:S(2)}, u32[]{:S(2)}) collective-permute-start(f32[136,128]{1,0:T(8,128)S(1)} %back_row.1), channel_id=1, source_target_pairs={{256,0},{264,8},{272,16},{280,24},{288,32},{296,40},{304,48},{312,... | collective-permute-start | bytes 208904 | tf_op jit(solution)/shard_map/ppermute | solution.py:292
  113.4 1.8 %collective-permute-start.8 = (f32[136,128]{1,0:T(8,128)S(1)}, f32[136,128]{1,0:T(8,128)S(1)}, u32[]{:S(2)}, u32[]{:S(2)}) collective-permute-start(f32[136,128]{1,0:T(8,128)S(1)} %back_row.1), channel_id=1, source_target_pairs={{128,0},{136,8},{144,16},{152,24},{160,32},{168,40},{176,48},{184,... | collective-permute-start | bytes 208904 | tf_op jit(solution)/shard_map/ppermute | solution.py:292
  115.3 2.1 %back_intra.1 = (bf16[128,512]{1,0:T(8,128)(2,1)}, f32[128,512]{1,0:T(8,128)S(1)}, f32[128,512]{1,0:T(8,128)S(1)}) custom-call(f32[4]{0:T(128)S(1)} %copy-done.6, s32[1,128]{1,0:T(1,128)S(1)} %bitcast.4, bf16[128,512]{1,0:T(8,128)(2,1)S(1)} %copy-done.4, bf16[128,512]{1,0:T(8,128)(2,1)S(1)} %copy-done.1, bf16[128,512]{1,0:T(8,128)(2,1)S(1)} %copy-done.3, ...), custom_call_target="tpu_custom_call" | custom-call | flops 67108864 | bytes 1704464 | tf_op jit(solution)/shard_map/back_intra/pallas_call | solution.py:265
  117.4 0.6 back_state.1
  118.1 15.4 %all_to_all.27.states = f32[4,128,128]{2,1,0:T(8,128)S(1)} all-to-all(f32[4,128,128]{2,1,0:T(8,128)S(1)} %back_state.1), channel_id=1, replica_groups={{0,8,16,24},{32,40,48,56},{64,72,80,88},{96,104,112,120},{128,136,144,1..., dimensions={0} | all-to-all | bytes 524288 | tf_op jit(solution)/shard_map/all_to_all | solution.py:335
  133.5 1.5 %finish.1 = (bf16[128,512]{1,0:T(8,128)(2,1)}, bf16[128,512]{1,0:T(8,128)(2,1)}) custom-call(f32[4]{0:T(128)S(1)} %copy-done.6, s32[1,128]{1,0:T(1,128)S(1)} %bitcast.5, bf16[128,512]{1,0:T(8,128)(2,1)S(1)} %copy-done.1, bf16[128,512]{1,0:T(8,128)(2,1)S(1)} %copy-done.3, f32[128,512]{1,0:T(8,128)S(1)} %get-tuple-element.42.key_part, ...), custom_call_target="tpu_custom_call" | custom-call | flops 33554432 | bytes 1311248 | tf_op jit(solution)/shard_map/finish/pallas_call | solution.py:265
  (23 shorter events, 0.1 us)
Async XLA Ops:
  0.6 0.7 copy-start.6
  0.6 0.7 copy-start.7
  1.3 0.9 copy-start
  2.2 0.9 copy-start.2
  20.3 12.6 %copy-start.1 = (bf16[128,512]{1,0:T(8,128)(2,1)S(1)}, bf16[128,512]{1,0:T(8,128)(2,1)}, u32[]{:S(2)}) copy-start(bf16[128,512]{1,0:T(8,128)(2,1)} %key.7) | copy-start | bytes 393220
  20.3 12.6 %copy-start.3 = (bf16[128,512]{1,0:T(8,128)(2,1)S(1)}, bf16[128,512]{1,0:T(8,128)(2,1)}, u32[]{:S(2)}) copy-start(bf16[128,512]{1,0:T(8,128)(2,1)} %value.7) | copy-start | bytes 393220
  20.3 12.6 %copy-start.4 = (bf16[128,512]{1,0:T(8,128)(2,1)S(1)}, bf16[128,512]{1,0:T(8,128)(2,1)}, u32[]{:S(2)}) copy-start(bf16[128,512]{1,0:T(8,128)(2,1)} %query.3) | copy-start | bytes 393220
  20.3 12.6 %copy-start.5 = (bf16[128,512]{1,0:T(8,128)(2,1)S(1)}, bf16[128,512]{1,0:T(8,128)(2,1)}, u32[]{:S(2)}) copy-start(bf16[128,512]{1,0:T(8,128)(2,1)} %grad.2) | copy-start | bytes 393220
  20.3 12.6 %copy-start.8 = (f32[512]{0:T(512)S(1)}, f32[512]{0:T(512)}, u32[]{:S(2)}) copy-start(f32[512]{0:T(512)} %param.11) | copy-start | bytes 6148
  20.3 34.4 %all-to-all-start.1 = ((f32[4,136,128]{2,1,0:T(8,128)}), f32[4,136,128]{2,1,0:T(8,128)S(1)}, u32[]{:S(2)}, u32[]{:S(2)}) async-start(f32[4,136,128]{2,1,0:T(8,128)} %group_total.1), calls=%async_computation.1 | async-start | bytes 557056 | tf_op jit(solution)/shard_map/all_to_all | solution.py:304
  34.1 23.7 %collective-permute-start.1 = (f32[3,128,128]{2,1,0:T(8,128)S(1)}, f32[3,128,128]{2,1,0:T(8,128)S(1)}, u32[]{:S(2)}, u32[]{:S(2)}) collective-permute-start(f32[3,128,128]{2,1,0:T(8,128)S(1)} %get-tuple-element.27), channel_id=1, source_target_pairs={{0,8},{8,0},{16,24},{24,16},{32,40},{40,32},{48,56},{56,48},{64,72... | collective-permute-start | bytes 589832 | tf_op jit(solution)/shard_map/ppermute | solution.py:288
  36.6 23.1 %collective-permute-start.2 = (f32[3,128,128]{2,1,0:T(8,128)S(1)}, f32[3,128,128]{2,1,0:T(8,128)S(1)}, u32[]{:S(2)}, u32[]{:S(2)}) collective-permute-start(f32[3,128,128]{2,1,0:T(8,128)S(1)} %get-tuple-element.28), channel_id=1, source_target_pairs={{0,16},{8,24},{16,0},{24,8},{32,48},{40,56},{48,32},{56,40},{64,80... | collective-permute-start | bytes 589832 | tf_op jit(solution)/shard_map/ppermute | solution.py:288
  40.0 19.7 %collective-permute-start.3 = (f32[3,128,128]{2,1,0:T(8,128)S(1)}, f32[3,128,128]{2,1,0:T(8,128)S(1)}, u32[]{:S(2)}, u32[]{:S(2)}) collective-permute-start(f32[3,128,128]{2,1,0:T(8,128)S(1)} %get-tuple-element.29), channel_id=1, source_target_pairs={{0,24},{8,16},{16,8},{24,0},{32,56},{40,48},{48,40},{56,32},{64,88... | collective-permute-start | bytes 589832 | tf_op jit(solution)/shard_map/ppermute | solution.py:288
  55.3 7.7 %collective-permute-start.4 = (f32[136,128]{1,0:T(8,128)S(1)}, f32[136,128]{1,0:T(8,128)S(1)}, u32[]{:S(2)}, u32[]{:S(2)}) collective-permute-start(f32[136,128]{1,0:T(8,128)S(1)} %row_total.1), channel_id=1, source_target_pairs={{0,256},{8,264},{16,272},{24,280},{32,288},{40,296},{48,304},{56,3... | collective-permute-start | bytes 208904 | tf_op jit(solution)/shard_map/ppermute | solution.py:292
  56.6 6.4 %collective-permute-start = (f32[136,128]{1,0:T(8,128)S(1)}, f32[136,128]{1,0:T(8,128)S(1)}, u32[]{:S(2)}, u32[]{:S(2)}) collective-permute-start(f32[136,128]{1,0:T(8,128)S(1)} %row_total.1), channel_id=1, source_target_pairs={{0,128},{8,136},{16,144},{24,152},{32,160},{40,168},{48,176},{56,1... | collective-permute-start | bytes 208904 | tf_op jit(solution)/shard_map/ppermute | solution.py:292
  83.2 26.3 %all-to-all-start.3 = ((f32[4,128,128]{2,1,0:T(8,128)}), f32[4,128,128]{2,1,0:T(8,128)S(1)}, u32[]{:S(2)}, u32[]{:S(2)}) async-start(f32[4,128,128]{2,1,0:T(8,128)} %get-tuple-element.38), calls=%async_computation.3 | async-start | bytes 524288 | tf_op jit(solution)/shard_map/all_to_all | solution.py:322
  90.2 25.1 %collective-permute-start.5 = (f32[2,128,128]{2,1,0:T(8,128)S(1)}, f32[2,128,128]{2,1,0:T(8,128)S(1)}, u32[]{:S(2)}, u32[]{:S(2)}) collective-permute-start(f32[2,128,128]{2,1,0:T(8,128)S(1)} %get-tuple-element.34), channel_id=1, source_target_pairs={{0,8},{8,0},{16,24},{24,16},{32,40},{40,32},{48,56},{56,48},{64,72... | collective-permute-start | bytes 393224 | tf_op jit(solution)/shard_map/ppermute | solution.py:288
  92.6 22.7 %collective-permute-start.6 = (f32[2,128,128]{2,1,0:T(8,128)S(1)}, f32[2,128,128]{2,1,0:T(8,128)S(1)}, u32[]{:S(2)}, u32[]{:S(2)}) collective-permute-start(f32[2,128,128]{2,1,0:T(8,128)S(1)} %get-tuple-element.35), channel_id=1, source_target_pairs={{0,16},{8,24},{16,0},{24,8},{32,48},{40,56},{48,32},{56,40},{64,80... | collective-permute-start | bytes 393224 | tf_op jit(solution)/shard_map/ppermute | solution.py:288
  95.8 19.5 %collective-permute-start.7 = (f32[2,128,128]{2,1,0:T(8,128)S(1)}, f32[2,128,128]{2,1,0:T(8,128)S(1)}, u32[]{:S(2)}, u32[]{:S(2)}) collective-permute-start(f32[2,128,128]{2,1,0:T(8,128)S(1)} %get-tuple-element.36), channel_id=1, source_target_pairs={{0,24},{8,16},{16,8},{24,0},{32,56},{40,48},{48,40},{56,32},{64,88... | collective-permute-start | bytes 393224 | tf_op jit(solution)/shard_map/ppermute | solution.py:288
  110.1 7.3 %collective-permute-start.9 = (f32[136,128]{1,0:T(8,128)S(1)}, f32[136,128]{1,0:T(8,128)S(1)}, u32[]{:S(2)}, u32[]{:S(2)}) collective-permute-start(f32[136,128]{1,0:T(8,128)S(1)} %back_row.1), channel_id=1, source_target_pairs={{256,0},{264,8},{272,16},{280,24},{288,32},{296,40},{304,48},{312,... | collective-permute-start | bytes 208904 | tf_op jit(solution)/shard_map/ppermute | solution.py:292
  113.4 4.0 %collective-permute-start.8 = (f32[136,128]{1,0:T(8,128)S(1)}, f32[136,128]{1,0:T(8,128)S(1)}, u32[]{:S(2)}, u32[]{:S(2)}) collective-permute-start(f32[136,128]{1,0:T(8,128)S(1)} %back_row.1), channel_id=1, source_target_pairs={{128,0},{136,8},{144,16},{152,24},{160,32},{168,40},{176,48},{184,... | collective-permute-start | bytes 208904 | tf_op jit(solution)/shard_map/ppermute | solution.py:292

commit v3 on v1

v3 whole, which is shorter than its diff:
```python
import functools

import jax
import jax.numpy as jnp
from jax import lax
from jax.experimental import pallas as pl
from jax.experimental.pallas import tpu as pltpu
from jax.sharding import PartitionSpec as P

HEADS = 32
HEAD_DIM = 128
BLOCK = 128
LOCAL = 4
MEMBERS = 4
GROUPS = 4
ROWS = 4
OWNERS = ROWS * MEMBERS
PIECE = LOCAL * HEAD_DIM // OWNERS
PAD = 8
DOC = ROWS * PIECE
TALL = DOC + 8

epsilon = 1e-06
f32 = jnp.float32
bf16 = jnp.bfloat16

VMEM = pl.BlockSpec(memory_space=pltpu.VMEM)
SMEM = pl.BlockSpec(memory_space=pltpu.SMEM)


def dot(a, b, a_dim, b_dim):
    return lax.dot_general(a, b, (((a_dim,), (b_dim,)), ((), ())), preferred_element_type=f32)


def square(row):
    return jnp.broadcast_to(row, (BLOCK, BLOCK))


def iota(axis):
    return lax.broadcasted_iota(jnp.int32, (BLOCK, BLOCK), axis).astype(f32)


def head(h):
    return slice(h * HEAD_DIM, (h + 1) * HEAD_DIM)


def outflow_of(doc_col, doc_row, rate):
    last = doc_row[:, BLOCK - 1 :]
    return jnp.where(doc_col == last, jnp.exp(-rate * (BLOCK - 1.0 - iota(0))), 0.0)


def inflow_of(doc_col, doc_row, rate):
    return jnp.where(doc_col == doc_row[:, 0:1], jnp.exp(-rate * (iota(0) + 1.0)), 0.0)


def decays_of(doc_col, doc_row, rate):
    offset = iota(0) - iota(1)
    inside = (offset >= 0.0) & (doc_col == doc_row)
    return jnp.where(inside, jnp.exp(-rate * jnp.maximum(offset, 0.0)), 0.0)


def docs_of(docs):
    row = docs[...].astype(f32)
    return square(row).T, row


def put_pieces(out, h, matrix):
    each = OWNERS // LOCAL
    for i in range(each):
        out[h * each + i, 0:PIECE, :] = matrix[i * PIECE : (i + 1) * PIECE]


def get_pieces(pieces, h):
    each = OWNERS // LOCAL
    return jnp.concatenate([pieces[h * each + i] for i in range(each)], axis=0)


def local_state_kernel(rates, docs, key, value, out):
    doc_col, doc_row = docs_of(docs)
    for h in range(LOCAL):
        outflow = outflow_of(doc_col, doc_row, rates[h])
        key_out = (key[:, head(h)].astype(f32) * outflow).astype(bf16)
        put_pieces(out, h, dot(key_out, value[:, head(h)], 0, 0))
    for i in range(OWNERS):
        out[i, PIECE:, :] = jnp.broadcast_to(doc_row, (PAD, BLOCK))


def intra_kernel(rates, docs, query, key, value, weights, attended):
    doc_col, doc_row = docs_of(docs)
    for h in range(LOCAL):
        scores = dot(query[:, head(h)], key[:, head(h)], 1, 1)
        low = (scores * decays_of(doc_col, doc_row, rates[h])).astype(bf16)
        weights[h] = low
        attended[:, head(h)] = dot(low, value[:, head(h)], 1, 0)


def attend_kernel(rates, docs, gain, query, grad, intra, states, attended, sums):
    doc_col, doc_row = docs_of(docs)
    squares = jnp.zeros((BLOCK, BLOCK), f32)
    crosses = jnp.zeros((BLOCK, BLOCK), f32)
    for h in range(LOCAL):
        low = get_pieces(states, h).astype(bf16)
        inflow = inflow_of(doc_col, doc_row, rates[h])
        whole = intra[:, head(h)] + inflow * dot(query[:, head(h)], low, 1, 0)
        attended[:, head(h)] = whole
        squares = squares + whole * whole
        crosses = crosses + gain[:, head(h)] * grad[:, head(h)].astype(f32) * whole
    square_row = jnp.sum(squares.T, axis=0, keepdims=True)
    cross_row = jnp.sum(crosses.T, axis=0, keepdims=True)
    for i in range(sums.shape[0]):
        sums[i, 0:1, :] = square_row
        sums[i, 1:2, :] = cross_row


def grad_kernel(rates, docs, gain, query, grad, attended, sums, low_grad, out):
    doc_col, doc_row = docs_of(docs)
    both = jnp.sum(sums[...], axis=0)
    width = HEADS * HEAD_DIM
    inv_rms = lax.rsqrt(both[0:1] / width + epsilon)
    slope = both[1:2] * (inv_rms * inv_rms * inv_rms) / width
    inv_col, slope_col = square(inv_rms).T, square(slope).T
    for h in range(LOCAL):
        scaled = gain[:, head(h)] * grad[:, head(h)].astype(f32)
        low = (scaled * inv_col - attended[:, head(h)] * slope_col).astype(bf16)
        low_grad[:, head(h)] = low
        inflow = inflow_of(doc_col, doc_row, rates[h])
        query_in = (query[:, head(h)].astype(f32) * inflow).astype(bf16)
        put_pieces(out, h, dot(query_in, low, 0, 0))


def back_intra_kernel(
    rates, docs, query, key, value, weights, low_grad, states, query_grad, key_part, value_part
):
    doc_col, doc_row = docs_of(docs)
    for h in range(LOCAL):
        low = low_grad[:, head(h)]
        scores = dot(low, value[:, head(h)], 1, 1)
        grad_weights = (scores * decays_of(doc_col, doc_row, rates[h])).astype(bf16)
        state = get_pieces(states, h).astype(bf16)
        inflow = inflow_of(doc_col, doc_row, rates[h])
        whole = dot(grad_weights, key[:, head(h)], 1, 0) + inflow * dot(low, state, 1, 1)
        query_grad[:, head(h)] = whole.astype(bf16)
        key_part[:, head(h)] = dot(grad_weights, query[:, head(h)], 0, 0)
        value_part[:, head(h)] = dot(weights[h], low, 0, 0)


def finish_kernel(rates, docs, key, value, key_part, value_part, states, key_grad, value_grad):
    doc_col, doc_row = docs_of(docs)
    for h in range(LOCAL):
        low = get_pieces(states, h).astype(bf16)
        outflow = outflow_of(doc_col, doc_row, rates[h])
        more = outflow * dot(value[:, head(h)], low, 1, 1)
        key_grad[:, head(h)] = (key_part[:, head(h)] + more).astype(bf16)
        more = outflow * dot(key[:, head(h)], low, 1, 0)
        value_grad[:, head(h)] = (value_part[:, head(h)] + more).astype(bf16)


def place():
    mine = lax.axis_index("seq")
    return mine // (GROUPS * MEMBERS), (mine // MEMBERS) % GROUPS


def my_rate(rates):
    return rates[place()[0] * LOCAL // ROWS]


def faded(rate, blocks):
    return jnp.exp(jnp.full((1, BLOCK), -BLOCK * blocks, f32) * rate)


def passing(same, fade):
    return jnp.where(same, fade, 0.0)


def first_doc(pieces, x, i):
    row = pieces[x * MEMBERS + i, PIECE : PIECE + 1, 0:1]
    return jnp.broadcast_to(row, (1, BLOCK))


def last_doc(pieces, x, i):
    row = pieces[x * MEMBERS + i, PIECE : PIECE + 1, BLOCK - 1 :]
    return jnp.broadcast_to(row, (1, BLOCK))


def state_of(total, x):
    return total[x * PIECE : (x + 1) * PIECE, :]


def doc_of(total, x):
    return total[DOC + x : DOC + x + 1, :]


def group_total_kernel(rates, pieces, out):
    fade = faded(my_rate(rates), 1.0)
    out[DOC:, :] = jnp.zeros((TALL - DOC, BLOCK), f32)
    for x in range(ROWS):
        total = pieces[x * MEMBERS, 0:PIECE, :]
        for i in range(1, MEMBERS):
            same = last_doc(pieces, x, i) == last_doc(pieces, x, i - 1)
            total = passing(same, fade) * total + pieces[x * MEMBERS + i, 0:PIECE, :]
        out[x * PIECE : (x + 1) * PIECE, :] = total
        out[DOC + x : DOC + x + 1, :] = last_doc(pieces, x, MEMBERS - 1)


def pair_total_kernel(rates, mine, theirs, out):
    first = place()[1] % 2 == 0
    fade = faded(my_rate(rates), 1.0 * MEMBERS)
    out[DOC:, :] = jnp.where(first, theirs[DOC:, :], mine[DOC:, :])
    for x in range(ROWS):
        same = doc_of(mine, x) == doc_of(theirs, x)
        low = jnp.where(first, state_of(mine, x), state_of(theirs, x))
        high = jnp.where(first, state_of(theirs, x), state_of(mine, x))
        out[x * PIECE : (x + 1) * PIECE, :] = passing(same, fade) * low + high


def row_docs(mine, theirs, group, x):
    low = jnp.where(group < 2, doc_of(mine, x), doc_of(theirs, x))
    high = jnp.where(group < 2, doc_of(theirs, x), doc_of(mine, x))
    return low, high


def before_group(partner, mine, theirs, group, x):
    low, _ = row_docs(mine, theirs, group, x)
    before = row_docs(mine, theirs, group, x - 1)[1] if x else -jnp.ones((1, BLOCK), f32)
    pair = jnp.where(group > 1, low, before)
    return before, pair, jnp.where(group % 2 == 1, doc_of(partner, x), pair)


def states_kernel(rates, pieces, partner, mine, theirs, out):
    group, rate = place()[1], my_rate(rates)
    one, four = faded(rate, 1.0), faded(rate, 1.0 * MEMBERS)
    eight = faded(rate, 2.0 * MEMBERS)
    carry = jnp.zeros((PIECE, BLOCK), f32)
    for x in range(ROWS):
        before, pair_doc, prev = before_group(partner, mine, theirs, group, x)
        low_doc, high_doc = row_docs(mine, theirs, group, x)
        low = jnp.where(group < 2, state_of(mine, x), state_of(theirs, x))
        high = jnp.where(group < 2, state_of(theirs, x), state_of(mine, x))
        half = passing(low_doc == before, eight) * carry + low
        state = jnp.where(group > 1, half, carry)
        longer = passing(doc_of(partner, x) == pair_doc, four) * state + state_of(partner, x)
        state = jnp.where(group % 2 == 1, longer, state)
        carry = passing(high_doc == low_doc, eight) * half + high
        for i in range(MEMBERS):
            out[x * MEMBERS + i] = passing(first_doc(pieces, x, i) == prev, 1.0) * state
            last = last_doc(pieces, x, i)
            if i < MEMBERS - 1:
                state = passing(last == prev, one) * state + pieces[x * MEMBERS + i, 0:PIECE, :]
            prev = last


def back_total_kernel(rates, pieces, partner, mine, theirs, grads, out):
    group, fade = place()[1], faded(my_rate(rates), 1.0)
    for x in range(ROWS):
        _, _, prev = before_group(partner, mine, theirs, group, x)
        total = jnp.zeros((PIECE, BLOCK), f32)
        for i in range(MEMBERS - 1, -1, -1):
            older = last_doc(pieces, x, i - 1) if i else prev
            local = passing(first_doc(pieces, x, i) == older, 1.0) * grads[x * MEMBERS + i]
            total = passing(last_doc(pieces, x, i) == older, fade) * total + local
        out[x * PIECE : (x + 1) * PIECE, :] = total


def back_pair_kernel(rates, total, partner, mine, theirs, grad, grad_theirs, out):
    group, fade = place()[1], faded(my_rate(rates), 1.0 * MEMBERS)
    first = group % 2 == 0
    for x in range(ROWS):
        _, before, _ = before_group(partner, mine, theirs, group, x)
        low_doc = jnp.where(first, doc_of(total, x), doc_of(partner, x))
        low = jnp.where(first, state_of(grad, x), state_of(grad_theirs, x))
        high = jnp.where(first, state_of(grad_theirs, x), state_of(grad, x))
        out[x * PIECE : (x + 1) * PIECE, :] = low + passing(low_doc == before, fade) * high


def back_states_kernel(
    rates, pieces, total, partner, mine, theirs, grads, partner_grad, pair_grad, other_grad, out
):
    group, rate = place()[1], my_rate(rates)
    one, four = faded(rate, 1.0), faded(rate, 1.0 * MEMBERS)
    eight = faded(rate, 2.0 * MEMBERS)
    carry = jnp.zeros((PIECE, BLOCK), f32)
    for x in range(ROWS - 1, -1, -1):
        before, _, _ = before_group(partner, mine, theirs, group, x)
        low_doc, high_doc = row_docs(mine, theirs, group, x)
        low = jnp.where(group < 2, state_of(pair_grad, x), state_of(other_grad, x))
        high = jnp.where(group < 2, state_of(other_grad, x), state_of(pair_grad, x))
        half = high + passing(high_doc == low_doc, eight) * carry
        state = jnp.where(group < 2, half, carry)
        same = doc_of(total, x) == doc_of(partner, x)
        longer = state_of(partner_grad, x) + passing(same, four) * state
        state = jnp.where(group % 2 == 0, longer, state)
        carry = low + passing(low_doc == before, eight) * half
        for i in range(MEMBERS - 1, -1, -1):
            out[x * MEMBERS + i] = state
            if i:
                last, older = last_doc(pieces, x, i), last_doc(pieces, x, i - 1)
                local = passing(first_doc(pieces, x, i) == older, 1.0) * grads[x * MEMBERS + i]
                state = passing(last == older, one) * state + local


def call(kernel, name, outs, *args, flops=1):
    shapes = [jax.ShapeDtypeStruct(shape, dtype) for shape, dtype in outs]
    moved = sum(a.size * a.dtype.itemsize for a in (*args, *shapes))
    out = pl.pallas_call(
        kernel,
        out_shape=shapes,
        in_specs=[SMEM] + [VMEM] * (len(args) - 1),
        out_specs=[VMEM] * len(shapes),
        name=name,
        compiler_params=pltpu.CompilerParams(vmem_limit_bytes=32 * 1024 * 1024),
        cost_estimate=pl.CostEstimate(flops=flops, bytes_accessed=moved, transcendentals=0),
    )(*args)
    return out[0] if len(out) == 1 else out


def per_device(query, key, value, grad, gain, rates, doc_ids):
    row_len = GROUPS * MEMBERS
    blocks = range(ROWS * row_len)
    owners = [
        [x * row_len + k * MEMBERS + i for x in range(ROWS) for i in range(MEMBERS)] for k in range(GROUPS)
    ]
    swap = functools.partial(
        lax.all_to_all, axis_name="seq", split_axis=0, concat_axis=0, axis_index_groups=owners, tiled=True
    )

    def other_group(total, d):
        return lax.ppermute(total, "seq", [(i, i ^ (d * MEMBERS)) for i in blocks])

    docs = doc_ids.reshape(1, BLOCK)
    gain = gain.reshape(1, LOCAL * HEAD_DIM)
    wide = (BLOCK, LOCAL * HEAD_DIM)
    cut = (OWNERS, PIECE, HEAD_DIM)
    one = 2 * LOCAL * BLOCK * BLOCK * HEAD_DIM

    local = call(
        local_state_kernel, "local_state", [((OWNERS, PIECE + PAD, HEAD_DIM), f32)],
        rates, docs, key, value, flops=one,
    )
    pieces = swap(local)
    total = call(group_total_kernel, "group_total", [((TALL, HEAD_DIM), f32)], rates, pieces)
    partner = other_group(total, 1)
    weights, intra = call(
        intra_kernel, "intra", [((LOCAL, BLOCK, BLOCK), bf16), (wide, f32)],
        rates, docs, query, key, value, flops=2 * one,
    )
    pair = call(pair_total_kernel, "pair_total", [((TALL, HEAD_DIM), f32)], rates, total, partner)
    other = other_group(pair, 3)
    states = swap(call(states_kernel, "states", [(cut, f32)], rates, pieces, partner, pair, other))
    attended, sums = call(
        attend_kernel, "attend", [(wide, f32), ((8, 2, BLOCK), f32)],
        rates, docs, gain, query, grad, intra, states, flops=one,
    )
    sums = lax.all_to_all(sums, "head", 0, 0, tiled=True)
    low_grad, local_grad = call(
        grad_kernel, "grad", [(wide, bf16), (cut, f32)],
        rates, docs, gain, query, grad, attended, sums, flops=one,
    )
    grads = swap(local_grad)
    total_grad = call(
        back_total_kernel, "back_total", [((DOC, HEAD_DIM), f32)], rates, pieces, partner, pair, other, grads
    )
    partner_grad = other_group(total_grad, 1)
    query_grad, key_part, value_part = call(
        back_intra_kernel, "back_intra", [(wide, bf16), (wide, f32), (wide, f32)],
        rates, docs, query, key, value, weights, low_grad, states, flops=5 * one,
    )
    pair_grad = call(
        back_pair_kernel, "back_pair", [((DOC, HEAD_DIM), f32)],
        rates, total, partner, pair, other, total_grad, partner_grad,
    )
    other_grad = other_group(pair_grad, 3)
    states_out = call(
        back_states_kernel, "back_states", [(cut, f32)],
        rates, pieces, total, partner, pair, other, grads, partner_grad, pair_grad, other_grad,
    )
    states_out = swap(states_out)
    key_grad, value_grad = call(
        finish_kernel, "finish", [(wide, bf16), (wide, bf16)],
        rates, docs, key, value, key_part, value_part, states_out, flops=2 * one,
    )
    return query_grad, key_grad, value_grad


def solution(mesh):
    return jax.shard_map(
        per_device,
        mesh=mesh,
        in_specs=(
            P("seq", "head"),
            P("seq", "head"),
            P("seq", "head"),
            P("seq", "head"),
            P("head"),
            P("head"),
            P("seq"),
        ),
        out_specs=(P("seq", "head"), P("seq", "head"), P("seq", "head")),
        check_vma=False,
    )
```

time: 148 us -> 132 us (0.89)
  blocking collectives: 85.6 us -> 42 us
  starting transfers between devices: 12.1 us -> 37.6 us
  waiting for transfers between devices: 33.6 us -> 35.3 us
    all_to_all x4 -> x2, blocking collectives: 76 us -> 32.4 us  [the longest x1 18.7 us: per_device(): pieces = swap(local)]
    ppermute x0 -> x4, starting transfers between devices: none -> 23.6 us  [other_group(): return lax.ppermute(total, 'seq', [(i, i ^ d * MEMBERS) for i in blocks])]
    ppermute x0 -> x4, waiting for transfers between devices: none -> 22.4 us  [other_group(): return lax.ppermute(total, 'seq', [(i, i ^ d * MEMBERS) for i in blocks])]
    all_to_all x2, waiting for transfers between devices: 33.6 us -> 13 us  [the longest x1 7.45 us: per_device(): swap(call(states_kernel, 'states', [(cut, f32)], rates, pieces, partner,...]
    all_to_all x2, starting transfers between devices: 12.1 us -> 14 us  [the longest x1 8.44 us: per_device(): swap(call(states_kernel, 'states', [(cut, f32)], rates, pieces, partner,...]
    pallas_call x10 -> x12, Pallas kernels: 11.3 us -> 12.6 us  [call(): pl.pallas_call(kernel, out_shape=shapes, in_specs=[SMEM] + [VMEM] * (len(...]
  transfers between devices with their start and end apart: 2 -> 6, of which waited for: 2 -> 6; matrix products, arithmetic and copies ran while one was open for 0% -> 0% of each run, Pallas kernels for 2% -> 3%
where the time goes in v3:
time: 132 us; the launch traced here: 131 us
  blocking collectives  42 us (32%)
  starting transfers between devices  37.6 us (28%)
  waiting for transfers between devices  35.3 us (27%)
  Pallas kernels  12.6 us (10%)
  local copies, waits for them, and re-layouts  2.49 us (2%)
    ppermute x4, starting transfers between devices, other_group(): return lax.ppermute(total, 'seq', [(i, i ^ d * MEMBERS) for i in blocks])  23.6 us
    ppermute x4, waiting for transfers between devices, other_group(): return lax.ppermute(total, 'seq', [(i, i ^ d * MEMBERS) for i in blocks])  22.4 us
    all_to_all x1, blocking collectives, per_device(): pieces = swap(local)  18.7 us
    all_to_all x1, blocking collectives, per_device(): grads = swap(local_grad)  13.8 us
    pallas_call x12, Pallas kernels, call(): pl.pallas_call(kernel, out_shape=shapes, in_specs=[SMEM] + [VMEM] * (len(...  12.6 us
    all_to_all x1, blocking collectives, per_device(): sums = lax.all_to_all(sums, 'head', 0, 0, tiled=True)  9.58 us
    all_to_all x1, starting transfers between devices, per_device(): swap(call(states_kernel, 'states', [(cut, f32)], rates, pieces, partner,...  8.44 us
    all_to_all x1, waiting for transfers between devices, per_device(): swap(call(states_kernel, 'states', [(cut, f32)], rates, pieces, partner,...  7.45 us
  transfers between devices with their start and end apart: 6, of which 6 were waited for; matrix products, arithmetic and copies ran while one was open for 0% of the time, Pallas kernels for 3%

profile of v3, /device:TPU:6, one launch (start us, length us, event | category | flops | bytes accessed | tf_op | source)
XLA Modules:
  0.0 130.8 jit_solution(6373503652897150086)
XLA Ops:
  0.7 0.6 copy-done.6
  1.3 0.0 copy-done.7
  1.3 0.9 copy-done
  2.2 0.9 copy-done.2
  3.1 0.9 local_state.1
  4.0 18.7 %all_to_all.25.pieces = f32[16,40,128]{2,1,0:T(8,128)S(1)} all-to-all(f32[16,40,128]{2,1,0:T(8,128)S(1)} %local_state.1), channel_id=1, replica_groups={{0,8,16,24,128,136,144,152,256,264,272,280,384,392,400,408},{32,40,48,5..., dimensions={0} | all-to-all | bytes 655360 | tf_op jit(solution)/shard_map/all_to_all | solution.py:339
  22.6 0.6 group_total.1.mine.total
  23.3 9.1 %collective-permute-start = (f32[136,128]{1,0:T(8,128)S(1)}, f32[136,128]{1,0:T(8,128)S(1)}, u32[]{:S(2)}, u32[]{:S(2)}) collective-permute-start(f32[136,128]{1,0:T(8,128)S(1)} %group_total.1.mine.total), channel_id=1, source_target_pairs={{0,32},{8,40},{16,48},{24,56},{32,0},{40,8},{48,16},{56,24},{64,96... | collective-permute-start | bytes 208904 | tf_op jit(solution)/shard_map/ppermute | solution.py:327
  32.4 4.6 %collective-permute-done.theirs.partner = f32[136,128]{1,0:T(8,128)S(1)} collective-permute-done((f32[136,128]{1,0:T(8,128)S(1)}, f32[136,128]{1,0:T(8,128)S(1)}, u32[]{:S(2)}, u32[]{:S(2)}) %collective-permute-start) | collective-permute-done | bytes 69664 | tf_op jit(solution)/shard_map/ppermute | solution.py:327
  37.0 0.6 pair_total.1.mine
  37.6 6.4 %collective-permute-start.1 = (f32[136,128]{1,0:T(8,128)S(1)}, f32[136,128]{1,0:T(8,128)S(1)}, u32[]{:S(2)}, u32[]{:S(2)}) collective-permute-start(f32[136,128]{1,0:T(8,128)S(1)} %pair_total.1.mine), channel_id=1, source_target_pairs={{0,96},{8,104},{16,112},{24,120},{32,64},{40,72},{48,80},{56,88},{... | collective-permute-start | bytes 208904 | tf_op jit(solution)/shard_map/ppermute | solution.py:327
  44.0 3.7 %collective-permute-done.1.theirs = f32[136,128]{1,0:T(8,128)S(1)} collective-permute-done((f32[136,128]{1,0:T(8,128)S(1)}, f32[136,128]{1,0:T(8,128)S(1)}, u32[]{:S(2)}, u32[]{:S(2)}) %collective-permute-start.1) | collective-permute-done | bytes 69664 | tf_op jit(solution)/shard_map/ppermute | solution.py:327
  47.7 1.3 %states.1 = f32[16,32,128]{2,1,0:T(8,128)} custom-call(f32[4]{0:T(128)S(1)} %copy-done.6, f32[16,40,128]{2,1,0:T(8,128)S(1)} %all_to_all.25.pieces, f32[136,128]{1,0:T(8,128)S(1)} %collective-permute-done.theirs.partner, f32[136,128]{1,0:T(8,128)S(1)} %pair_total.1.mine, f32[136,128]{1,0:T(8,128)S(1)} %collective-permute-done.1.theirs), custom_call_target="tpu_custom_call" | custom-call | flops 1 | bytes 798736 | tf_op jit(solution)/shard_map/states/pallas_call | solution.py:304
  49.0 8.4 %all-to-all-start.1 = ((f32[16,32,128]{2,1,0:T(8,128)}), f32[16,32,128]{2,1,0:T(8,128)S(1)}, u32[]{:S(2)}, u32[]{:S(2)}) async-start(f32[16,32,128]{2,1,0:T(8,128)} %states.1), calls=%async_computation.1 | async-start | bytes 524288 | tf_op jit(solution)/shard_map/all_to_all | solution.py:348
  57.5 1.3 intra.1
  58.8 0.0 copy-start.8
  58.8 7.4 %all-to-all-done.1.states = f32[16,32,128]{2,1,0:T(8,128)S(1)} async-done(((f32[16,32,128]{2,1,0:T(8,128)}), f32[16,32,128]{2,1,0:T(8,128)S(1)}, u32[]{:S(2)}, u32[]{:S(2)}) %all-to-all-start.1) | async-done | bytes 262176 | tf_op jit(solution)/shard_map/all_to_all | solution.py:348
  66.3 0.8 attend.1
  67.1 9.6 %all_to_all.26.sums = f32[8,2,128]{2,1,0:T(2,128)S(1)} all-to-all(f32[8,2,128]{2,1,0:T(2,128)S(1)} %get-tuple-element.17), channel_id=1, replica_groups=mesh['seq'=64,'head'=8] {'head'}, dimensions={0} | all-to-all | bytes 16384 | tf_op jit(solution)/shard_map/all_to_all | solution.py:353
  76.7 0.9 grad.4
  77.6 13.8 %all_to_all.27.grads = f32[16,32,128]{2,1,0:T(8,128)S(1)} all-to-all(f32[16,32,128]{2,1,0:T(8,128)S(1)} %get-tuple-element.22), channel_id=1, replica_groups={{0,8,16,24,128,136,144,152,256,264,272,280,384,392,400,408},{32,40,48,5..., dimensions={0} | all-to-all | bytes 524288 | tf_op jit(solution)/shard_map/all_to_all | solution.py:358
  91.4 0.7 back_total.1.grad
  92.0 5.0 %collective-permute-start.2 = (f32[128,128]{1,0:T(8,128)S(1)}, f32[128,128]{1,0:T(8,128)S(1)}, u32[]{:S(2)}, u32[]{:S(2)}) collective-permute-start(f32[128,128]{1,0:T(8,128)S(1)} %back_total.1.grad), channel_id=1, source_target_pairs={{0,32},{8,40},{16,48},{24,56},{32,0},{40,8},{48,16},{56,24},{64,96... | collective-permute-start | bytes 196616 | tf_op jit(solution)/shard_map/ppermute | solution.py:327
  97.1 7.0 %collective-permute-done.2.grad_theirs.partner_grad = f32[128,128]{1,0:T(8,128)S(1)} collective-permute-done((f32[128,128]{1,0:T(8,128)S(1)}, f32[128,128]{1,0:T(8,128)S(1)}, u32[]{:S(2)}, u32[]{:S(2)}) %collective-permute-start.2) | collective-permute-done | bytes 65568 | tf_op jit(solution)/shard_map/ppermute | solution.py:327
  104.1 0.6 back_pair.1.pair_grad
  104.7 3.0 %collective-permute-start.3 = (f32[128,128]{1,0:T(8,128)S(1)}, f32[128,128]{1,0:T(8,128)S(1)}, u32[]{:S(2)}, u32[]{:S(2)}) collective-permute-start(f32[128,128]{1,0:T(8,128)S(1)} %back_pair.1.pair_grad), channel_id=1, source_target_pairs={{0,96},{8,104},{16,112},{24,120},{32,64},{40,72},{48,80},{56,88},{... | collective-permute-start | bytes 196616 | tf_op jit(solution)/shard_map/ppermute | solution.py:327
  107.7 7.1 %collective-permute-done.3.other_grad = f32[128,128]{1,0:T(8,128)S(1)} collective-permute-done((f32[128,128]{1,0:T(8,128)S(1)}, f32[128,128]{1,0:T(8,128)S(1)}, u32[]{:S(2)}, u32[]{:S(2)}) %collective-permute-start.3) | collective-permute-done | bytes 65568 | tf_op jit(solution)/shard_map/ppermute | solution.py:327
  114.8 1.4 %back_states.1 = f32[16,32,128]{2,1,0:T(8,128)} custom-call(f32[4]{0:T(128)S(1)} %copy-done.6, f32[16,40,128]{2,1,0:T(8,128)S(1)} %all_to_all.25.pieces, f32[136,128]{1,0:T(8,128)S(1)} %group_total.1.mine.total, f32[136,128]{1,0:T(8,128)S(1)} %collective-permute-done.theirs.partner, f32[136,128]{1,0:T(8,128)S(1)} %pair_total.1.mine, ...), custom_call_target="tpu_custom_call" | custom-call | flops 1 | bytes 1327120 | tf_op jit(solution)/shard_map/back_states/pallas_call | solution.py:304
  116.1 5.5 %all-to-all-start.4 = ((f32[16,32,128]{2,1,0:T(8,128)}), f32[16,32,128]{2,1,0:T(8,128)S(1)}, u32[]{:S(2)}, u32[]{:S(2)}) async-start(f32[16,32,128]{2,1,0:T(8,128)} %back_states.1), calls=%async_computation.4 | async-start | bytes 524288 | tf_op jit(solution)/shard_map/all_to_all | solution.py:376
  121.6 2.1 %back_intra.1 = (bf16[128,512]{1,0:T(8,128)(2,1)}, f32[128,512]{1,0:T(8,128)S(1)}, f32[128,512]{1,0:T(8,128)S(1)}) custom-call(f32[4]{0:T(128)S(1)} %copy-done.6, s32[1,128]{1,0:T(1,128)S(1)} %bitcast.6, bf16[128,512]{1,0:T(8,128)(2,1)S(1)} %copy-done.4, bf16[128,512]{1,0:T(8,128)(2,1)S(1)} %copy-done.1, bf16[128,512]{1,0:T(8,128)(2,1)S(1)} %copy-done.3, ...), custom_call_target="tpu_custom_call" | custom-call | flops 83886080 | bytes 1573392 | tf_op jit(solution)/shard_map/back_intra/pallas_call | solution.py:304
  123.8 5.5 %all-to-all-done.4.states = f32[16,32,128]{2,1,0:T(8,128)S(1)} async-done(((f32[16,32,128]{2,1,0:T(8,128)}), f32[16,32,128]{2,1,0:T(8,128)S(1)}, u32[]{:S(2)}, u32[]{:S(2)}) %all-to-all-start.4) | async-done | bytes 262176 | tf_op jit(solution)/shard_map/all_to_all | solution.py:376
  129.3 1.5 %finish.1 = (bf16[128,512]{1,0:T(8,128)(2,1)}, bf16[128,512]{1,0:T(8,128)(2,1)}) custom-call(f32[4]{0:T(128)S(1)} %copy-done.6, s32[1,128]{1,0:T(1,128)S(1)} %bitcast.7, bf16[128,512]{1,0:T(8,128)(2,1)S(1)} %copy-done.1, bf16[128,512]{1,0:T(8,128)(2,1)S(1)} %copy-done.3, f32[128,512]{1,0:T(8,128)S(1)} %get-tuple-element.20.key_part, ...), custom_call_target="tpu_custom_call" | custom-call | flops 33554432 | bytes 1311248 | tf_op jit(solution)/shard_map/finish/pallas_call | solution.py:304
  (13 shorter events, 0.0 us)
Async XLA Ops:
  0.6 0.7 copy-start.6
  0.6 0.7 copy-start.7
  1.3 0.9 copy-start
  2.2 0.9 copy-start.2
  23.3 13.7 %collective-permute-start = (f32[136,128]{1,0:T(8,128)S(1)}, f32[136,128]{1,0:T(8,128)S(1)}, u32[]{:S(2)}, u32[]{:S(2)}) collective-permute-start(f32[136,128]{1,0:T(8,128)S(1)} %group_total.1.mine.total), channel_id=1, source_target_pairs={{0,32},{8,40},{16,48},{24,56},{32,0},{40,8},{48,16},{56,24},{64,96... | collective-permute-start | bytes 208904 | tf_op jit(solution)/shard_map/ppermute | solution.py:327
  37.6 10.1 %collective-permute-start.1 = (f32[136,128]{1,0:T(8,128)S(1)}, f32[136,128]{1,0:T(8,128)S(1)}, u32[]{:S(2)}, u32[]{:S(2)}) collective-permute-start(f32[136,128]{1,0:T(8,128)S(1)} %pair_total.1.mine), channel_id=1, source_target_pairs={{0,96},{8,104},{16,112},{24,120},{32,64},{40,72},{48,80},{56,88},{... | collective-permute-start | bytes 208904 | tf_op jit(solution)/shard_map/ppermute | solution.py:327
  49.0 8.5 %copy-start.1 = (bf16[128,512]{1,0:T(8,128)(2,1)S(1)}, bf16[128,512]{1,0:T(8,128)(2,1)}, u32[]{:S(2)}) copy-start(bf16[128,512]{1,0:T(8,128)(2,1)} %key.7) | copy-start | bytes 393220
  49.0 8.5 %copy-start.3 = (bf16[128,512]{1,0:T(8,128)(2,1)S(1)}, bf16[128,512]{1,0:T(8,128)(2,1)}, u32[]{:S(2)}) copy-start(bf16[128,512]{1,0:T(8,128)(2,1)} %value.7) | copy-start | bytes 393220
  49.0 8.5 %copy-start.4 = (bf16[128,512]{1,0:T(8,128)(2,1)S(1)}, bf16[128,512]{1,0:T(8,128)(2,1)}, u32[]{:S(2)}) copy-start(bf16[128,512]{1,0:T(8,128)(2,1)} %query.7) | copy-start | bytes 393220
  49.0 17.2 %all-to-all-start.1 = ((f32[16,32,128]{2,1,0:T(8,128)}), f32[16,32,128]{2,1,0:T(8,128)S(1)}, u32[]{:S(2)}, u32[]{:S(2)}) async-start(f32[16,32,128]{2,1,0:T(8,128)} %states.1), calls=%async_computation.1 | async-start | bytes 524288 | tf_op jit(solution)/shard_map/all_to_all | solution.py:348
  57.5 8.8 %copy-start.5 = (bf16[128,512]{1,0:T(8,128)(2,1)S(1)}, bf16[128,512]{1,0:T(8,128)(2,1)}, u32[]{:S(2)}) copy-start(bf16[128,512]{1,0:T(8,128)(2,1)} %grad.5) | copy-start | bytes 393220
  58.8 7.5 %copy-start.8 = (f32[512]{0:T(512)S(1)}, f32[512]{0:T(512)}, u32[]{:S(2)}) copy-start(f32[512]{0:T(512)} %param.11) | copy-start | bytes 6148
  92.0 12.1 %collective-permute-start.2 = (f32[128,128]{1,0:T(8,128)S(1)}, f32[128,128]{1,0:T(8,128)S(1)}, u32[]{:S(2)}, u32[]{:S(2)}) collective-permute-start(f32[128,128]{1,0:T(8,128)S(1)} %back_total.1.grad), channel_id=1, source_target_pairs={{0,32},{8,40},{16,48},{24,56},{32,0},{40,8},{48,16},{56,24},{64,96... | collective-permute-start | bytes 196616 | tf_op jit(solution)/shard_map/ppermute | solution.py:327
  104.7 10.1 %collective-permute-start.3 = (f32[128,128]{1,0:T(8,128)S(1)}, f32[128,128]{1,0:T(8,128)S(1)}, u32[]{:S(2)}, u32[]{:S(2)}) collective-permute-start(f32[128,128]{1,0:T(8,128)S(1)} %back_pair.1.pair_grad), channel_id=1, source_target_pairs={{0,96},{8,104},{16,112},{24,120},{32,64},{40,72},{48,80},{56,88},{... | collective-permute-start | bytes 196616 | tf_op jit(solution)/shard_map/ppermute | solution.py:327
  116.1 13.1 %all-to-all-start.4 = ((f32[16,32,128]{2,1,0:T(8,128)}), f32[16,32,128]{2,1,0:T(8,128)S(1)}, u32[]{:S(2)}, u32[]{:S(2)}) async-start(f32[16,32,128]{2,1,0:T(8,128)} %back_states.1), calls=%async_computation.4 | async-start | bytes 524288 | tf_op jit(solution)/shard_map/all_to_all | solution.py:376

commit v4 on v3

--- a/solution.py
+++ b/solution.py
@@ -75,7 +75,15 @@
     return jnp.concatenate([pieces[h * each + i] for i in range(each)], axis=0)
 
 
-def local_state_kernel(rates, docs, key, value, out):
+def local_state_kernel(
+    rates_in, docs_in, key_in, value_in, out, fades, rates, docs, key, value, sems
+):
+    pairs = ((rates_in, rates), (docs_in, docs), (key_in, key), (value_in, value))
+    copies = [pltpu.make_async_copy(a, b, sems.at[i]) for i, (a, b) in enumerate(pairs)]
+    for copy in copies:
+        copy.start()
+    for copy in copies:
+        copy.wait()
     doc_col, doc_row = docs_of(docs)
     for h in range(LOCAL):
         outflow = outflow_of(doc_col, doc_row, rates[h])
@@ -83,28 +91,36 @@
         put_pieces(out, h, dot(key_out, value[:, head(h)], 0, 0))
     for i in range(OWNERS):
         out[i, PIECE:, :] = jnp.broadcast_to(doc_row, (PAD, BLOCK))
-
-
-def intra_kernel(rates, docs, query, key, value, weights, attended):
+    mine = rates[place()[0] * LOCAL // ROWS]
+    for i, blocks in enumerate((1, MEMBERS, 2 * MEMBERS)):
+        fades[i : i + 1, :] = jnp.exp(jnp.full((1, BLOCK), -1.0 * BLOCK * blocks, f32) * mine)
+
+
+def intra_kernel(
+    rates, docs, gain, query, key, value, grad, weights, attended, scaled, query_in, inflows, outflows
+):
     doc_col, doc_row = docs_of(docs)
+    scaled[...] = gain[...] * grad[...].astype(f32)
     for h in range(LOCAL):
         scores = dot(query[:, head(h)], key[:, head(h)], 1, 1)
         low = (scores * decays_of(doc_col, doc_row, rates[h])).astype(bf16)
         weights[h] = low
         attended[:, head(h)] = dot(low, value[:, head(h)], 1, 0)
-
-
-def attend_kernel(rates, docs, gain, query, grad, intra, states, attended, sums):
-    doc_col, doc_row = docs_of(docs)
+        inflow = inflow_of(doc_col, doc_row, rates[h])
+        inflows[h] = inflow
+        query_in[:, head(h)] = (query[:, head(h)].astype(f32) * inflow).astype(bf16)
+        outflows[h] = outflow_of(doc_col, doc_row, rates[h])
+
+
+def attend_kernel(inflow, query, scaled, intra, states, attended, sums):
     squares = jnp.zeros((BLOCK, BLOCK), f32)
     crosses = jnp.zeros((BLOCK, BLOCK), f32)
     for h in range(LOCAL):
         low = get_pieces(states, h).astype(bf16)
-        inflow = inflow_of(doc_col, doc_row, rates[h])
-        whole = intra[:, head(h)] + inflow * dot(query[:, head(h)], low, 1, 0)
+        whole = intra[:, head(h)] + inflow[h] * dot(query[:, head(h)], low, 1, 0)
         attended[:, head(h)] = whole
         squares = squares + whole * whole
-        crosses = crosses + gain[:, head(h)] * grad[:, head(h)].astype(f32) * whole
+        crosses = crosses + scaled[:, head(h)] * whole
     square_row = jnp.sum(squares.T, axis=0, keepdims=True)
     cross_row = jnp.sum(crosses.T, axis=0, keepdims=True)
     for i in range(sums.shape[0]):
@@ -112,24 +128,20 @@
         sums[i, 1:2, :] = cross_row
 
 
-def grad_kernel(rates, docs, gain, query, grad, attended, sums, low_grad, out):
-    doc_col, doc_row = docs_of(docs)
+def grad_kernel(query_in, scaled, attended, sums, low_grad, out):
     both = jnp.sum(sums[...], axis=0)
     width = HEADS * HEAD_DIM
     inv_rms = lax.rsqrt(both[0:1] / width + epsilon)
     slope = both[1:2] * (inv_rms * inv_rms * inv_rms) / width
     inv_col, slope_col = square(inv_rms).T, square(slope).T
     for h in range(LOCAL):
-        scaled = gain[:, head(h)] * grad[:, head(h)].astype(f32)
-        low = (scaled * inv_col - attended[:, head(h)] * slope_col).astype(bf16)
+        low = (scaled[:, head(h)] * inv_col - attended[:, head(h)] * slope_col).astype(bf16)
         low_grad[:, head(h)] = low
-        inflow = inflow_of(doc_col, doc_row, rates[h])
-        query_in = (query[:, head(h)].astype(f32) * inflow).astype(bf16)
-        put_pieces(out, h, dot(query_in, low, 0, 0))
+        put_pieces(out, h, dot(query_in[:, head(h)], low, 0, 0))
 
 
 def back_intra_kernel(
-    rates, docs, query, key, value, weights, low_grad, states, query_grad, key_part, value_part
+    rates, docs, inflow, query, key, value, weights, low_grad, states, query_grad, key_part, value_part
 ):
     doc_col, doc_row = docs_of(docs)
     for h in range(LOCAL):
@@ -137,21 +149,18 @@
         scores = dot(low, value[:, head(h)], 1, 1)
         grad_weights = (scores * decays_of(doc_col, doc_row, rates[h])).astype(bf16)
         state = get_pieces(states, h).astype(bf16)
-        inflow = inflow_of(doc_col, doc_row, rates[h])
-        whole = dot(grad_weights, key[:, head(h)], 1, 0) + inflow * dot(low, state, 1, 1)
+        whole = dot(grad_weights, key[:, head(h)], 1, 0) + inflow[h] * dot(low, state, 1, 1)
         query_grad[:, head(h)] = whole.astype(bf16)
         key_part[:, head(h)] = dot(grad_weights, query[:, head(h)], 0, 0)
         value_part[:, head(h)] = dot(weights[h], low, 0, 0)
 
 
-def finish_kernel(rates, docs, key, value, key_part, value_part, states, key_grad, value_grad):
-    doc_col, doc_row = docs_of(docs)
+def finish_kernel(outflow, key, value, key_part, value_part, states, key_grad, value_grad):
     for h in range(LOCAL):
         low = get_pieces(states, h).astype(bf16)
-        outflow = outflow_of(doc_col, doc_row, rates[h])
-        more = outflow * dot(value[:, head(h)], low, 1, 1)
+        more = outflow[h] * dot(value[:, head(h)], low, 1, 1)
         key_grad[:, head(h)] = (key_part[:, head(h)] + more).astype(bf16)
-        more = outflow * dot(key[:, head(h)], low, 1, 0)
+        more = outflow[h] * dot(key[:, head(h)], low, 1, 0)
         value_grad[:, head(h)] = (value_part[:, head(h)] + more).astype(bf16)
 
 
@@ -160,14 +169,6 @@
     return mine // (GROUPS * MEMBERS), (mine // MEMBERS) % GROUPS
 
 
-def my_rate(rates):
-    return rates[place()[0] * LOCAL // ROWS]
-
-
-def faded(rate, blocks):
-    return jnp.exp(jnp.full((1, BLOCK), -BLOCK * blocks, f32) * rate)
-
-
 def passing(same, fade):
     return jnp.where(same, fade, 0.0)
 
@@ -190,8 +191,8 @@
     return total[DOC + x : DOC + x + 1, :]
 
 
-def group_total_kernel(rates, pieces, out):
-    fade = faded(my_rate(rates), 1.0)
+def group_total_kernel(fades, pieces, out):
+    fade = fades[0:1, :]
     out[DOC:, :] = jnp.zeros((TALL - DOC, BLOCK), f32)
     for x in range(ROWS):
         total = pieces[x * MEMBERS, 0:PIECE, :]
@@ -202,9 +203,9 @@
         out[DOC + x : DOC + x + 1, :] = last_doc(pieces, x, MEMBERS - 1)
 
 
-def pair_total_kernel(rates, mine, theirs, out):
+def pair_total_kernel(fades, mine, theirs, out):
     first = place()[1] % 2 == 0
-    fade = faded(my_rate(rates), 1.0 * MEMBERS)
+    fade = fades[1:2, :]
     out[DOC:, :] = jnp.where(first, theirs[DOC:, :], mine[DOC:, :])
     for x in range(ROWS):
         same = doc_of(mine, x) == doc_of(theirs, x)
@@ -226,10 +227,9 @@
     return before, pair, jnp.where(group % 2 == 1, doc_of(partner, x), pair)
 
 
-def states_kernel(rates, pieces, partner, mine, theirs, out):
-    group, rate = place()[1], my_rate(rates)
-    one, four = faded(rate, 1.0), faded(rate, 1.0 * MEMBERS)
-    eight = faded(rate, 2.0 * MEMBERS)
+def states_kernel(fades, pieces, partner, mine, theirs, out):
+    group = place()[1]
+    one, four, eight = fades[0:1, :], fades[1:2, :], fades[2:3, :]
     carry = jnp.zeros((PIECE, BLOCK), f32)
     for x in range(ROWS):
         before, pair_doc, prev = before_group(partner, mine, theirs, group, x)
@@ -249,8 +249,8 @@
             prev = last
 
 
-def back_total_kernel(rates, pieces, partner, mine, theirs, grads, out):
-    group, fade = place()[1], faded(my_rate(rates), 1.0)
+def back_total_kernel(fades, pieces, partner, mine, theirs, grads, out):
+    group, fade = place()[1], fades[0:1, :]
     for x in range(ROWS):
         _, _, prev = before_group(partner, mine, theirs, group, x)
         total = jnp.zeros((PIECE, BLOCK), f32)
@@ -261,8 +261,8 @@
         out[x * PIECE : (x + 1) * PIECE, :] = total
 
 
-def back_pair_kernel(rates, total, partner, mine, theirs, grad, grad_theirs, out):
-    group, fade = place()[1], faded(my_rate(rates), 1.0 * MEMBERS)
+def back_pair_kernel(fades, total, partner, mine, theirs, grad, grad_theirs, out):
+    group, fade = place()[1], fades[1:2, :]
     first = group % 2 == 0
     for x in range(ROWS):
         _, before, _ = before_group(partner, mine, theirs, group, x)
@@ -273,11 +273,10 @@
 
 
 def back_states_kernel(
-    rates, pieces, total, partner, mine, theirs, grads, partner_grad, pair_grad, other_grad, out
+    fades, pieces, total, partner, mine, theirs, grads, partner_grad, pair_grad, other_grad, out
 ):
-    group, rate = place()[1], my_rate(rates)
-    one, four = faded(rate, 1.0), faded(rate, 1.0 * MEMBERS)
-    eight = faded(rate, 2.0 * MEMBERS)
+    group = place()[1]
+    one, four, eight = fades[0:1, :], fades[1:2, :], fades[2:3, :]
     carry = jnp.zeros((PIECE, BLOCK), f32)
     for x in range(ROWS - 1, -1, -1):
         before, _, _ = before_group(partner, mine, theirs, group, x)
@@ -299,12 +298,13 @@
 
 
 def call(kernel, name, outs, *args, flops=1):
+    scalars = args[0].shape == (LOCAL,)
     shapes = [jax.ShapeDtypeStruct(shape, dtype) for shape, dtype in outs]
     moved = sum(a.size * a.dtype.itemsize for a in (*args, *shapes))
     out = pl.pallas_call(
         kernel,
         out_shape=shapes,
-        in_specs=[SMEM] + [VMEM] * (len(args) - 1),
+        in_specs=[SMEM if scalars else VMEM] + [VMEM] * (len(args) - 1),
         out_specs=[VMEM] * len(shapes),
         name=name,
         compiler_params=pltpu.CompilerParams(vmem_limit_bytes=32 * 1024 * 1024),
@@ -329,54 +329,73 @@
     docs = doc_ids.reshape(1, BLOCK)
     gain = gain.reshape(1, LOCAL * HEAD_DIM)
     wide = (BLOCK, LOCAL * HEAD_DIM)
+    each = (LOCAL, BLOCK, BLOCK)
     cut = (OWNERS, PIECE, HEAD_DIM)
     one = 2 * LOCAL * BLOCK * BLOCK * HEAD_DIM
 
-    local = call(
-        local_state_kernel, "local_state", [((OWNERS, PIECE + PAD, HEAD_DIM), f32)],
-        rates, docs, key, value, flops=one,
-    )
+    local, fades = pl.pallas_call(
+        local_state_kernel,
+        out_shape=[
+            jax.ShapeDtypeStruct((OWNERS, PIECE + PAD, HEAD_DIM), f32),
+            jax.ShapeDtypeStruct((8, BLOCK), f32),
+        ],
+        in_specs=[pl.BlockSpec(memory_space=pl.ANY)] * 4,
+        out_specs=[VMEM] * 2,
+        scratch_shapes=[
+            pltpu.SMEM((LOCAL,), f32),
+            pltpu.VMEM((1, BLOCK), jnp.int32),
+            pltpu.VMEM(wide, bf16),
+            pltpu.VMEM(wide, bf16),
+            pltpu.SemaphoreType.DMA((4,)),
+        ],
+        name="local_state",
+        compiler_params=pltpu.CompilerParams(vmem_limit_bytes=60 * 1024 * 1024),
+        cost_estimate=pl.CostEstimate(flops=one, bytes_accessed=1 << 19, transcendentals=0),
+    )(rates, docs, key, value)
     pieces = swap(local)
-    total = call(group_total_kernel, "group_total", [((TALL, HEAD_DIM), f32)], rates, pieces)
+    total = call(group_total_kernel, "group_total", [((TALL, HEAD_DIM), f32)], fades, pieces)
     partner = other_group(total, 1)
-    weights, intra = call(
-        intra_kernel, "intra", [((LOCAL, BLOCK, BLOCK), bf16), (wide, f32)],
-        rates, docs, query, key, value, flops=2 * one,
-    )
-    pair = call(pair_total_kernel, "pair_total", [((TALL, HEAD_DIM), f32)], rates, total, partner)
+    weights, intra, scaled, query_in, inflow, outflow = call(
+        intra_kernel, "intra",
+        [(each, bf16), (wide, f32), (wide, f32), (wide, bf16), (each, f32), (each, f32)],
+        rates, docs, gain, query, key, value, grad, flops=2 * one,
+    )
+    partner, weights, intra = lax.optimization_barrier((partner, weights, intra))
+    pair = call(pair_total_kernel, "pair_total", [((TALL, HEAD_DIM), f32)], fades, total, partner)
     other = other_group(pair, 3)
-    states = swap(call(states_kernel, "states", [(cut, f32)], rates, pieces, partner, pair, other))
+    states = swap(call(states_kernel, "states", [(cut, f32)], fades, pieces, partner, pair, other))
     attended, sums = call(
         attend_kernel, "attend", [(wide, f32), ((8, 2, BLOCK), f32)],
-        rates, docs, gain, query, grad, intra, states, flops=one,
+        inflow, query, scaled, intra, states, flops=one,
     )
     sums = lax.all_to_all(sums, "head", 0, 0, tiled=True)
     low_grad, local_grad = call(
         grad_kernel, "grad", [(wide, bf16), (cut, f32)],
-        rates, docs, gain, query, grad, attended, sums, flops=one,
+        query_in, scaled, attended, sums, flops=one,
     )
     grads = swap(local_grad)
     total_grad = call(
-        back_total_kernel, "back_total", [((DOC, HEAD_DIM), f32)], rates, pieces, partner, pair, other, grads
+        back_total_kernel, "back_total", [((DOC, HEAD_DIM), f32)], fades, pieces, partner, pair, other, grads
     )
     partner_grad = other_group(total_grad, 1)
     query_grad, key_part, value_part = call(
         back_intra_kernel, "back_intra", [(wide, bf16), (wide, f32), (wide, f32)],
-        rates, docs, query, key, value, weights, low_grad, states, flops=5 * one,
-    )
+        rates, docs, inflow, query, key, value, weights, low_grad, states, flops=5 * one,
+    )
+    partner_grad, key_part, value_part = lax.optimization_barrier((partner_grad, key_part, value_part))
     pair_grad = call(
         back_pair_kernel, "back_pair", [((DOC, HEAD_DIM), f32)],
-        rates, total, partner, pair, other, total_grad, partner_grad,
+        fades, total, partner, pair, other, total_grad, partner_grad,
     )
     other_grad = other_group(pair_grad, 3)
     states_out = call(
         back_states_kernel, "back_states", [(cut, f32)],
-        rates, pieces, total, partner, pair, other, grads, partner_grad, pair_grad, other_grad,
+        fades, pieces, total, partner, pair, other, grads, partner_grad, pair_grad, other_grad,
     )
     states_out = swap(states_out)
     key_grad, value_grad = call(
         finish_kernel, "finish", [(wide, bf16), (wide, bf16)],
-        rates, docs, key, value, key_part, value_part, states_out, flops=2 * one,
+        outflow, key, value, key_part, value_part, states_out, flops=2 * one,
     )
     return query_grad, key_grad, value_grad
 

time: 132 us -> 124 us (0.939)
  blocking collectives: 42 us -> 71.5 us
  waiting for transfers between devices: 35.3 us -> 19.6 us
  starting transfers between devices: 37.6 us -> 22.9 us
  Pallas kernels: 12.6 us -> 7.51 us
  local copies, waits for them, and re-layouts: 2.49 us -> 0.04 us
    all_to_all x0 -> x2, blocking collectives: none -> 29.1 us  [the longest x1 16.9 us: per_device(): swap(call(states_kernel, 'states', [(cut, f32)], fades, pieces, partner,...]
    all_to_all x2 -> x0, starting transfers between devices: 14 us -> none  [the longest x1 8.44 us: per_device(): swap(call(states_kernel, 'states', [(cut, f32)], rates, pieces, partner,...]
    all_to_all x2 -> x0, waiting for transfers between devices: 13 us -> none  [the longest x1 7.45 us: per_device(): swap(call(states_kernel, 'states', [(cut, f32)], rates, pieces, partner,...]
    pallas_call x12, Pallas kernels: 12.6 us -> 7.51 us  [the longest x11 5.44 us: call(): pl.pallas_call(kernel, out_shape=shapes, in_specs=[SMEM if scalars else V...]
    ppermute x4, waiting for transfers between devices: 22.4 us -> 19.6 us  [other_group(): return lax.ppermute(total, 'seq', [(i, i ^ d * MEMBERS) for i in blocks])]
    unnamed x18 -> x16, local copies, waits for them, and re-layouts: 2.49 us -> 0.04 us
  transfers between devices with their start and end apart: 6 -> 4, of which waited for: 6 -> 4; matrix products, arithmetic and copies ran while one was open for 0% -> 0% of each run, Pallas kernels for 3% -> 3%
where the time goes in v4:
time: 124 us; the launch traced here: 122 us
  blocking collectives  71.5 us (58%)
  starting transfers between devices  22.9 us (18%)
  waiting for transfers between devices  19.6 us (16%)
  Pallas kernels  7.51 us (6%)
    ppermute x4, starting transfers between devices, other_group(): return lax.ppermute(total, 'seq', [(i, i ^ d * MEMBERS) for i in blocks])  22.9 us
    ppermute x4, waiting for transfers between devices, other_group(): return lax.ppermute(total, 'seq', [(i, i ^ d * MEMBERS) for i in blocks])  19.6 us
    all_to_all x1, blocking collectives, per_device(): pieces = swap(local)  19 us
    all_to_all x1, blocking collectives, per_device(): swap(call(states_kernel, 'states', [(cut, f32)], fades, pieces, partner,...  16.9 us
    all_to_all x1, blocking collectives, per_device(): grads = swap(local_grad)  13.8 us
    all_to_all x1, blocking collectives, per_device(): states_out = swap(states_out)  12.2 us
    all_to_all x1, blocking collectives, per_device(): sums = lax.all_to_all(sums, 'head', 0, 0, tiled=True)  9.58 us
    pallas_call x11, Pallas kernels, call(): pl.pallas_call(kernel, out_shape=shapes, in_specs=[SMEM if scalars else V...  5.44 us
  transfers between devices with their start and end apart: 4, of which 4 were waited for; matrix products, arithmetic and copies ran while one was open for 0% of the time, Pallas kernels for 3%

profile of v4, /device:TPU:6, one launch (start us, length us, event | category | flops | bytes accessed | tf_op | source)
XLA Modules:
  0.0 122.4 jit_solution(1803832404873838060)
XLA Ops:
  0.6 2.1 %local_state.1 = (f32[16,40,128]{2,1,0:T(8,128)}, f32[8,128]{1,0:T(8,128)}) custom-call(f32[4]{0:T(128)} %rates.3, s32[1,128]{1,0:T(1,128)} %bitcast.2, bf16[128,512]{1,0:T(8,128)(2,1)} %key.5, bf16[128,512]{1,0:T(8,128)(2,1)} %value.5), custom_call_target="tpu_custom_call" | custom-call | flops 16777216 | bytes 524288 | tf_op jit(solution)/shard_map/local_state/pallas_call | solution.py:336
  2.7 0.0 copy-start.3
  2.7 0.0 copy-start.4
  2.7 19.0 %all_to_all.25.pieces = f32[16,40,128]{2,1,0:T(8,128)S(1)} all-to-all(f32[16,40,128]{2,1,0:T(8,128)} %get-tuple-element.28), channel_id=1, replica_groups={{0,8,16,24,128,136,144,152,256,264,272,280,384,392,400,408},{32,40,48,5..., dimensions={0} | all-to-all | bytes 655360 | tf_op jit(solution)/shard_map/all_to_all | solution.py:355
  21.7 0.0 copy-start.7
  21.8 0.1 group_total.1.mine.total
  21.8 0.0 copy-start.5
  21.9 0.0 copy-start.6
  21.9 9.2 %collective-permute-start = (f32[136,128]{1,0:T(8,128)S(1)}, f32[136,128]{1,0:T(8,128)S(1)}, u32[]{:S(2)}, u32[]{:S(2)}) collective-permute-start(f32[136,128]{1,0:T(8,128)S(1)} %group_total.1.mine.total), channel_id=1, source_target_pairs={{0,32},{8,40},{16,48},{24,56},{32,0},{40,8},{48,16},{56,24},{64,96... | collective-permute-start | bytes 208904 | tf_op jit(solution)/shard_map/ppermute | solution.py:327
  31.1 0.0 copy-done.4
  31.1 0.0 copy-done
  31.1 0.0 copy-done.1
  31.1 0.0 copy-done.2
  31.2 1.3 %intra.1 = (bf16[4,128,128]{2,1,0:T(8,128)(2,1)S(1)}, f32[128,512]{1,0:T(8,128)S(1)}, f32[128,512]{1,0:T(8,128)S(1)}, bf16[128,512]{1,0:T(8,128)(2,1)S(1)}, f32[...) custom-call(f32[4]{0:T(128)S(1)} %copy-done.5, s32[1,128]{1,0:T(1,128)S(1)} %bitcast.3, f32[1,512]{1,0:T(1,128)S(1)} %bitcast.5, ...), custom_call_target="tpu_custom_call" | custom-call | flops 33554432 | bytes 1837584 | tf_op jit(solution)/shard_map/intra/pallas_call | solution.py:304
  32.5 3.2 %collective-permute-done.theirs.partner = f32[136,128]{1,0:T(8,128)S(1)} collective-permute-done((f32[136,128]{1,0:T(8,128)S(1)}, f32[136,128]{1,0:T(8,128)S(1)}, u32[]{:S(2)}, u32[]{:S(2)}) %collective-permute-start) | collective-permute-done | bytes 69664 | tf_op jit(solution)/shard_map/ppermute | solution.py:327
  35.7 6.4 %collective-permute-start.1 = (f32[136,128]{1,0:T(8,128)S(1)}, f32[136,128]{1,0:T(8,128)S(1)}, u32[]{:S(2)}, u32[]{:S(2)}) collective-permute-start(f32[136,128]{1,0:T(8,128)S(1)} %pair_total.1.mine), channel_id=1, source_target_pairs={{0,96},{8,104},{16,112},{24,120},{32,64},{40,72},{48,80},{56,88},{... | collective-permute-start | bytes 208904 | tf_op jit(solution)/shard_map/ppermute | solution.py:327
  42.2 3.7 %collective-permute-done.1.theirs = f32[136,128]{1,0:T(8,128)S(1)} collective-permute-done((f32[136,128]{1,0:T(8,128)S(1)}, f32[136,128]{1,0:T(8,128)S(1)}, u32[]{:S(2)}, u32[]{:S(2)}) %collective-permute-start.1) | collective-permute-done | bytes 69664 | tf_op jit(solution)/shard_map/ppermute | solution.py:327
  45.9 0.1 states.1
  46.0 16.9 %all_to_all.26.states = f32[16,32,128]{2,1,0:T(8,128)S(1)} all-to-all(f32[16,32,128]{2,1,0:T(8,128)S(1)} %states.1), channel_id=1, replica_groups={{0,8,16,24,128,136,144,152,256,264,272,280,384,392,400,408},{32,40,48,5..., dimensions={0} | all-to-all | bytes 524288 | tf_op jit(solution)/shard_map/all_to_all | solution.py:366
  62.9 0.3 attend.1
  63.1 9.6 %all_to_all.27.sums = f32[8,2,128]{2,1,0:T(2,128)S(1)} all-to-all(f32[8,2,128]{2,1,0:T(2,128)S(1)} %get-tuple-element.37), channel_id=1, replica_groups=mesh['seq'=64,'head'=8] {'head'}, dimensions={0} | all-to-all | bytes 16384 | tf_op jit(solution)/shard_map/all_to_all | solution.py:371
  72.7 0.3 grad.3
  73.0 13.8 %all_to_all.28.grads = f32[16,32,128]{2,1,0:T(8,128)S(1)} all-to-all(f32[16,32,128]{2,1,0:T(8,128)S(1)} %get-tuple-element.41), channel_id=1, replica_groups={{0,8,16,24,128,136,144,152,256,264,272,280,384,392,400,408},{32,40,48,5..., dimensions={0} | all-to-all | bytes 524288 | tf_op jit(solution)/shard_map/all_to_all | solution.py:376
  86.8 0.1 back_total.1.grad
  86.9 4.3 %collective-permute-start.2 = (f32[128,128]{1,0:T(8,128)S(1)}, f32[128,128]{1,0:T(8,128)S(1)}, u32[]{:S(2)}, u32[]{:S(2)}) collective-permute-start(f32[128,128]{1,0:T(8,128)S(1)} %back_total.1.grad), channel_id=1, source_target_pairs={{0,32},{8,40},{16,48},{24,56},{32,0},{40,8},{48,16},{56,24},{64,96... | collective-permute-start | bytes 196616 | tf_op jit(solution)/shard_map/ppermute | solution.py:327
  91.3 2.1 %back_intra.1 = (bf16[128,512]{1,0:T(8,128)(2,1)}, f32[128,512]{1,0:T(8,128)S(1)}, f32[128,512]{1,0:T(8,128)S(1)}) custom-call(f32[4]{0:T(128)S(1)} %copy-done.5, s32[1,128]{1,0:T(1,128)S(1)} %bitcast.4, f32[4,128,128]{2,1,0:T(8,128)S(1)} %get-tuple-element.26.inflow, bf16[128,512]{1,0:T(8,128)(2,1)S(1)} %copy-done.2, bf16[128,512]{1,0:T(8,128)(2,1)S(1)} %copy-done, ...), custom_call_target="tpu_custom_call" | custom-call | flops 83886080 | bytes 1835536 | tf_op jit(solution)/shard_map/back_intra/pallas_call | solution.py:304
  93.4 5.6 %collective-permute-done.2.grad_theirs.partner_grad = f32[128,128]{1,0:T(8,128)S(1)} collective-permute-done((f32[128,128]{1,0:T(8,128)S(1)}, f32[128,128]{1,0:T(8,128)S(1)}, u32[]{:S(2)}, u32[]{:S(2)}) %collective-permute-start.2) | collective-permute-done | bytes 65568 | tf_op jit(solution)/shard_map/ppermute | solution.py:327
  99.0 2.9 %collective-permute-start.3 = (f32[128,128]{1,0:T(8,128)S(1)}, f32[128,128]{1,0:T(8,128)S(1)}, u32[]{:S(2)}, u32[]{:S(2)}) collective-permute-start(f32[128,128]{1,0:T(8,128)S(1)} %back_pair.1.pair_grad), channel_id=1, source_target_pairs={{0,96},{8,104},{16,112},{24,120},{32,64},{40,72},{48,80},{56,88},{... | collective-permute-start | bytes 196616 | tf_op jit(solution)/shard_map/ppermute | solution.py:327
  102.0 7.1 %collective-permute-done.3.other_grad = f32[128,128]{1,0:T(8,128)S(1)} collective-permute-done((f32[128,128]{1,0:T(8,128)S(1)}, f32[128,128]{1,0:T(8,128)S(1)}, u32[]{:S(2)}, u32[]{:S(2)}) %collective-permute-start.3) | collective-permute-done | bytes 65568 | tf_op jit(solution)/shard_map/ppermute | solution.py:327
  109.1 0.1 back_states.1
  109.2 12.2 %all_to_all.29.states = f32[16,32,128]{2,1,0:T(8,128)S(1)} all-to-all(f32[16,32,128]{2,1,0:T(8,128)S(1)} %back_states.1), channel_id=1, replica_groups={{0,8,16,24,128,136,144,152,256,264,272,280,384,392,400,408},{32,40,48,5..., dimensions={0} | all-to-all | bytes 524288 | tf_op jit(solution)/shard_map/all_to_all | solution.py:395
  121.5 1.0 finish.1
  (9 shorter events, 0.1 us)
Async XLA Ops:
  2.7 19.0 %copy-start.3 = (f32[8,128]{1,0:T(8,128)S(1)}, f32[8,128]{1,0:T(8,128)}, u32[]{:S(2)}) copy-start(f32[8,128]{1,0:T(8,128)} %get-tuple-element.27.fades) | copy-start | bytes 12292
  2.7 28.4 %copy-start.4 = (bf16[128,512]{1,0:T(8,128)(2,1)S(1)}, bf16[128,512]{1,0:T(8,128)(2,1)}, u32[]{:S(2)}) copy-start(bf16[128,512]{1,0:T(8,128)(2,1)} %grad.2) | copy-start | bytes 393220
  21.7 9.4 %copy-start = (bf16[128,512]{1,0:T(8,128)(2,1)S(1)}, bf16[128,512]{1,0:T(8,128)(2,1)}, u32[]{:S(2)}) copy-start(bf16[128,512]{1,0:T(8,128)(2,1)} %key.5) | copy-start | bytes 393220
  21.7 9.4 %copy-start.1 = (bf16[128,512]{1,0:T(8,128)(2,1)S(1)}, bf16[128,512]{1,0:T(8,128)(2,1)}, u32[]{:S(2)}) copy-start(bf16[128,512]{1,0:T(8,128)(2,1)} %value.5) | copy-start | bytes 393220
  21.7 9.4 %copy-start.2 = (bf16[128,512]{1,0:T(8,128)(2,1)S(1)}, bf16[128,512]{1,0:T(8,128)(2,1)}, u32[]{:S(2)}) copy-start(bf16[128,512]{1,0:T(8,128)(2,1)} %query.5) | copy-start | bytes 393220
  21.7 9.4 %copy-start.7 = (f32[512]{0:T(512)S(1)}, f32[512]{0:T(512)}, u32[]{:S(2)}) copy-start(f32[512]{0:T(512)} %param.11) | copy-start | bytes 6148
  21.8 9.3 %copy-start.5 = (f32[4]{0:T(128)S(1)}, f32[4]{0:T(128)}, u32[]{:S(2)}) copy-start(f32[4]{0:T(128)} %rates.3) | copy-start | bytes 52
  21.9 9.3 %copy-start.6 = (s32[128]{0:T(128)S(1)}, s32[128]{0:T(128)}, u32[]{:S(2)}) copy-start(s32[128]{0:T(128)} %param.13) | copy-start | bytes 1540
  21.9 13.8 %collective-permute-start = (f32[136,128]{1,0:T(8,128)S(1)}, f32[136,128]{1,0:T(8,128)S(1)}, u32[]{:S(2)}, u32[]{:S(2)}) collective-permute-start(f32[136,128]{1,0:T(8,128)S(1)} %group_total.1.mine.total), channel_id=1, source_target_pairs={{0,32},{8,40},{16,48},{24,56},{32,0},{40,8},{48,16},{56,24},{64,96... | collective-permute-start | bytes 208904 | tf_op jit(solution)/shard_map/ppermute | solution.py:327
  35.7 10.1 %collective-permute-start.1 = (f32[136,128]{1,0:T(8,128)S(1)}, f32[136,128]{1,0:T(8,128)S(1)}, u32[]{:S(2)}, u32[]{:S(2)}) collective-permute-start(f32[136,128]{1,0:T(8,128)S(1)} %pair_total.1.mine), channel_id=1, source_target_pairs={{0,96},{8,104},{16,112},{24,120},{32,64},{40,72},{48,80},{56,88},{... | collective-permute-start | bytes 208904 | tf_op jit(solution)/shard_map/ppermute | solution.py:327
  86.9 12.1 %collective-permute-start.2 = (f32[128,128]{1,0:T(8,128)S(1)}, f32[128,128]{1,0:T(8,128)S(1)}, u32[]{:S(2)}, u32[]{:S(2)}) collective-permute-start(f32[128,128]{1,0:T(8,128)S(1)} %back_total.1.grad), channel_id=1, source_target_pairs={{0,32},{8,40},{16,48},{24,56},{32,0},{40,8},{48,16},{56,24},{64,96... | collective-permute-start | bytes 196616 | tf_op jit(solution)/shard_map/ppermute | solution.py:327
  99.0 10.1 %collective-permute-start.3 = (f32[128,128]{1,0:T(8,128)S(1)}, f32[128,128]{1,0:T(8,128)S(1)}, u32[]{:S(2)}, u32[]{:S(2)}) collective-permute-start(f32[128,128]{1,0:T(8,128)S(1)} %back_pair.1.pair_grad), channel_id=1, source_target_pairs={{0,96},{8,104},{16,112},{24,120},{32,64},{40,72},{48,80},{56,88},{... | collective-permute-start | bytes 196616 | tf_op jit(solution)/shard_map/ppermute | solution.py:327

commit v5 on v4

--- a/solution.py
+++ b/solution.py
@@ -16,7 +16,7 @@
 ROWS = 4
 OWNERS = ROWS * MEMBERS
 PIECE = LOCAL * HEAD_DIM // OWNERS
-PAD = 8
+SENT = PIECE + 1
 DOC = ROWS * PIECE
 TALL = DOC + 8
 
@@ -67,7 +67,7 @@
 def put_pieces(out, h, matrix):
     each = OWNERS // LOCAL
     for i in range(each):
-        out[h * each + i, 0:PIECE, :] = matrix[i * PIECE : (i + 1) * PIECE]
+        out[h * each + i] = matrix[i * PIECE : (i + 1) * PIECE]
 
 
 def get_pieces(pieces, h):
@@ -88,10 +88,12 @@
     for h in range(LOCAL):
         outflow = outflow_of(doc_col, doc_row, rates[h])
         key_out = (key[:, head(h)].astype(f32) * outflow).astype(bf16)
-        put_pieces(out, h, dot(key_out, value[:, head(h)], 0, 0))
-    for i in range(OWNERS):
-        out[i, PIECE:, :] = jnp.broadcast_to(doc_row, (PAD, BLOCK))
-    mine = rates[place()[0] * LOCAL // ROWS]
+        state = dot(key_out, value[:, head(h)], 0, 0)
+        for i in range(OWNERS // LOCAL):
+            start = (h * OWNERS // LOCAL + i) * SENT
+            out[start : start + PIECE, :] = state[i * PIECE : (i + 1) * PIECE]
+            out[start + PIECE : start + SENT, :] = doc_row
+    mine = rates[lax.axis_index("seq") // (GROUPS * MEMBERS) * LOCAL // ROWS]
     for i, blocks in enumerate((1, MEMBERS, 2 * MEMBERS)):
         fades[i : i + 1, :] = jnp.exp(jnp.full((1, BLOCK), -1.0 * BLOCK * blocks, f32) * mine)
 
@@ -165,8 +167,9 @@
 
 
 def place():
-    mine = lax.axis_index("seq")
-    return mine // (GROUPS * MEMBERS), (mine // MEMBERS) % GROUPS
+    group, odd = (lax.axis_index("seq") // MEMBERS) % GROUPS, lax.axis_index("head") % 2
+    turn = (group + odd) % GROUPS
+    return turn, odd == 1, (odd == 1) & (turn == 0), (odd == 1) & (turn == 1)
 
 
 def passing(same, fade):
@@ -174,13 +177,20 @@
 
 
 def first_doc(pieces, x, i):
-    row = pieces[x * MEMBERS + i, PIECE : PIECE + 1, 0:1]
+    start = (x * MEMBERS + i) * SENT + PIECE
+    row = pieces[start : start + 1, 0:1]
     return jnp.broadcast_to(row, (1, BLOCK))
 
 
 def last_doc(pieces, x, i):
-    row = pieces[x * MEMBERS + i, PIECE : PIECE + 1, BLOCK - 1 :]
+    start = (x * MEMBERS + i) * SENT + PIECE
+    row = pieces[start : start + 1, BLOCK - 1 :]
     return jnp.broadcast_to(row, (1, BLOCK))
+
+
+def piece_of(pieces, x, i):
+    start = (x * MEMBERS + i) * SENT
+    return pieces[start : start + PIECE, :]
 
 
 def state_of(total, x):
@@ -189,70 +199,99 @@
 
 def doc_of(total, x):
     return total[DOC + x : DOC + x + 1, :]
+
+
+def pick(read, total, x, late, empty):
+    soon = read(total, x) if x < ROWS else empty
+    return jnp.where(late, read(total, x - 1) if x else empty, soon)
+
+
+def state_at(total, x, late):
+    return pick(state_of, total, x, late, jnp.zeros((PIECE, BLOCK), f32))
+
+
+def doc_at(total, x, late):
+    return pick(doc_of, total, x, late, -jnp.ones((1, BLOCK), f32))
+
+
+def ordered(first, mine, theirs):
+    return jnp.where(first, mine, theirs), jnp.where(first, theirs, mine)
 
 
 def group_total_kernel(fades, pieces, out):
     fade = fades[0:1, :]
     out[DOC:, :] = jnp.zeros((TALL - DOC, BLOCK), f32)
     for x in range(ROWS):
-        total = pieces[x * MEMBERS, 0:PIECE, :]
+        total = piece_of(pieces, x, 0)
         for i in range(1, MEMBERS):
             same = last_doc(pieces, x, i) == last_doc(pieces, x, i - 1)
-            total = passing(same, fade) * total + pieces[x * MEMBERS + i, 0:PIECE, :]
+            total = passing(same, fade) * total + piece_of(pieces, x, i)
         out[x * PIECE : (x + 1) * PIECE, :] = total
         out[DOC + x : DOC + x + 1, :] = last_doc(pieces, x, MEMBERS - 1)
 
 
 def pair_total_kernel(fades, mine, theirs, out):
-    first = place()[1] % 2 == 0
-    fade = fades[1:2, :]
-    out[DOC:, :] = jnp.where(first, theirs[DOC:, :], mine[DOC:, :])
-    for x in range(ROWS):
-        same = doc_of(mine, x) == doc_of(theirs, x)
-        low = jnp.where(first, state_of(mine, x), state_of(theirs, x))
-        high = jnp.where(first, state_of(theirs, x), state_of(mine, x))
-        out[x * PIECE : (x + 1) * PIECE, :] = passing(same, fade) * low + high
-
-
-def row_docs(mine, theirs, group, x):
-    low = jnp.where(group < 2, doc_of(mine, x), doc_of(theirs, x))
-    high = jnp.where(group < 2, doc_of(theirs, x), doc_of(mine, x))
-    return low, high
-
-
-def before_group(partner, mine, theirs, group, x):
-    low, _ = row_docs(mine, theirs, group, x)
-    before = row_docs(mine, theirs, group, x - 1)[1] if x else -jnp.ones((1, BLOCK), f32)
-    pair = jnp.where(group > 1, low, before)
-    return before, pair, jnp.where(group % 2 == 1, doc_of(partner, x), pair)
+    turn, _, late, partner_late = place()
+    first, fade = turn % 2 == 0, fades[1:2, :]
+    out[DOC:, :] = jnp.zeros((TALL - DOC, BLOCK), f32)
+    for x in range(ROWS):
+        low_doc, high_doc = ordered(first, doc_at(mine, x, late), doc_at(theirs, x, partner_late))
+        low, high = ordered(first, state_at(mine, x, late), state_at(theirs, x, partner_late))
+        out[x * PIECE : (x + 1) * PIECE, :] = passing(low_doc == high_doc, fade) * low + high
+        out[DOC + x : DOC + x + 1, :] = high_doc
+
+
+def row_docs(mine, theirs, turn, x):
+    return ordered(turn < 2, doc_of(mine, x), doc_of(theirs, x))
+
+
+def before_row(mine, theirs, turn, x):
+    return row_docs(mine, theirs, turn, x - 1)[1] if x else -jnp.ones((1, BLOCK), f32)
+
+
+def before_pair(mine, theirs, turn, x):
+    before = before_row(mine, theirs, turn, x)
+    return jnp.where(turn > 1, row_docs(mine, theirs, turn, x)[0], before) if x < ROWS else before
+
+
+def before_group(partner, mine, theirs, x):
+    turn, _, _, partner_late = place()
+    before = before_pair(mine, theirs, turn, x)
+    return jnp.where(turn % 2 == 1, doc_at(partner, x, partner_late), before) if x < ROWS else before
 
 
 def states_kernel(fades, pieces, partner, mine, theirs, out):
-    group = place()[1]
+    turn, _, late, partner_late = place()
     one, four, eight = fades[0:1, :], fades[1:2, :], fades[2:3, :]
     carry = jnp.zeros((PIECE, BLOCK), f32)
-    for x in range(ROWS):
-        before, pair_doc, prev = before_group(partner, mine, theirs, group, x)
-        low_doc, high_doc = row_docs(mine, theirs, group, x)
-        low = jnp.where(group < 2, state_of(mine, x), state_of(theirs, x))
-        high = jnp.where(group < 2, state_of(theirs, x), state_of(mine, x))
-        half = passing(low_doc == before, eight) * carry + low
-        state = jnp.where(group > 1, half, carry)
-        longer = passing(doc_of(partner, x) == pair_doc, four) * state + state_of(partner, x)
-        state = jnp.where(group % 2 == 1, longer, state)
+    entries = []
+    for x in range(ROWS):
+        low_doc, high_doc = row_docs(mine, theirs, turn, x)
+        low, high = ordered(turn < 2, state_of(mine, x), state_of(theirs, x))
+        half = passing(low_doc == before_row(mine, theirs, turn, x), eight) * carry + low
+        state = jnp.where(turn > 1, half, carry)
+        same = doc_at(partner, x, partner_late) == before_pair(mine, theirs, turn, x)
+        longer = passing(same, four) * state + state_at(partner, x, partner_late)
+        entries.append(jnp.where(turn % 2 == 1, longer, state))
         carry = passing(high_doc == low_doc, eight) * half + high
+    entries.append(carry)
+    docs = [before_group(partner, mine, theirs, x) for x in range(ROWS + 1)]
+    for x in range(ROWS):
+        state = jnp.where(late, entries[x + 1], entries[x])
+        prev = jnp.where(late, docs[x + 1], docs[x])
         for i in range(MEMBERS):
             out[x * MEMBERS + i] = passing(first_doc(pieces, x, i) == prev, 1.0) * state
             last = last_doc(pieces, x, i)
             if i < MEMBERS - 1:
-                state = passing(last == prev, one) * state + pieces[x * MEMBERS + i, 0:PIECE, :]
+                state = passing(last == prev, one) * state + piece_of(pieces, x, i)
             prev = last
 
 
 def back_total_kernel(fades, pieces, partner, mine, theirs, grads, out):
-    group, fade = place()[1], fades[0:1, :]
-    for x in range(ROWS):
-        _, _, prev = before_group(partner, mine, theirs, group, x)
+    late, fade = place()[2], fades[0:1, :]
+    docs = [before_group(partner, mine, theirs, x) for x in range(ROWS + 1)]
+    for x in range(ROWS):
+        prev = jnp.where(late, docs[x + 1], docs[x])
         total = jnp.zeros((PIECE, BLOCK), f32)
         for i in range(MEMBERS - 1, -1, -1):
             older = last_doc(pieces, x, i - 1) if i else prev
@@ -262,33 +301,40 @@
 
 
 def back_pair_kernel(fades, total, partner, mine, theirs, grad, grad_theirs, out):
-    group, fade = place()[1], fades[1:2, :]
-    first = group % 2 == 0
-    for x in range(ROWS):
-        _, before, _ = before_group(partner, mine, theirs, group, x)
-        low_doc = jnp.where(first, doc_of(total, x), doc_of(partner, x))
-        low = jnp.where(first, state_of(grad, x), state_of(grad_theirs, x))
-        high = jnp.where(first, state_of(grad_theirs, x), state_of(grad, x))
-        out[x * PIECE : (x + 1) * PIECE, :] = low + passing(low_doc == before, fade) * high
+    turn, odd, late, partner_late = place()
+    first, fade = turn % 2 == 0, fades[1:2, :]
+    pairs = []
+    for x in range(ROWS + 1):
+        low_doc = jnp.where(first, doc_at(total, x, late), doc_at(partner, x, partner_late))
+        low, high = ordered(first, state_at(grad, x, late), state_at(grad_theirs, x, partner_late))
+        same = low_doc == before_pair(mine, theirs, turn, x)
+        pairs.append(low + passing(same, fade) * high)
+    for x in range(ROWS):
+        out[x * PIECE : (x + 1) * PIECE, :] = jnp.where(odd & (turn < 2), pairs[x + 1], pairs[x])
 
 
 def back_states_kernel(
     fades, pieces, total, partner, mine, theirs, grads, partner_grad, pair_grad, other_grad, out
 ):
-    group = place()[1]
+    turn, odd, late, partner_late = place()
     one, four, eight = fades[0:1, :], fades[1:2, :], fades[2:3, :]
-    carry = jnp.zeros((PIECE, BLOCK), f32)
+
+    def low_grad(x):
+        return jnp.where(turn < 2, state_at(pair_grad, x, odd), state_at(other_grad, x, odd))
+
+    carry = low_grad(ROWS)
+    entries = [jnp.zeros((PIECE, BLOCK), f32)]
     for x in range(ROWS - 1, -1, -1):
-        before, _, _ = before_group(partner, mine, theirs, group, x)
-        low_doc, high_doc = row_docs(mine, theirs, group, x)
-        low = jnp.where(group < 2, state_of(pair_grad, x), state_of(other_grad, x))
-        high = jnp.where(group < 2, state_of(other_grad, x), state_of(pair_grad, x))
+        low_doc, high_doc = row_docs(mine, theirs, turn, x)
+        high = jnp.where(turn < 2, state_of(other_grad, x), state_of(pair_grad, x))
         half = high + passing(high_doc == low_doc, eight) * carry
-        state = jnp.where(group < 2, half, carry)
-        same = doc_of(total, x) == doc_of(partner, x)
-        longer = state_of(partner_grad, x) + passing(same, four) * state
-        state = jnp.where(group % 2 == 0, longer, state)
-        carry = low + passing(low_doc == before, eight) * half
+        state = jnp.where(turn < 2, half, carry)
+        same = doc_at(total, x, late) == doc_at(partner, x, partner_late)
+        longer = state_at(partner_grad, x, partner_late) + passing(same, four) * state
+        entries.insert(0, jnp.where(turn % 2 == 0, longer, state))
+        carry = low_grad(x) + passing(low_doc == before_row(mine, theirs, turn, x), eight) * half
+    for x in range(ROWS):
+        state = jnp.where(late, entries[x + 1], entries[x])
         for i in range(MEMBERS - 1, -1, -1):
             out[x * MEMBERS + i] = state
             if i:
@@ -323,8 +369,15 @@
         lax.all_to_all, axis_name="seq", split_axis=0, concat_axis=0, axis_index_groups=owners, tiled=True
     )
 
-    def other_group(total, d):
-        return lax.ppermute(total, "seq", [(i, i ^ (d * MEMBERS)) for i in blocks])
+    heads = lax.axis_size("head")
+
+    def other_group(total, step):
+        pairs = [
+            (i * heads + h, (i ^ ((1, 3)[(step + h) % 2] * MEMBERS)) * heads + h)
+            for i in blocks
+            for h in range(heads)
+        ]
+        return lax.ppermute(total, ("seq", "head"), pairs)
 
     docs = doc_ids.reshape(1, BLOCK)
     gain = gain.reshape(1, LOCAL * HEAD_DIM)
@@ -336,7 +389,7 @@
     local, fades = pl.pallas_call(
         local_state_kernel,
         out_shape=[
-            jax.ShapeDtypeStruct((OWNERS, PIECE + PAD, HEAD_DIM), f32),
+            jax.ShapeDtypeStruct((OWNERS * SENT, HEAD_DIM), f32),
             jax.ShapeDtypeStruct((8, BLOCK), f32),
         ],
         in_specs=[pl.BlockSpec(memory_space=pl.ANY)] * 4,
@@ -352,9 +405,9 @@
         compiler_params=pltpu.CompilerParams(vmem_limit_bytes=60 * 1024 * 1024),
         cost_estimate=pl.CostEstimate(flops=one, bytes_accessed=1 << 19, transcendentals=0),
     )(rates, docs, key, value)
-    pieces = swap(local)
+    pieces = swap(local.reshape(OWNERS, SENT, 1, HEAD_DIM)).reshape(local.shape)
     total = call(group_total_kernel, "group_total", [((TALL, HEAD_DIM), f32)], fades, pieces)
-    partner = other_group(total, 1)
+    partner = other_group(total, 0)
     weights, intra, scaled, query_in, inflow, outflow = call(
         intra_kernel, "intra",
         [(each, bf16), (wide, f32), (wide, f32), (wide, bf16), (each, f32), (each, f32)],
@@ -362,7 +415,7 @@
     )
     partner, weights, intra = lax.optimization_barrier((partner, weights, intra))
     pair = call(pair_total_kernel, "pair_total", [((TALL, HEAD_DIM), f32)], fades, total, partner)
-    other = other_group(pair, 3)
+    other = other_group(pair, 1)
     states = swap(call(states_kernel, "states", [(cut, f32)], fades, pieces, partner, pair, other))
     attended, sums = call(
         attend_kernel, "attend", [(wide, f32), ((8, 2, BLOCK), f32)],
@@ -377,7 +430,7 @@
     total_grad = call(
         back_total_kernel, "back_total", [((DOC, HEAD_DIM), f32)], fades, pieces, partner, pair, other, grads
     )
-    partner_grad = other_group(total_grad, 1)
+    partner_grad = other_group(total_grad, 0)
     query_grad, key_part, value_part = call(
         back_intra_kernel, "back_intra", [(wide, bf16), (wide, f32), (wide, f32)],
         rates, docs, inflow, query, key, value, weights, low_grad, states, flops=5 * one,
@@ -387,7 +440,7 @@
         back_pair_kernel, "back_pair", [((DOC, HEAD_DIM), f32)],
         fades, total, partner, pair, other, total_grad, partner_grad,
     )
-    other_grad = other_group(pair_grad, 3)
+    other_grad = other_group(pair_grad, 1)
     states_out = call(
         back_states_kernel, "back_states", [(cut, f32)],
         fades, pieces, total, partner, pair, other, grads, partner_grad, pair_grad, other_grad,

time: 124 us -> 121 us (0.976)
  waiting for transfers between devices: 19.6 us -> 13.8 us
  starting transfers between devices: 22.9 us -> 28.3 us
  blocking collectives: 71.5 us -> 69.3 us
    ppermute x4, waiting for transfers between devices: 19.6 us -> 13.8 us  [other_group(): return lax.ppermute(total, ('seq', 'head'), pairs)]
    ppermute x4, starting transfers between devices: 22.9 us -> 28.3 us  [other_group(): return lax.ppermute(total, ('seq', 'head'), pairs)]
    all_to_all x1, blocking collectives: 16.9 us -> 13.6 us  [per_device(): swap(call(states_kernel, 'states', [(cut, f32)], fades, pieces, partner,...]
    all_to_all x1, blocking collectives: 12.2 us -> 14.3 us  [per_device(): states_out = swap(states_out)]
where the time goes in v5:
time: 121 us; the launch traced here: 120 us
  blocking collectives  69.3 us (57%)
  starting transfers between devices  28.3 us (23%)
  waiting for transfers between devices  13.8 us (11%)
  Pallas kernels  7.51 us (6%)
    ppermute x4, starting transfers between devices, other_group(): return lax.ppermute(total, ('seq', 'head'), pairs)  28.3 us
    all_to_all x1, blocking collectives, per_device(): pieces = swap(local.reshape(OWNERS, SENT, 1, HEAD_DIM)).reshape(local.shape)  17.8 us
    all_to_all x1, blocking collectives, per_device(): states_out = swap(states_out)  14.3 us
    all_to_all x1, blocking collectives, per_device(): grads = swap(local_grad)  14 us
    ppermute x4, waiting for transfers between devices, other_group(): return lax.ppermute(total, ('seq', 'head'), pairs)  13.8 us
    all_to_all x1, blocking collectives, per_device(): swap(call(states_kernel, 'states', [(cut, f32)], fades, pieces, partner,...  13.6 us
    all_to_all x1, blocking collectives, per_device(): sums = lax.all_to_all(sums, 'head', 0, 0, tiled=True)  9.58 us
    pallas_call x11, Pallas kernels, call(): pl.pallas_call(kernel, out_shape=shapes, in_specs=[SMEM if scalars else V...  5.46 us
  transfers between devices with their start and end apart: 4, of which 4 were waited for; matrix products, arithmetic and copies ran while one was open for 0% of the time, Pallas kernels for 3%

profile of v5, /device:TPU:6, one launch (start us, length us, event | category | flops | bytes accessed | tf_op | source)
XLA Modules:
  0.0 119.7 jit_solution(3606923034738806084)
XLA Ops:
  0.6 2.0 %local_state.1 = (f32[528,128]{1,0:T(8,128)}, f32[8,128]{1,0:T(8,128)}) custom-call(f32[4]{0:T(128)} %rates.3, s32[1,128]{1,0:T(1,128)} %bitcast.8, bf16[128,512]{1,0:T(8,128)(2,1)} %key.5, bf16[128,512]{1,0:T(8,128)(2,1)} %value.5), custom_call_target="tpu_custom_call" | custom-call | flops 16777216 | bytes 524288 | tf_op jit(solution)/shard_map/local_state/pallas_call | solution.py:389
  2.7 0.0 copy-start.3
  2.7 0.0 copy-start.2
  2.7 0.0 copy-start.4
  2.7 17.8 %all_to_all.25 = f32[16,33,1,128]{3,2,1,0:T(1,128)S(1)} all-to-all(f32[16,33,1,128]{3,2,1,0:T(1,128)} %bitcast.12), channel_id=1, replica_groups={{0,8,16,24,128,136,144,152,256,264,272,280,384,392,400,408},{32,40,48,5..., dimensions={0} | all-to-all | bytes 540672 | tf_op jit(solution)/shard_map/all_to_all | solution.py:408
  20.5 0.0 copy-done.3
  20.5 0.1 group_total.1.mine.total
  20.6 0.0 copy-start.5
  20.6 0.0 copy-start.6
  20.6 9.2 %collective-permute-start = (f32[136,128]{1,0:T(8,128)S(1)}, f32[136,128]{1,0:T(8,128)S(1)}, u32[]{:S(2)}, u32[]{:S(2)}) collective-permute-start(f32[136,128]{1,0:T(8,128)S(1)} %group_total.1.mine.total), channel_id=1, source_target_pairs={{0,32},{1,97},{2,34},{3,99},{4,36},{5,101},{6,38},{7,103},{8,40},{... | collective-permute-start | bytes 208904 | tf_op jit(solution)/shard_map/ppermute | solution.py:380
  29.9 0.0 copy-done.2
  29.9 0.0 copy-done.4
  29.9 0.0 copy-done
  29.9 1.3 %intra.1 = (bf16[4,128,128]{2,1,0:T(8,128)(2,1)S(1)}, f32[128,512]{1,0:T(8,128)S(1)}, f32[128,512]{1,0:T(8,128)S(1)}, bf16[128,512]{1,0:T(8,128)(2,1)S(1)}, f32[...) custom-call(f32[4]{0:T(128)S(1)} %copy-done.5, s32[1,128]{1,0:T(1,128)S(1)} %bitcast.9, f32[1,512]{1,0:T(1,128)S(1)} %bitcast.11, ...), custom_call_target="tpu_custom_call" | custom-call | flops 33554432 | bytes 1837584 | tf_op jit(solution)/shard_map/intra/pallas_call | solution.py:350
  31.2 3.1 %collective-permute-done.theirs.partner = f32[136,128]{1,0:T(8,128)S(1)} collective-permute-done((f32[136,128]{1,0:T(8,128)S(1)}, f32[136,128]{1,0:T(8,128)S(1)}, u32[]{:S(2)}, u32[]{:S(2)}) %collective-permute-start) | collective-permute-done | bytes 69664 | tf_op jit(solution)/shard_map/ppermute | solution.py:380
  34.4 7.2 %collective-permute-start.1 = (f32[136,128]{1,0:T(8,128)S(1)}, f32[136,128]{1,0:T(8,128)S(1)}, u32[]{:S(2)}, u32[]{:S(2)}) collective-permute-start(f32[136,128]{1,0:T(8,128)S(1)} %pair_total.1.mine), channel_id=1, source_target_pairs={{0,96},{1,33},{2,98},{3,35},{4,100},{5,37},{6,102},{7,39},{8,104},... | collective-permute-start | bytes 208904 | tf_op jit(solution)/shard_map/ppermute | solution.py:380
  41.6 3.7 %collective-permute-done.1.theirs = f32[136,128]{1,0:T(8,128)S(1)} collective-permute-done((f32[136,128]{1,0:T(8,128)S(1)}, f32[136,128]{1,0:T(8,128)S(1)}, u32[]{:S(2)}, u32[]{:S(2)}) %collective-permute-start.1) | collective-permute-done | bytes 69664 | tf_op jit(solution)/shard_map/ppermute | solution.py:380
  45.3 0.1 states.1
  45.4 13.6 %all_to_all.26.states = f32[16,32,128]{2,1,0:T(8,128)S(1)} all-to-all(f32[16,32,128]{2,1,0:T(8,128)S(1)} %states.1), channel_id=1, replica_groups={{0,8,16,24,128,136,144,152,256,264,272,280,384,392,400,408},{32,40,48,5..., dimensions={0} | all-to-all | bytes 524288 | tf_op jit(solution)/shard_map/all_to_all | solution.py:419
  59.0 0.3 attend.1
  59.3 9.6 %all_to_all.27.sums = f32[8,2,128]{2,1,0:T(2,128)S(1)} all-to-all(f32[8,2,128]{2,1,0:T(2,128)S(1)} %get-tuple-element.37), channel_id=1, replica_groups=mesh['seq'=64,'head'=8] {'head'}, dimensions={0} | all-to-all | bytes 16384 | tf_op jit(solution)/shard_map/all_to_all | solution.py:424
  68.9 0.3 grad.3
  69.1 14.0 %all_to_all.28.grads = f32[16,32,128]{2,1,0:T(8,128)S(1)} all-to-all(f32[16,32,128]{2,1,0:T(8,128)S(1)} %get-tuple-element.41), channel_id=1, replica_groups={{0,8,16,24,128,136,144,152,256,264,272,280,384,392,400,408},{32,40,48,5..., dimensions={0} | all-to-all | bytes 524288 | tf_op jit(solution)/shard_map/all_to_all | solution.py:429
  83.2 0.1 back_total.1.grad
  83.3 5.6 %collective-permute-start.2 = (f32[128,128]{1,0:T(8,128)S(1)}, f32[128,128]{1,0:T(8,128)S(1)}, u32[]{:S(2)}, u32[]{:S(2)}) collective-permute-start(f32[128,128]{1,0:T(8,128)S(1)} %back_total.1.grad), channel_id=1, source_target_pairs={{0,32},{1,97},{2,34},{3,99},{4,36},{5,101},{6,38},{7,103},{8,40},{... | collective-permute-start | bytes 196616 | tf_op jit(solution)/shard_map/ppermute | solution.py:380
  88.9 2.1 %back_intra.1 = (bf16[128,512]{1,0:T(8,128)(2,1)}, f32[128,512]{1,0:T(8,128)S(1)}, f32[128,512]{1,0:T(8,128)S(1)}) custom-call(f32[4]{0:T(128)S(1)} %copy-done.5, s32[1,128]{1,0:T(1,128)S(1)} %bitcast.10, f32[4,128,128]{2,1,0:T(8,128)S(1)} %get-tuple-element.26.inflow, bf16[128,512]{1,0:T(8,128)(2,1)S(1)} %copy-done.2, bf16[128,512]{1,0:T(8,128)(2,1)S(1)} %copy-done, ...), custom_call_target="tpu_custom_call" | custom-call | flops 83886080 | bytes 1835536 | tf_op jit(solution)/shard_map/back_intra/pallas_call | solution.py:350
  91.0 3.1 %collective-permute-done.2.grad_theirs.partner_grad = f32[128,128]{1,0:T(8,128)S(1)} collective-permute-done((f32[128,128]{1,0:T(8,128)S(1)}, f32[128,128]{1,0:T(8,128)S(1)}, u32[]{:S(2)}, u32[]{:S(2)}) %collective-permute-start.2) | collective-permute-done | bytes 65568 | tf_op jit(solution)/shard_map/ppermute | solution.py:380
  94.2 6.3 %collective-permute-start.3 = (f32[128,128]{1,0:T(8,128)S(1)}, f32[128,128]{1,0:T(8,128)S(1)}, u32[]{:S(2)}, u32[]{:S(2)}) collective-permute-start(f32[128,128]{1,0:T(8,128)S(1)} %back_pair.1.pair_grad), channel_id=1, source_target_pairs={{0,96},{1,33},{2,98},{3,35},{4,100},{5,37},{6,102},{7,39},{8,104},... | collective-permute-start | bytes 196616 | tf_op jit(solution)/shard_map/ppermute | solution.py:380
  100.5 3.8 %collective-permute-done.3.other_grad = f32[128,128]{1,0:T(8,128)S(1)} collective-permute-done((f32[128,128]{1,0:T(8,128)S(1)}, f32[128,128]{1,0:T(8,128)S(1)}, u32[]{:S(2)}, u32[]{:S(2)}) %collective-permute-start.3) | collective-permute-done | bytes 65568 | tf_op jit(solution)/shard_map/ppermute | solution.py:380
  104.4 0.1 back_states.1
  104.5 14.3 %all_to_all.29.states = f32[16,32,128]{2,1,0:T(8,128)S(1)} all-to-all(f32[16,32,128]{2,1,0:T(8,128)S(1)} %back_states.1), channel_id=1, replica_groups={{0,8,16,24,128,136,144,152,256,264,272,280,384,392,400,408},{32,40,48,5..., dimensions={0} | all-to-all | bytes 524288 | tf_op jit(solution)/shard_map/all_to_all | solution.py:448
  118.8 1.0 finish.1
  (9 shorter events, 0.1 us)
Async XLA Ops:
  2.7 17.8 %copy-start.3 = (f32[8,128]{1,0:T(8,128)S(1)}, f32[8,128]{1,0:T(8,128)}, u32[]{:S(2)}) copy-start(f32[8,128]{1,0:T(8,128)} %get-tuple-element.27.fades) | copy-start | bytes 12292
  2.7 27.2 %copy-start.2 = (bf16[128,512]{1,0:T(8,128)(2,1)S(1)}, bf16[128,512]{1,0:T(8,128)(2,1)}, u32[]{:S(2)}) copy-start(bf16[128,512]{1,0:T(8,128)(2,1)} %query.5) | copy-start | bytes 393220
  2.7 27.2 %copy-start.4 = (bf16[128,512]{1,0:T(8,128)(2,1)S(1)}, bf16[128,512]{1,0:T(8,128)(2,1)}, u32[]{:S(2)}) copy-start(bf16[128,512]{1,0:T(8,128)(2,1)} %grad.2) | copy-start | bytes 393220
  20.5 9.4 %copy-start = (bf16[128,512]{1,0:T(8,128)(2,1)S(1)}, bf16[128,512]{1,0:T(8,128)(2,1)}, u32[]{:S(2)}) copy-start(bf16[128,512]{1,0:T(8,128)(2,1)} %key.5) | copy-start | bytes 393220
  20.5 9.4 %copy-start.1 = (bf16[128,512]{1,0:T(8,128)(2,1)S(1)}, bf16[128,512]{1,0:T(8,128)(2,1)}, u32[]{:S(2)}) copy-start(bf16[128,512]{1,0:T(8,128)(2,1)} %value.5) | copy-start | bytes 393220
  20.5 9.4 %copy-start.7 = (f32[512]{0:T(512)S(1)}, f32[512]{0:T(512)}, u32[]{:S(2)}) copy-start(f32[512]{0:T(512)} %param.11) | copy-start | bytes 6148
  20.6 9.3 %copy-start.5 = (f32[4]{0:T(128)S(1)}, f32[4]{0:T(128)}, u32[]{:S(2)}) copy-start(f32[4]{0:T(128)} %rates.3) | copy-start | bytes 52
  20.6 9.3 %copy-start.6 = (s32[128]{0:T(128)S(1)}, s32[128]{0:T(128)}, u32[]{:S(2)}) copy-start(s32[128]{0:T(128)} %param.13) | copy-start | bytes 1540
  20.6 13.7 %collective-permute-start = (f32[136,128]{1,0:T(8,128)S(1)}, f32[136,128]{1,0:T(8,128)S(1)}, u32[]{:S(2)}, u32[]{:S(2)}) collective-permute-start(f32[136,128]{1,0:T(8,128)S(1)} %group_total.1.mine.total), channel_id=1, source_target_pairs={{0,32},{1,97},{2,34},{3,99},{4,36},{5,101},{6,38},{7,103},{8,40},{... | collective-permute-start | bytes 208904 | tf_op jit(solution)/shard_map/ppermute | solution.py:380
  34.4 10.9 %collective-permute-start.1 = (f32[136,128]{1,0:T(8,128)S(1)}, f32[136,128]{1,0:T(8,128)S(1)}, u32[]{:S(2)}, u32[]{:S(2)}) collective-permute-start(f32[136,128]{1,0:T(8,128)S(1)} %pair_total.1.mine), channel_id=1, source_target_pairs={{0,96},{1,33},{2,98},{3,35},{4,100},{5,37},{6,102},{7,39},{8,104},... | collective-permute-start | bytes 208904 | tf_op jit(solution)/shard_map/ppermute | solution.py:380
  83.3 10.8 %collective-permute-start.2 = (f32[128,128]{1,0:T(8,128)S(1)}, f32[128,128]{1,0:T(8,128)S(1)}, u32[]{:S(2)}, u32[]{:S(2)}) collective-permute-start(f32[128,128]{1,0:T(8,128)S(1)} %back_total.1.grad), channel_id=1, source_target_pairs={{0,32},{1,97},{2,34},{3,99},{4,36},{5,101},{6,38},{7,103},{8,40},{... | collective-permute-start | bytes 196616 | tf_op jit(solution)/shard_map/ppermute | solution.py:380
  94.2 10.2 %collective-permute-start.3 = (f32[128,128]{1,0:T(8,128)S(1)}, f32[128,128]{1,0:T(8,128)S(1)}, u32[]{:S(2)}, u32[]{:S(2)}) collective-permute-start(f32[128,128]{1,0:T(8,128)S(1)} %back_pair.1.pair_grad), channel_id=1, source_target_pairs={{0,96},{1,33},{2,98},{3,35},{4,100},{5,37},{6,102},{7,39},{8,104},... | collective-permute-start | bytes 196616 | tf_op jit(solution)/shard_map/ppermute | solution.py:380

commit v6 on v5

--- a/solution.py
+++ b/solution.py
@@ -15,6 +15,7 @@
 GROUPS = 4
 ROWS = 4
 OWNERS = ROWS * MEMBERS
+FLIP = 5
 PIECE = LOCAL * HEAD_DIM // OWNERS
 SENT = PIECE + 1
 DOC = ROWS * PIECE
@@ -82,20 +83,22 @@
     copies = [pltpu.make_async_copy(a, b, sems.at[i]) for i, (a, b) in enumerate(pairs)]
     for copy in copies:
         copy.start()
-    for copy in copies:
+    for copy in copies[:2]:
         copy.wait()
     doc_col, doc_row = docs_of(docs)
-    for h in range(LOCAL):
-        outflow = outflow_of(doc_col, doc_row, rates[h])
-        key_out = (key[:, head(h)].astype(f32) * outflow).astype(bf16)
+    outflows = [outflow_of(doc_col, doc_row, rates[h]) for h in range(LOCAL)]
+    mine = rates[position(lax.axis_index("seq") // (GROUPS * MEMBERS) * MEMBERS) // MEMBERS * LOCAL // ROWS]
+    for i, blocks in enumerate((1, MEMBERS, 2 * MEMBERS)):
+        fades[i : i + 1, :] = jnp.exp(jnp.full((1, BLOCK), -1.0 * BLOCK * blocks, f32) * mine)
+    for copy in copies[2:]:
+        copy.wait()
+    for h in range(LOCAL):
+        key_out = (key[:, head(h)].astype(f32) * outflows[h]).astype(bf16)
         state = dot(key_out, value[:, head(h)], 0, 0)
         for i in range(OWNERS // LOCAL):
             start = (h * OWNERS // LOCAL + i) * SENT
             out[start : start + PIECE, :] = state[i * PIECE : (i + 1) * PIECE]
             out[start + PIECE : start + SENT, :] = doc_row
-    mine = rates[lax.axis_index("seq") // (GROUPS * MEMBERS) * LOCAL // ROWS]
-    for i, blocks in enumerate((1, MEMBERS, 2 * MEMBERS)):
-        fades[i : i + 1, :] = jnp.exp(jnp.full((1, BLOCK), -1.0 * BLOCK * blocks, f32) * mine)
 
 
 def intra_kernel(
@@ -167,7 +170,7 @@
 
 
 def place():
-    group, odd = (lax.axis_index("seq") // MEMBERS) % GROUPS, lax.axis_index("head") % 2
+    group, odd = (lax.axis_index("seq") // MEMBERS) % GROUPS, (lax.axis_index("head") + 1) % 2
     turn = (group + odd) % GROUPS
     return turn, odd == 1, (odd == 1) & (turn == 0), (odd == 1) & (turn == 1)
 
@@ -176,21 +179,34 @@
     return jnp.where(same, fade, 0.0)
 
 
+def flipped():
+    return lax.axis_index("head") % 2 == 1
+
+
+def position(block):
+    return jnp.where(flipped(), block ^ FLIP, block)
+
+
+def slot(x, i):
+    return position(x * MEMBERS + i)
+
+
+def rows_of(pieces, x, i, first, count):
+    start = (x * MEMBERS + i) * SENT + first
+    other = ((x * MEMBERS + i) ^ FLIP) * SENT + first
+    return jnp.where(flipped(), pieces[other : other + count, :], pieces[start : start + count, :])
+
+
 def first_doc(pieces, x, i):
-    start = (x * MEMBERS + i) * SENT + PIECE
-    row = pieces[start : start + 1, 0:1]
-    return jnp.broadcast_to(row, (1, BLOCK))
+    return jnp.broadcast_to(rows_of(pieces, x, i, PIECE, 1)[:, 0:1], (1, BLOCK))
 
 
 def last_doc(pieces, x, i):
-    start = (x * MEMBERS + i) * SENT + PIECE
-    row = pieces[start : start + 1, BLOCK - 1 :]
-    return jnp.broadcast_to(row, (1, BLOCK))
+    return jnp.broadcast_to(rows_of(pieces, x, i, PIECE, 1)[:, BLOCK - 1 :], (1, BLOCK))
 
 
 def piece_of(pieces, x, i):
-    start = (x * MEMBERS + i) * SENT
-    return pieces[start : start + PIECE, :]
+    return rows_of(pieces, x, i, 0, PIECE)
 
 
 def state_of(total, x):
@@ -280,7 +296,7 @@
         state = jnp.where(late, entries[x + 1], entries[x])
         prev = jnp.where(late, docs[x + 1], docs[x])
         for i in range(MEMBERS):
-            out[x * MEMBERS + i] = passing(first_doc(pieces, x, i) == prev, 1.0) * state
+            out[slot(x, i)] = passing(first_doc(pieces, x, i) == prev, 1.0) * state
             last = last_doc(pieces, x, i)
             if i < MEMBERS - 1:
                 state = passing(last == prev, one) * state + piece_of(pieces, x, i)
@@ -295,7 +311,7 @@
         total = jnp.zeros((PIECE, BLOCK), f32)
         for i in range(MEMBERS - 1, -1, -1):
             older = last_doc(pieces, x, i - 1) if i else prev
-            local = passing(first_doc(pieces, x, i) == older, 1.0) * grads[x * MEMBERS + i]
+            local = passing(first_doc(pieces, x, i) == older, 1.0) * grads[slot(x, i)]
             total = passing(last_doc(pieces, x, i) == older, fade) * total + local
         out[x * PIECE : (x + 1) * PIECE, :] = total
 
@@ -336,10 +352,10 @@
     for x in range(ROWS):
         state = jnp.where(late, entries[x + 1], entries[x])
         for i in range(MEMBERS - 1, -1, -1):
-            out[x * MEMBERS + i] = state
+            out[slot(x, i)] = state
             if i:
                 last, older = last_doc(pieces, x, i), last_doc(pieces, x, i - 1)
-                local = passing(first_doc(pieces, x, i) == older, 1.0) * grads[x * MEMBERS + i]
+                local = passing(first_doc(pieces, x, i) == older, 1.0) * grads[slot(x, i)]
                 state = passing(last == older, one) * state + local
 
 
@@ -365,15 +381,17 @@
     owners = [
         [x * row_len + k * MEMBERS + i for x in range(ROWS) for i in range(MEMBERS)] for k in range(GROUPS)
     ]
+    heads = lax.axis_size("head")
+    orders = [
+        [group[j ^ (FLIP * (h % 2))] * heads + h for j in range(OWNERS)] for group in owners for h in range(heads)
+    ]
     swap = functools.partial(
-        lax.all_to_all, axis_name="seq", split_axis=0, concat_axis=0, axis_index_groups=owners, tiled=True
-    )
-
-    heads = lax.axis_size("head")
+        lax.all_to_all, axis_name=("seq", "head"), split_axis=0, concat_axis=0, axis_index_groups=orders, tiled=True
+    )
 
     def other_group(total, step):
         pairs = [
-            (i * heads + h, (i ^ ((1, 3)[(step + h) % 2] * MEMBERS)) * heads + h)
+            (i * heads + h, (i ^ ((1, 3)[(step + h + 1) % 2] * MEMBERS)) * heads + h)
             for i in blocks
             for h in range(heads)
         ]

time: 121 us -> 118 us (0.975)
  blocking collectives: 69.3 us -> 62.4 us
  waiting for transfers between devices: 13.8 us -> 16.3 us
    ppermute x4, waiting for transfers between devices: 13.8 us -> 16.3 us  [other_group(): return lax.ppermute(total, ('seq', 'head'), pairs)]
    all_to_all x1, blocking collectives: 14.3 us -> 11.8 us  [per_device(): states_out = swap(states_out)]
    all_to_all x1, blocking collectives: 14 us -> 12.4 us  [per_device(): grads = swap(local_grad)]
    all_to_all x1, blocking collectives: 17.8 us -> 16.3 us  [per_device(): pieces = swap(local.reshape(OWNERS, SENT, 1, HEAD_DIM)).reshape(local.shape)]
    all_to_all x1, blocking collectives: 13.6 us -> 12.3 us  [per_device(): swap(call(states_kernel, 'states', [(cut, f32)], fades, pieces, partner,...]
where the time goes in v6:
time: 118 us; the launch traced here: 117 us
  blocking collectives  62.4 us (53%)
  starting transfers between devices  29.5 us (25%)
  waiting for transfers between devices  16.3 us (14%)
  Pallas kernels  7.45 us (6%)
    ppermute x4, starting transfers between devices, other_group(): return lax.ppermute(total, ('seq', 'head'), pairs)  29.5 us
    all_to_all x1, blocking collectives, per_device(): pieces = swap(local.reshape(OWNERS, SENT, 1, HEAD_DIM)).reshape(local.shape)  16.3 us
    ppermute x4, waiting for transfers between devices, other_group(): return lax.ppermute(total, ('seq', 'head'), pairs)  16.3 us
    all_to_all x1, blocking collectives, per_device(): grads = swap(local_grad)  12.4 us
    all_to_all x1, blocking collectives, per_device(): swap(call(states_kernel, 'states', [(cut, f32)], fades, pieces, partner,...  12.3 us
    all_to_all x1, blocking collectives, per_device(): states_out = swap(states_out)  11.8 us
    all_to_all x1, blocking collectives, per_device(): sums = lax.all_to_all(sums, 'head', 0, 0, tiled=True)  9.58 us
    pallas_call x11, Pallas kernels, call(): pl.pallas_call(kernel, out_shape=shapes, in_specs=[SMEM if scalars else V...  5.52 us
  transfers between devices with their start and end apart: 4, of which 4 were waited for; matrix products, arithmetic and copies ran while one was open for 0% of the time, Pallas kernels for 3%

profile of v6, /device:TPU:6, one launch (start us, length us, event | category | flops | bytes accessed | tf_op | source)
XLA Modules:
  0.0 116.6 jit_solution(3533001211069571137)
XLA Ops:
  0.6 1.9 %local_state.1 = (f32[528,128]{1,0:T(8,128)}, f32[8,128]{1,0:T(8,128)}) custom-call(f32[4]{0:T(128)} %rates.3, s32[1,128]{1,0:T(1,128)} %bitcast.8, bf16[128,512]{1,0:T(8,128)(2,1)} %key.5, bf16[128,512]{1,0:T(8,128)(2,1)} %value.5), custom_call_target="tpu_custom_call" | custom-call | flops 16777216 | bytes 524288 | tf_op jit(solution)/shard_map/local_state/pallas_call | solution.py:407
  2.6 0.0 copy-start.3
  2.6 0.0 copy-start.2
  2.6 0.0 copy-start.4
  2.6 16.3 %all_to_all.25 = f32[16,33,1,128]{3,2,1,0:T(1,128)S(1)} all-to-all(f32[16,33,1,128]{3,2,1,0:T(1,128)} %bitcast.12), channel_id=1, replica_groups={{0,8,16,24,128,136,144,152,256,264,272,280,384,392,400,408},{137,129,15..., dimensions={0} | all-to-all | bytes 540672 | tf_op jit(solution)/shard_map/all_to_all | solution.py:426
  19.0 0.0 copy-done.3
  19.0 0.1 group_total.1.mine.total
  19.1 0.0 copy-start.5
  19.1 0.0 copy-start.6
  19.1 9.9 %collective-permute-start = (f32[136,128]{1,0:T(8,128)S(1)}, f32[136,128]{1,0:T(8,128)S(1)}, u32[]{:S(2)}, u32[]{:S(2)}) collective-permute-start(f32[136,128]{1,0:T(8,128)S(1)} %group_total.1.mine.total), channel_id=1, source_target_pairs={{0,96},{1,33},{2,98},{3,35},{4,100},{5,37},{6,102},{7,39},{8,104},... | collective-permute-start | bytes 208904 | tf_op jit(solution)/shard_map/ppermute | solution.py:398
  29.0 0.0 copy-done.2
  29.1 0.0 copy-done.4
  29.1 0.0 copy-done
  29.1 1.3 %intra.1 = (bf16[4,128,128]{2,1,0:T(8,128)(2,1)S(1)}, f32[128,512]{1,0:T(8,128)S(1)}, f32[128,512]{1,0:T(8,128)S(1)}, bf16[128,512]{1,0:T(8,128)(2,1)S(1)}, f32[...) custom-call(f32[4]{0:T(128)S(1)} %copy-done.5, s32[1,128]{1,0:T(1,128)S(1)} %bitcast.9, f32[1,512]{1,0:T(1,128)S(1)} %bitcast.11, ...), custom_call_target="tpu_custom_call" | custom-call | flops 33554432 | bytes 1837584 | tf_op jit(solution)/shard_map/intra/pallas_call | solution.py:366
  30.4 2.7 %collective-permute-done.theirs.partner = f32[136,128]{1,0:T(8,128)S(1)} collective-permute-done((f32[136,128]{1,0:T(8,128)S(1)}, f32[136,128]{1,0:T(8,128)S(1)}, u32[]{:S(2)}, u32[]{:S(2)}) %collective-permute-start) | collective-permute-done | bytes 69664 | tf_op jit(solution)/shard_map/ppermute | solution.py:398
  33.2 7.3 %collective-permute-start.1 = (f32[136,128]{1,0:T(8,128)S(1)}, f32[136,128]{1,0:T(8,128)S(1)}, u32[]{:S(2)}, u32[]{:S(2)}) collective-permute-start(f32[136,128]{1,0:T(8,128)S(1)} %pair_total.1.mine), channel_id=1, source_target_pairs={{0,32},{1,97},{2,34},{3,99},{4,36},{5,101},{6,38},{7,103},{8,40},{... | collective-permute-start | bytes 208904 | tf_op jit(solution)/shard_map/ppermute | solution.py:398
  40.5 4.8 %collective-permute-done.1.theirs = f32[136,128]{1,0:T(8,128)S(1)} collective-permute-done((f32[136,128]{1,0:T(8,128)S(1)}, f32[136,128]{1,0:T(8,128)S(1)}, u32[]{:S(2)}, u32[]{:S(2)}) %collective-permute-start.1) | collective-permute-done | bytes 69664 | tf_op jit(solution)/shard_map/ppermute | solution.py:398
  45.3 0.1 states.1
  45.4 12.3 %all_to_all.26.states = f32[16,32,128]{2,1,0:T(8,128)S(1)} all-to-all(f32[16,32,128]{2,1,0:T(8,128)S(1)} %states.1), channel_id=1, replica_groups={{0,8,16,24,128,136,144,152,256,264,272,280,384,392,400,408},{137,129,15..., dimensions={0} | all-to-all | bytes 524288 | tf_op jit(solution)/shard_map/all_to_all | solution.py:437
  57.7 0.3 attend.1
  58.0 9.6 %all_to_all.27.sums = f32[8,2,128]{2,1,0:T(2,128)S(1)} all-to-all(f32[8,2,128]{2,1,0:T(2,128)S(1)} %get-tuple-element.37), channel_id=1, replica_groups=mesh['seq'=64,'head'=8] {'head'}, dimensions={0} | all-to-all | bytes 16384 | tf_op jit(solution)/shard_map/all_to_all | solution.py:442
  67.6 0.3 grad.3
  67.8 12.4 %all_to_all.28.grads = f32[16,32,128]{2,1,0:T(8,128)S(1)} all-to-all(f32[16,32,128]{2,1,0:T(8,128)S(1)} %get-tuple-element.41), channel_id=1, replica_groups={{0,8,16,24,128,136,144,152,256,264,272,280,384,392,400,408},{137,129,15..., dimensions={0} | all-to-all | bytes 524288 | tf_op jit(solution)/shard_map/all_to_all | solution.py:447
  80.3 0.1 back_total.1.grad
  80.4 6.6 %collective-permute-start.2 = (f32[128,128]{1,0:T(8,128)S(1)}, f32[128,128]{1,0:T(8,128)S(1)}, u32[]{:S(2)}, u32[]{:S(2)}) collective-permute-start(f32[128,128]{1,0:T(8,128)S(1)} %back_total.1.grad), channel_id=1, source_target_pairs={{0,96},{1,33},{2,98},{3,35},{4,100},{5,37},{6,102},{7,39},{8,104},... | collective-permute-start | bytes 196616 | tf_op jit(solution)/shard_map/ppermute | solution.py:398
  87.0 2.1 %back_intra.1 = (bf16[128,512]{1,0:T(8,128)(2,1)}, f32[128,512]{1,0:T(8,128)S(1)}, f32[128,512]{1,0:T(8,128)S(1)}) custom-call(f32[4]{0:T(128)S(1)} %copy-done.5, s32[1,128]{1,0:T(1,128)S(1)} %bitcast.10, f32[4,128,128]{2,1,0:T(8,128)S(1)} %get-tuple-element.26.inflow, bf16[128,512]{1,0:T(8,128)(2,1)S(1)} %copy-done.2, bf16[128,512]{1,0:T(8,128)(2,1)S(1)} %copy-done, ...), custom_call_target="tpu_custom_call" | custom-call | flops 83886080 | bytes 1835536 | tf_op jit(solution)/shard_map/back_intra/pallas_call | solution.py:366
  89.1 2.5 %collective-permute-done.2.grad_theirs.partner_grad = f32[128,128]{1,0:T(8,128)S(1)} collective-permute-done((f32[128,128]{1,0:T(8,128)S(1)}, f32[128,128]{1,0:T(8,128)S(1)}, u32[]{:S(2)}, u32[]{:S(2)}) %collective-permute-start.2) | collective-permute-done | bytes 65568 | tf_op jit(solution)/shard_map/ppermute | solution.py:398
  91.7 5.7 %collective-permute-start.3 = (f32[128,128]{1,0:T(8,128)S(1)}, f32[128,128]{1,0:T(8,128)S(1)}, u32[]{:S(2)}, u32[]{:S(2)}) collective-permute-start(f32[128,128]{1,0:T(8,128)S(1)} %back_pair.1.pair_grad), channel_id=1, source_target_pairs={{0,32},{1,97},{2,34},{3,99},{4,36},{5,101},{6,38},{7,103},{8,40},{... | collective-permute-start | bytes 196616 | tf_op jit(solution)/shard_map/ppermute | solution.py:398
  97.4 6.3 %collective-permute-done.3.other_grad = f32[128,128]{1,0:T(8,128)S(1)} collective-permute-done((f32[128,128]{1,0:T(8,128)S(1)}, f32[128,128]{1,0:T(8,128)S(1)}, u32[]{:S(2)}, u32[]{:S(2)}) %collective-permute-start.3) | collective-permute-done | bytes 65568 | tf_op jit(solution)/shard_map/ppermute | solution.py:398
  103.6 0.1 back_states.1
  103.8 11.8 %all_to_all.29.states = f32[16,32,128]{2,1,0:T(8,128)S(1)} all-to-all(f32[16,32,128]{2,1,0:T(8,128)S(1)} %back_states.1), channel_id=1, replica_groups={{0,8,16,24,128,136,144,152,256,264,272,280,384,392,400,408},{137,129,15..., dimensions={0} | all-to-all | bytes 524288 | tf_op jit(solution)/shard_map/all_to_all | solution.py:466
  115.6 1.0 finish.1
  (9 shorter events, 0.1 us)
Async XLA Ops:
  2.6 16.4 %copy-start.3 = (f32[8,128]{1,0:T(8,128)S(1)}, f32[8,128]{1,0:T(8,128)}, u32[]{:S(2)}) copy-start(f32[8,128]{1,0:T(8,128)} %get-tuple-element.27.fades) | copy-start | bytes 12292
  2.6 26.5 %copy-start.2 = (bf16[128,512]{1,0:T(8,128)(2,1)S(1)}, bf16[128,512]{1,0:T(8,128)(2,1)}, u32[]{:S(2)}) copy-start(bf16[128,512]{1,0:T(8,128)(2,1)} %query.5) | copy-start | bytes 393220
  2.6 26.5 %copy-start.4 = (bf16[128,512]{1,0:T(8,128)(2,1)S(1)}, bf16[128,512]{1,0:T(8,128)(2,1)}, u32[]{:S(2)}) copy-start(bf16[128,512]{1,0:T(8,128)(2,1)} %grad.2) | copy-start | bytes 393220
  19.0 10.1 %copy-start = (bf16[128,512]{1,0:T(8,128)(2,1)S(1)}, bf16[128,512]{1,0:T(8,128)(2,1)}, u32[]{:S(2)}) copy-start(bf16[128,512]{1,0:T(8,128)(2,1)} %key.5) | copy-start | bytes 393220
  19.0 10.1 %copy-start.1 = (bf16[128,512]{1,0:T(8,128)(2,1)S(1)}, bf16[128,512]{1,0:T(8,128)(2,1)}, u32[]{:S(2)}) copy-start(bf16[128,512]{1,0:T(8,128)(2,1)} %value.5) | copy-start | bytes 393220
  19.0 10.1 %copy-start.7 = (f32[512]{0:T(512)S(1)}, f32[512]{0:T(512)}, u32[]{:S(2)}) copy-start(f32[512]{0:T(512)} %param.11) | copy-start | bytes 6148
  19.1 10.0 %copy-start.5 = (f32[4]{0:T(128)S(1)}, f32[4]{0:T(128)}, u32[]{:S(2)}) copy-start(f32[4]{0:T(128)} %rates.3) | copy-start | bytes 52
  19.1 10.0 %copy-start.6 = (s32[128]{0:T(128)S(1)}, s32[128]{0:T(128)}, u32[]{:S(2)}) copy-start(s32[128]{0:T(128)} %param.13) | copy-start | bytes 1540
  19.1 14.0 %collective-permute-start = (f32[136,128]{1,0:T(8,128)S(1)}, f32[136,128]{1,0:T(8,128)S(1)}, u32[]{:S(2)}, u32[]{:S(2)}) collective-permute-start(f32[136,128]{1,0:T(8,128)S(1)} %group_total.1.mine.total), channel_id=1, source_target_pairs={{0,96},{1,33},{2,98},{3,35},{4,100},{5,37},{6,102},{7,39},{8,104},... | collective-permute-start | bytes 208904 | tf_op jit(solution)/shard_map/ppermute | solution.py:398
  33.2 12.1 %collective-permute-start.1 = (f32[136,128]{1,0:T(8,128)S(1)}, f32[136,128]{1,0:T(8,128)S(1)}, u32[]{:S(2)}, u32[]{:S(2)}) collective-permute-start(f32[136,128]{1,0:T(8,128)S(1)} %pair_total.1.mine), channel_id=1, source_target_pairs={{0,32},{1,97},{2,34},{3,99},{4,36},{5,101},{6,38},{7,103},{8,40},{... | collective-permute-start | bytes 208904 | tf_op jit(solution)/shard_map/ppermute | solution.py:398
  80.4 11.3 %collective-permute-start.2 = (f32[128,128]{1,0:T(8,128)S(1)}, f32[128,128]{1,0:T(8,128)S(1)}, u32[]{:S(2)}, u32[]{:S(2)}) collective-permute-start(f32[128,128]{1,0:T(8,128)S(1)} %back_total.1.grad), channel_id=1, source_target_pairs={{0,96},{1,33},{2,98},{3,35},{4,100},{5,37},{6,102},{7,39},{8,104},... | collective-permute-start | bytes 196616 | tf_op jit(solution)/shard_map/ppermute | solution.py:398
  91.7 11.9 %collective-permute-start.3 = (f32[128,128]{1,0:T(8,128)S(1)}, f32[128,128]{1,0:T(8,128)S(1)}, u32[]{:S(2)}, u32[]{:S(2)}) collective-permute-start(f32[128,128]{1,0:T(8,128)S(1)} %back_pair.1.pair_grad), channel_id=1, source_target_pairs={{0,32},{1,97},{2,34},{3,99},{4,36},{5,101},{6,38},{7,103},{8,40},{... | collective-permute-start | bytes 196616 | tf_op jit(solution)/shard_map/ppermute | solution.py:398

commit v7 on v6

--- a/solution.py
+++ b/solution.py
@@ -15,7 +15,7 @@
 GROUPS = 4
 ROWS = 4
 OWNERS = ROWS * MEMBERS
-FLIP = 5
+FLIPS = (10, 15)
 PIECE = LOCAL * HEAD_DIM // OWNERS
 SENT = PIECE + 1
 DOC = ROWS * PIECE
@@ -184,7 +184,7 @@
 
 
 def position(block):
-    return jnp.where(flipped(), block ^ FLIP, block)
+    return jnp.where(flipped(), block ^ FLIPS[1], block ^ FLIPS[0])
 
 
 def slot(x, i):
@@ -192,8 +192,8 @@
 
 
 def rows_of(pieces, x, i, first, count):
-    start = (x * MEMBERS + i) * SENT + first
-    other = ((x * MEMBERS + i) ^ FLIP) * SENT + first
+    start = ((x * MEMBERS + i) ^ FLIPS[0]) * SENT + first
+    other = ((x * MEMBERS + i) ^ FLIPS[1]) * SENT + first
     return jnp.where(flipped(), pieces[other : other + count, :], pieces[start : start + count, :])
 
 
@@ -383,7 +383,7 @@
     ]
     heads = lax.axis_size("head")
     orders = [
-        [group[j ^ (FLIP * (h % 2))] * heads + h for j in range(OWNERS)] for group in owners for h in range(heads)
+        [group[j ^ FLIPS[h % 2]] * heads + h for j in range(OWNERS)] for group in owners for h in range(heads)
     ]
     swap = functools.partial(
         lax.all_to_all, axis_name=("seq", "head"), split_axis=0, concat_axis=0, axis_index_groups=orders, tiled=True
@@ -439,7 +439,8 @@
         attend_kernel, "attend", [(wide, f32), ((8, 2, BLOCK), f32)],
         inflow, query, scaled, intra, states, flops=one,
     )
-    sums = lax.all_to_all(sums, "head", 0, 0, tiled=True)
+    spread = [[0, 3, 4, 7, 2, 1, 6, 5]]
+    sums = lax.all_to_all(sums, "head", 0, 0, axis_index_groups=spread, tiled=True)
     low_grad, local_grad = call(
         grad_kernel, "grad", [(wide, bf16), (cut, f32)],
         query_in, scaled, attended, sums, flops=one,

time: 118 us -> 118 us (level)
  blocking collectives: 62.4 us -> 70.4 us
  waiting for transfers between devices: 16.3 us -> 9.76 us
    ppermute x4, waiting for transfers between devices: 16.3 us -> 9.76 us  [other_group(): return lax.ppermute(total, ('seq', 'head'), pairs)]
    all_to_all x1, blocking collectives: 12.3 us -> 15.9 us  [per_device(): swap(call(states_kernel, 'states', [(cut, f32)], fades, pieces, partner,...]
    all_to_all x1, blocking collectives: 11.8 us -> 15.4 us  [per_device(): states_out = swap(states_out)]
where the time goes in v7:
time: 118 us; the launch traced here: 117 us
  blocking collectives  70.4 us (60%)
  starting transfers between devices  28.6 us (24%)
  waiting for transfers between devices  9.76 us (8%)
  Pallas kernels  7.46 us (6%)
    ppermute x4, starting transfers between devices, other_group(): return lax.ppermute(total, ('seq', 'head'), pairs)  28.6 us
    all_to_all x1, blocking collectives, per_device(): pieces = swap(local.reshape(OWNERS, SENT, 1, HEAD_DIM)).reshape(local.shape)  17.1 us
    all_to_all x1, blocking collectives, per_device(): swap(call(states_kernel, 'states', [(cut, f32)], fades, pieces, partner,...  15.9 us
    all_to_all x1, blocking collectives, per_device(): states_out = swap(states_out)  15.4 us
    all_to_all x1, blocking collectives, per_device(): grads = swap(local_grad)  12.5 us
    ppermute x4, waiting for transfers between devices, other_group(): return lax.ppermute(total, ('seq', 'head'), pairs)  9.76 us
    all_to_all x1, blocking collectives, per_device(): lax.all_to_all(sums, 'head', 0, 0, axis_index_groups=spread, tiled=True)  9.55 us
    pallas_call x11, Pallas kernels, call(): pl.pallas_call(kernel, out_shape=shapes, in_specs=[SMEM if scalars else V...  5.52 us
  transfers between devices with their start and end apart: 4, of which 4 were waited for; matrix products, arithmetic and copies ran while one was open for 0% of the time, Pallas kernels for 3%

profile of v7, /device:TPU:6, one launch (start us, length us, event | category | flops | bytes accessed | tf_op | source)
XLA Modules:
  0.0 117.1 jit_solution(16099255940305579775)
XLA Ops:
  0.6 1.9 %local_state.1 = (f32[528,128]{1,0:T(8,128)}, f32[8,128]{1,0:T(8,128)}) custom-call(f32[4]{0:T(128)} %rates.3, s32[1,128]{1,0:T(1,128)} %bitcast.8, bf16[128,512]{1,0:T(8,128)(2,1)} %key.5, bf16[128,512]{1,0:T(8,128)(2,1)} %value.5), custom_call_target="tpu_custom_call" | custom-call | flops 16777216 | bytes 524288 | tf_op jit(solution)/shard_map/local_state/pallas_call | solution.py:407
  2.6 0.0 copy-start.3
  2.6 0.0 copy-start.2
  2.6 0.0 copy-start.4
  2.6 17.1 %all_to_all.25 = f32[16,33,1,128]{3,2,1,0:T(1,128)S(1)} all-to-all(f32[16,33,1,128]{3,2,1,0:T(1,128)} %bitcast.12), channel_id=1, replica_groups={{272,280,256,264,400,408,384,392,16,24,0,8,144,152,128,136},{409,401,39..., dimensions={0} | all-to-all | bytes 540672 | tf_op jit(solution)/shard_map/all_to_all | solution.py:426
  19.7 0.0 copy-done.3
  19.7 0.1 group_total.1.mine.total
  19.8 0.0 copy-start.5
  19.8 0.0 copy-start.6
  19.8 8.9 %collective-permute-start = (f32[136,128]{1,0:T(8,128)S(1)}, f32[136,128]{1,0:T(8,128)S(1)}, u32[]{:S(2)}, u32[]{:S(2)}) collective-permute-start(f32[136,128]{1,0:T(8,128)S(1)} %group_total.1.mine.total), channel_id=1, source_target_pairs={{0,96},{1,33},{2,98},{3,35},{4,100},{5,37},{6,102},{7,39},{8,104},... | collective-permute-start | bytes 208904 | tf_op jit(solution)/shard_map/ppermute | solution.py:398
  28.7 0.0 copy-done.2
  28.7 0.0 copy-done.4
  28.8 0.0 copy-done
  28.8 1.3 %intra.1 = (bf16[4,128,128]{2,1,0:T(8,128)(2,1)S(1)}, f32[128,512]{1,0:T(8,128)S(1)}, f32[128,512]{1,0:T(8,128)S(1)}, bf16[128,512]{1,0:T(8,128)(2,1)S(1)}, f32[...) custom-call(f32[4]{0:T(128)S(1)} %copy-done.5, s32[1,128]{1,0:T(1,128)S(1)} %bitcast.9, f32[1,512]{1,0:T(1,128)S(1)} %bitcast.11, ...), custom_call_target="tpu_custom_call" | custom-call | flops 33554432 | bytes 1837584 | tf_op jit(solution)/shard_map/intra/pallas_call | solution.py:366
  30.1 1.0 collective-permute-done.theirs.partner
  31.2 6.8 %collective-permute-start.1 = (f32[136,128]{1,0:T(8,128)S(1)}, f32[136,128]{1,0:T(8,128)S(1)}, u32[]{:S(2)}, u32[]{:S(2)}) collective-permute-start(f32[136,128]{1,0:T(8,128)S(1)} %pair_total.1.mine), channel_id=1, source_target_pairs={{0,32},{1,97},{2,34},{3,99},{4,36},{5,101},{6,38},{7,103},{8,40},{... | collective-permute-start | bytes 208904 | tf_op jit(solution)/shard_map/ppermute | solution.py:398
  38.0 3.4 %collective-permute-done.1.theirs = f32[136,128]{1,0:T(8,128)S(1)} collective-permute-done((f32[136,128]{1,0:T(8,128)S(1)}, f32[136,128]{1,0:T(8,128)S(1)}, u32[]{:S(2)}, u32[]{:S(2)}) %collective-permute-start.1) | collective-permute-done | bytes 69664 | tf_op jit(solution)/shard_map/ppermute | solution.py:398
  41.4 0.1 states.1
  41.5 15.9 %all_to_all.26.states = f32[16,32,128]{2,1,0:T(8,128)S(1)} all-to-all(f32[16,32,128]{2,1,0:T(8,128)S(1)} %states.1), channel_id=1, replica_groups={{272,280,256,264,400,408,384,392,16,24,0,8,144,152,128,136},{409,401,39..., dimensions={0} | all-to-all | bytes 524288 | tf_op jit(solution)/shard_map/all_to_all | solution.py:437
  57.4 0.3 attend.1
  57.7 9.6 %all_to_all.27.sums = f32[8,2,128]{2,1,0:T(2,128)S(1)} all-to-all(f32[8,2,128]{2,1,0:T(2,128)S(1)} %get-tuple-element.37), channel_id=1, replica_groups={{0,3,4,7,2,1,6,5},{8,11,12,15,10,9,14,13},{16,19,20,23,18,17,22,21},{24..., dimensions={0} | all-to-all | bytes 16384 | tf_op jit(solution)/shard_map/all_to_all | solution.py:443
  67.3 0.3 grad.3
  67.6 12.5 %all_to_all.28.grads = f32[16,32,128]{2,1,0:T(8,128)S(1)} all-to-all(f32[16,32,128]{2,1,0:T(8,128)S(1)} %get-tuple-element.41), channel_id=1, replica_groups={{272,280,256,264,400,408,384,392,16,24,0,8,144,152,128,136},{409,401,39..., dimensions={0} | all-to-all | bytes 524288 | tf_op jit(solution)/shard_map/all_to_all | solution.py:448
  80.0 0.1 back_total.1.grad
  80.2 6.8 %collective-permute-start.2 = (f32[128,128]{1,0:T(8,128)S(1)}, f32[128,128]{1,0:T(8,128)S(1)}, u32[]{:S(2)}, u32[]{:S(2)}) collective-permute-start(f32[128,128]{1,0:T(8,128)S(1)} %back_total.1.grad), channel_id=1, source_target_pairs={{0,96},{1,33},{2,98},{3,35},{4,100},{5,37},{6,102},{7,39},{8,104},... | collective-permute-start | bytes 196616 | tf_op jit(solution)/shard_map/ppermute | solution.py:398
  86.9 2.1 %back_intra.1 = (bf16[128,512]{1,0:T(8,128)(2,1)}, f32[128,512]{1,0:T(8,128)S(1)}, f32[128,512]{1,0:T(8,128)S(1)}) custom-call(f32[4]{0:T(128)S(1)} %copy-done.5, s32[1,128]{1,0:T(1,128)S(1)} %bitcast.10, f32[4,128,128]{2,1,0:T(8,128)S(1)} %get-tuple-element.26.inflow, bf16[128,512]{1,0:T(8,128)(2,1)S(1)} %copy-done.2, bf16[128,512]{1,0:T(8,128)(2,1)S(1)} %copy-done, ...), custom_call_target="tpu_custom_call" | custom-call | flops 83886080 | bytes 1835536 | tf_op jit(solution)/shard_map/back_intra/pallas_call | solution.py:366
  89.1 1.3 %collective-permute-done.2.grad_theirs.partner_grad = f32[128,128]{1,0:T(8,128)S(1)} collective-permute-done((f32[128,128]{1,0:T(8,128)S(1)}, f32[128,128]{1,0:T(8,128)S(1)}, u32[]{:S(2)}, u32[]{:S(2)}) %collective-permute-start.2) | collective-permute-done | bytes 65568 | tf_op jit(solution)/shard_map/ppermute | solution.py:398
  90.4 6.1 %collective-permute-start.3 = (f32[128,128]{1,0:T(8,128)S(1)}, f32[128,128]{1,0:T(8,128)S(1)}, u32[]{:S(2)}, u32[]{:S(2)}) collective-permute-start(f32[128,128]{1,0:T(8,128)S(1)} %back_pair.1.pair_grad), channel_id=1, source_target_pairs={{0,32},{1,97},{2,34},{3,99},{4,36},{5,101},{6,38},{7,103},{8,40},{... | collective-permute-start | bytes 196616 | tf_op jit(solution)/shard_map/ppermute | solution.py:398
  96.5 4.1 %collective-permute-done.3.other_grad = f32[128,128]{1,0:T(8,128)S(1)} collective-permute-done((f32[128,128]{1,0:T(8,128)S(1)}, f32[128,128]{1,0:T(8,128)S(1)}, u32[]{:S(2)}, u32[]{:S(2)}) %collective-permute-start.3) | collective-permute-done | bytes 65568 | tf_op jit(solution)/shard_map/ppermute | solution.py:398
  100.6 0.1 back_states.1
  100.7 15.4 %all_to_all.29.states = f32[16,32,128]{2,1,0:T(8,128)S(1)} all-to-all(f32[16,32,128]{2,1,0:T(8,128)S(1)} %back_states.1), channel_id=1, replica_groups={{272,280,256,264,400,408,384,392,16,24,0,8,144,152,128,136},{409,401,39..., dimensions={0} | all-to-all | bytes 524288 | tf_op jit(solution)/shard_map/all_to_all | solution.py:467
  116.2 1.0 finish.1
  (9 shorter events, 0.1 us)
Async XLA Ops:
  2.6 17.1 %copy-start.3 = (f32[8,128]{1,0:T(8,128)S(1)}, f32[8,128]{1,0:T(8,128)}, u32[]{:S(2)}) copy-start(f32[8,128]{1,0:T(8,128)} %get-tuple-element.27.fades) | copy-start | bytes 12292
  2.6 26.2 %copy-start.2 = (bf16[128,512]{1,0:T(8,128)(2,1)S(1)}, bf16[128,512]{1,0:T(8,128)(2,1)}, u32[]{:S(2)}) copy-start(bf16[128,512]{1,0:T(8,128)(2,1)} %query.5) | copy-start | bytes 393220
  2.6 26.2 %copy-start.4 = (bf16[128,512]{1,0:T(8,128)(2,1)S(1)}, bf16[128,512]{1,0:T(8,128)(2,1)}, u32[]{:S(2)}) copy-start(bf16[128,512]{1,0:T(8,128)(2,1)} %grad.2) | copy-start | bytes 393220
  19.7 9.1 %copy-start = (bf16[128,512]{1,0:T(8,128)(2,1)S(1)}, bf16[128,512]{1,0:T(8,128)(2,1)}, u32[]{:S(2)}) copy-start(bf16[128,512]{1,0:T(8,128)(2,1)} %key.5) | copy-start | bytes 393220
  19.7 9.1 %copy-start.1 = (bf16[128,512]{1,0:T(8,128)(2,1)S(1)}, bf16[128,512]{1,0:T(8,128)(2,1)}, u32[]{:S(2)}) copy-start(bf16[128,512]{1,0:T(8,128)(2,1)} %value.5) | copy-start | bytes 393220
  19.7 9.1 %copy-start.7 = (f32[512]{0:T(512)S(1)}, f32[512]{0:T(512)}, u32[]{:S(2)}) copy-start(f32[512]{0:T(512)} %param.11) | copy-start | bytes 6148
  19.8 9.0 %copy-start.5 = (f32[4]{0:T(128)S(1)}, f32[4]{0:T(128)}, u32[]{:S(2)}) copy-start(f32[4]{0:T(128)} %rates.3) | copy-start | bytes 52
  19.8 9.0 %copy-start.6 = (s32[128]{0:T(128)S(1)}, s32[128]{0:T(128)}, u32[]{:S(2)}) copy-start(s32[128]{0:T(128)} %param.13) | copy-start | bytes 1540
  19.8 11.3 %collective-permute-start = (f32[136,128]{1,0:T(8,128)S(1)}, f32[136,128]{1,0:T(8,128)S(1)}, u32[]{:S(2)}, u32[]{:S(2)}) collective-permute-start(f32[136,128]{1,0:T(8,128)S(1)} %group_total.1.mine.total), channel_id=1, source_target_pairs={{0,96},{1,33},{2,98},{3,35},{4,100},{5,37},{6,102},{7,39},{8,104},... | collective-permute-start | bytes 208904 | tf_op jit(solution)/shard_map/ppermute | solution.py:398
  31.2 10.2 %collective-permute-start.1 = (f32[136,128]{1,0:T(8,128)S(1)}, f32[136,128]{1,0:T(8,128)S(1)}, u32[]{:S(2)}, u32[]{:S(2)}) collective-permute-start(f32[136,128]{1,0:T(8,128)S(1)} %pair_total.1.mine), channel_id=1, source_target_pairs={{0,32},{1,97},{2,34},{3,99},{4,36},{5,101},{6,38},{7,103},{8,40},{... | collective-permute-start | bytes 208904 | tf_op jit(solution)/shard_map/ppermute | solution.py:398
  80.2 10.2 %collective-permute-start.2 = (f32[128,128]{1,0:T(8,128)S(1)}, f32[128,128]{1,0:T(8,128)S(1)}, u32[]{:S(2)}, u32[]{:S(2)}) collective-permute-start(f32[128,128]{1,0:T(8,128)S(1)} %back_total.1.grad), channel_id=1, source_target_pairs={{0,96},{1,33},{2,98},{3,35},{4,100},{5,37},{6,102},{7,39},{8,104},... | collective-permute-start | bytes 196616 | tf_op jit(solution)/shard_map/ppermute | solution.py:398
  90.4 10.2 %collective-permute-start.3 = (f32[128,128]{1,0:T(8,128)S(1)}, f32[128,128]{1,0:T(8,128)S(1)}, u32[]{:S(2)}, u32[]{:S(2)}) collective-permute-start(f32[128,128]{1,0:T(8,128)S(1)} %back_pair.1.pair_grad), channel_id=1, source_target_pairs={{0,32},{1,97},{2,34},{3,99},{4,36},{5,101},{6,38},{7,103},{8,40},{... | collective-permute-start | bytes 196616 | tf_op jit(solution)/shard_map/ppermute | solution.py:398

commit v8 on v7

--- a/solution.py
+++ b/solution.py
@@ -454,12 +454,12 @@
         back_intra_kernel, "back_intra", [(wide, bf16), (wide, f32), (wide, f32)],
         rates, docs, inflow, query, key, value, weights, low_grad, states, flops=5 * one,
     )
-    partner_grad, key_part, value_part = lax.optimization_barrier((partner_grad, key_part, value_part))
     pair_grad = call(
         back_pair_kernel, "back_pair", [((DOC, HEAD_DIM), f32)],
         fades, total, partner, pair, other, total_grad, partner_grad,
     )
     other_grad = other_group(pair_grad, 1)
+    other_grad, key_part, value_part = lax.optimization_barrier((other_grad, key_part, value_part))
     states_out = call(
         back_states_kernel, "back_states", [(cut, f32)],
         fades, pieces, total, partner, pair, other, grads, partner_grad, pair_grad, other_grad,

time: 118 us -> 118 us (level)
  no operation moved by 1% of the time
where the time goes in v8:
time: 118 us; the launch traced here: 117 us
  blocking collectives  70.4 us (60%)
  starting transfers between devices  28.6 us (24%)
  waiting for transfers between devices  9.76 us (8%)
  Pallas kernels  7.46 us (6%)
    ppermute x4, starting transfers between devices, other_group(): return lax.ppermute(total, ('seq', 'head'), pairs)  28.6 us
    all_to_all x1, blocking collectives, per_device(): pieces = swap(local.reshape(OWNERS, SENT, 1, HEAD_DIM)).reshape(local.shape)  17.1 us
    all_to_all x1, blocking collectives, per_device(): swap(call(states_kernel, 'states', [(cut, f32)], fades, pieces, partner,...  15.9 us
    all_to_all x1, blocking collectives, per_device(): states_out = swap(states_out)  15.4 us
    all_to_all x1, blocking collectives, per_device(): grads = swap(local_grad)  12.5 us
    ppermute x4, waiting for transfers between devices, other_group(): return lax.ppermute(total, ('seq', 'head'), pairs)  9.76 us
    all_to_all x1, blocking collectives, per_device(): lax.all_to_all(sums, 'head', 0, 0, axis_index_groups=spread, tiled=True)  9.55 us
    pallas_call x11, Pallas kernels, call(): pl.pallas_call(kernel, out_shape=shapes, in_specs=[SMEM if scalars else V...  5.52 us
  transfers between devices with their start and end apart: 4, of which 4 were waited for; matrix products, arithmetic and copies ran while one was open for 0% of the time, Pallas kernels for 3%

profile of v8, /device:TPU:6, one launch (start us, length us, event | category | flops | bytes accessed | tf_op | source)
XLA Modules:
  0.0 117.1 jit_solution(13966685076866925292)
XLA Ops:
  0.6 1.9 %local_state.1 = (f32[528,128]{1,0:T(8,128)}, f32[8,128]{1,0:T(8,128)}) custom-call(f32[4]{0:T(128)} %rates.3, s32[1,128]{1,0:T(1,128)} %bitcast.8, bf16[128,512]{1,0:T(8,128)(2,1)} %key.5, bf16[128,512]{1,0:T(8,128)(2,1)} %value.5), custom_call_target="tpu_custom_call" | custom-call | flops 16777216 | bytes 524288 | tf_op jit(solution)/shard_map/local_state/pallas_call | solution.py:407
  2.6 0.0 copy-start.3
  2.6 0.0 copy-start.2
  2.6 0.0 copy-start.4
  2.6 17.1 %all_to_all.25 = f32[16,33,1,128]{3,2,1,0:T(1,128)S(1)} all-to-all(f32[16,33,1,128]{3,2,1,0:T(1,128)} %bitcast.12), channel_id=1, replica_groups={{272,280,256,264,400,408,384,392,16,24,0,8,144,152,128,136},{409,401,39..., dimensions={0} | all-to-all | bytes 540672 | tf_op jit(solution)/shard_map/all_to_all | solution.py:426
  19.7 0.0 copy-done.3
  19.7 0.1 group_total.1.mine.total
  19.8 0.0 copy-start.5
  19.8 0.0 copy-start.6
  19.8 8.9 %collective-permute-start = (f32[136,128]{1,0:T(8,128)S(1)}, f32[136,128]{1,0:T(8,128)S(1)}, u32[]{:S(2)}, u32[]{:S(2)}) collective-permute-start(f32[136,128]{1,0:T(8,128)S(1)} %group_total.1.mine.total), channel_id=1, source_target_pairs={{0,96},{1,33},{2,98},{3,35},{4,100},{5,37},{6,102},{7,39},{8,104},... | collective-permute-start | bytes 208904 | tf_op jit(solution)/shard_map/ppermute | solution.py:398
  28.7 0.0 copy-done.2
  28.7 0.0 copy-done.4
  28.8 0.0 copy-done
  28.8 1.3 %intra.1 = (bf16[4,128,128]{2,1,0:T(8,128)(2,1)S(1)}, f32[128,512]{1,0:T(8,128)S(1)}, f32[128,512]{1,0:T(8,128)S(1)}, bf16[128,512]{1,0:T(8,128)(2,1)S(1)}, f32[...) custom-call(f32[4]{0:T(128)S(1)} %copy-done.5, s32[1,128]{1,0:T(1,128)S(1)} %bitcast.9, f32[1,512]{1,0:T(1,128)S(1)} %bitcast.11, ...), custom_call_target="tpu_custom_call" | custom-call | flops 33554432 | bytes 1837584 | tf_op jit(solution)/shard_map/intra/pallas_call | solution.py:366
  30.1 1.0 collective-permute-done.theirs.partner
  31.2 6.8 %collective-permute-start.1 = (f32[136,128]{1,0:T(8,128)S(1)}, f32[136,128]{1,0:T(8,128)S(1)}, u32[]{:S(2)}, u32[]{:S(2)}) collective-permute-start(f32[136,128]{1,0:T(8,128)S(1)} %pair_total.1.mine), channel_id=1, source_target_pairs={{0,32},{1,97},{2,34},{3,99},{4,36},{5,101},{6,38},{7,103},{8,40},{... | collective-permute-start | bytes 208904 | tf_op jit(solution)/shard_map/ppermute | solution.py:398
  38.0 3.4 %collective-permute-done.1.theirs = f32[136,128]{1,0:T(8,128)S(1)} collective-permute-done((f32[136,128]{1,0:T(8,128)S(1)}, f32[136,128]{1,0:T(8,128)S(1)}, u32[]{:S(2)}, u32[]{:S(2)}) %collective-permute-start.1) | collective-permute-done | bytes 69664 | tf_op jit(solution)/shard_map/ppermute | solution.py:398
  41.4 0.1 states.1
  41.5 15.9 %all_to_all.26.states = f32[16,32,128]{2,1,0:T(8,128)S(1)} all-to-all(f32[16,32,128]{2,1,0:T(8,128)S(1)} %states.1), channel_id=1, replica_groups={{272,280,256,264,400,408,384,392,16,24,0,8,144,152,128,136},{409,401,39..., dimensions={0} | all-to-all | bytes 524288 | tf_op jit(solution)/shard_map/all_to_all | solution.py:437
  57.4 0.3 attend.1
  57.7 9.6 %all_to_all.27.sums = f32[8,2,128]{2,1,0:T(2,128)S(1)} all-to-all(f32[8,2,128]{2,1,0:T(2,128)S(1)} %get-tuple-element.37), channel_id=1, replica_groups={{0,3,4,7,2,1,6,5},{8,11,12,15,10,9,14,13},{16,19,20,23,18,17,22,21},{24..., dimensions={0} | all-to-all | bytes 16384 | tf_op jit(solution)/shard_map/all_to_all | solution.py:443
  67.3 0.3 grad.3
  67.6 12.5 %all_to_all.28.grads = f32[16,32,128]{2,1,0:T(8,128)S(1)} all-to-all(f32[16,32,128]{2,1,0:T(8,128)S(1)} %get-tuple-element.41), channel_id=1, replica_groups={{272,280,256,264,400,408,384,392,16,24,0,8,144,152,128,136},{409,401,39..., dimensions={0} | all-to-all | bytes 524288 | tf_op jit(solution)/shard_map/all_to_all | solution.py:448
  80.0 0.1 back_total.1.grad
  80.2 6.8 %collective-permute-start.2 = (f32[128,128]{1,0:T(8,128)S(1)}, f32[128,128]{1,0:T(8,128)S(1)}, u32[]{:S(2)}, u32[]{:S(2)}) collective-permute-start(f32[128,128]{1,0:T(8,128)S(1)} %back_total.1.grad), channel_id=1, source_target_pairs={{0,96},{1,33},{2,98},{3,35},{4,100},{5,37},{6,102},{7,39},{8,104},... | collective-permute-start | bytes 196616 | tf_op jit(solution)/shard_map/ppermute | solution.py:398
  86.9 3.4 %collective-permute-done.2.grad_theirs.partner_grad = f32[128,128]{1,0:T(8,128)S(1)} collective-permute-done((f32[128,128]{1,0:T(8,128)S(1)}, f32[128,128]{1,0:T(8,128)S(1)}, u32[]{:S(2)}, u32[]{:S(2)}) %collective-permute-start.2) | collective-permute-done | bytes 65568 | tf_op jit(solution)/shard_map/ppermute | solution.py:398
  90.4 6.1 %collective-permute-start.3 = (f32[128,128]{1,0:T(8,128)S(1)}, f32[128,128]{1,0:T(8,128)S(1)}, u32[]{:S(2)}, u32[]{:S(2)}) collective-permute-start(f32[128,128]{1,0:T(8,128)S(1)} %back_pair.1.pair_grad), channel_id=1, source_target_pairs={{0,32},{1,97},{2,34},{3,99},{4,36},{5,101},{6,38},{7,103},{8,40},{... | collective-permute-start | bytes 196616 | tf_op jit(solution)/shard_map/ppermute | solution.py:398
  96.5 2.1 %back_intra.1 = (bf16[128,512]{1,0:T(8,128)(2,1)}, f32[128,512]{1,0:T(8,128)S(1)}, f32[128,512]{1,0:T(8,128)S(1)}) custom-call(f32[4]{0:T(128)S(1)} %copy-done.5, s32[1,128]{1,0:T(1,128)S(1)} %bitcast.10, f32[4,128,128]{2,1,0:T(8,128)S(1)} %get-tuple-element.26.inflow, bf16[128,512]{1,0:T(8,128)(2,1)S(1)} %copy-done.2, bf16[128,512]{1,0:T(8,128)(2,1)S(1)} %copy-done, ...), custom_call_target="tpu_custom_call" | custom-call | flops 83886080 | bytes 1835536 | tf_op jit(solution)/shard_map/back_intra/pallas_call | solution.py:366
  98.6 1.9 %collective-permute-done.3.other_grad = f32[128,128]{1,0:T(8,128)S(1)} collective-permute-done((f32[128,128]{1,0:T(8,128)S(1)}, f32[128,128]{1,0:T(8,128)S(1)}, u32[]{:S(2)}, u32[]{:S(2)}) %collective-permute-start.3) | collective-permute-done | bytes 65568 | tf_op jit(solution)/shard_map/ppermute | solution.py:398
  100.6 0.1 back_states.1
  100.7 15.4 %all_to_all.29.states = f32[16,32,128]{2,1,0:T(8,128)S(1)} all-to-all(f32[16,32,128]{2,1,0:T(8,128)S(1)} %back_states.1), channel_id=1, replica_groups={{272,280,256,264,400,408,384,392,16,24,0,8,144,152,128,136},{409,401,39..., dimensions={0} | all-to-all | bytes 524288 | tf_op jit(solution)/shard_map/all_to_all | solution.py:467
  116.2 1.0 finish.1
  (9 shorter events, 0.1 us)
Async XLA Ops:
  2.6 17.1 %copy-start.3 = (f32[8,128]{1,0:T(8,128)S(1)}, f32[8,128]{1,0:T(8,128)}, u32[]{:S(2)}) copy-start(f32[8,128]{1,0:T(8,128)} %get-tuple-element.27.fades) | copy-start | bytes 12292
  2.6 26.2 %copy-start.2 = (bf16[128,512]{1,0:T(8,128)(2,1)S(1)}, bf16[128,512]{1,0:T(8,128)(2,1)}, u32[]{:S(2)}) copy-start(bf16[128,512]{1,0:T(8,128)(2,1)} %query.5) | copy-start | bytes 393220
  2.6 26.2 %copy-start.4 = (bf16[128,512]{1,0:T(8,128)(2,1)S(1)}, bf16[128,512]{1,0:T(8,128)(2,1)}, u32[]{:S(2)}) copy-start(bf16[128,512]{1,0:T(8,128)(2,1)} %grad.2) | copy-start | bytes 393220
  19.7 9.1 %copy-start = (bf16[128,512]{1,0:T(8,128)(2,1)S(1)}, bf16[128,512]{1,0:T(8,128)(2,1)}, u32[]{:S(2)}) copy-start(bf16[128,512]{1,0:T(8,128)(2,1)} %key.5) | copy-start | bytes 393220
  19.7 9.1 %copy-start.1 = (bf16[128,512]{1,0:T(8,128)(2,1)S(1)}, bf16[128,512]{1,0:T(8,128)(2,1)}, u32[]{:S(2)}) copy-start(bf16[128,512]{1,0:T(8,128)(2,1)} %value.5) | copy-start | bytes 393220
  19.7 9.1 %copy-start.7 = (f32[512]{0:T(512)S(1)}, f32[512]{0:T(512)}, u32[]{:S(2)}) copy-start(f32[512]{0:T(512)} %param.11) | copy-start | bytes 6148
  19.8 9.0 %copy-start.5 = (f32[4]{0:T(128)S(1)}, f32[4]{0:T(128)}, u32[]{:S(2)}) copy-start(f32[4]{0:T(128)} %rates.3) | copy-start | bytes 52
  19.8 9.0 %copy-start.6 = (s32[128]{0:T(128)S(1)}, s32[128]{0:T(128)}, u32[]{:S(2)}) copy-start(s32[128]{0:T(128)} %param.13) | copy-start | bytes 1540
  19.8 11.3 %collective-permute-start = (f32[136,128]{1,0:T(8,128)S(1)}, f32[136,128]{1,0:T(8,128)S(1)}, u32[]{:S(2)}, u32[]{:S(2)}) collective-permute-start(f32[136,128]{1,0:T(8,128)S(1)} %group_total.1.mine.total), channel_id=1, source_target_pairs={{0,96},{1,33},{2,98},{3,35},{4,100},{5,37},{6,102},{7,39},{8,104},... | collective-permute-start | bytes 208904 | tf_op jit(solution)/shard_map/ppermute | solution.py:398
  31.2 10.2 %collective-permute-start.1 = (f32[136,128]{1,0:T(8,128)S(1)}, f32[136,128]{1,0:T(8,128)S(1)}, u32[]{:S(2)}, u32[]{:S(2)}) collective-permute-start(f32[136,128]{1,0:T(8,128)S(1)} %pair_total.1.mine), channel_id=1, source_target_pairs={{0,32},{1,97},{2,34},{3,99},{4,36},{5,101},{6,38},{7,103},{8,40},{... | collective-permute-start | bytes 208904 | tf_op jit(solution)/shard_map/ppermute | solution.py:398
  80.2 10.2 %collective-permute-start.2 = (f32[128,128]{1,0:T(8,128)S(1)}, f32[128,128]{1,0:T(8,128)S(1)}, u32[]{:S(2)}, u32[]{:S(2)}) collective-permute-start(f32[128,128]{1,0:T(8,128)S(1)} %back_total.1.grad), channel_id=1, source_target_pairs={{0,96},{1,33},{2,98},{3,35},{4,100},{5,37},{6,102},{7,39},{8,104},... | collective-permute-start | bytes 196616 | tf_op jit(solution)/shard_map/ppermute | solution.py:398
  90.4 10.2 %collective-permute-start.3 = (f32[128,128]{1,0:T(8,128)S(1)}, f32[128,128]{1,0:T(8,128)S(1)}, u32[]{:S(2)}, u32[]{:S(2)}) collective-permute-start(f32[128,128]{1,0:T(8,128)S(1)} %back_pair.1.pair_grad), channel_id=1, source_target_pairs={{0,32},{1,97},{2,34},{3,99},{4,36},{5,101},{6,38},{7,103},{8,40},{... | collective-permute-start | bytes 196616 | tf_op jit(solution)/shard_map/ppermute | solution.py:398
